TPU v7x, 32 devices: a whole 2x2x4 slice. The times are simulated.
32 devices in a mesh: leaf: 8 (over z, core), front: 4 (over y, x).
Axes of the slice: x: 2, y: 2, z: 4, core: 2. Of those that a mesh axis runs over, the one named last changes fastest.
Arguments:
- parent_border_inverse: float32 [8, 1536, 1536], P('leaf', 'front')
- parent_border_rows: float32 [8, 1536, 768], P('leaf', 'front'), may hold values from -0.09 to 0.09
- parent_diagonal_inverse: float32 [8, 768, 768], P('leaf', 'front')
- child_border_rows: float32 [16, 1024, 512], P('leaf', 'front'), may hold values from -0.13 to 0.13
- child_factor_inverse: float32 [16, 512, 512], P('leaf', 'front')
- child_index: int32 [16, 1024], replicated, may hold values from 0 to 2303, as said below
- child_parent: int32 [16], replicated, may hold values from 0 to 7, as said below
Outputs:
- parent_variance: float32 [8, 768], P('leaf')
- child_variance: float32 [16, 512], P('leaf')
Inputs may be any that keep to these rules, and one draw needn't show every extreme that they name: `child_index`: each row holds 1024 distinct positions in increasing order, the first 0 and the last 2303. `child_parent`: child c's parent is c // 2 or c // 2 with its lowest bit flipped, and every parent has exactly two children.
All inputs are finite; a program needn't handle non-finite values.
Results may differ from a plain program's by a relative error of at most 0.0003.
Values sent between devices are 32-bit elements; how exact they have to be, the bound alone decides.
No kernel may reach another device: no remote copies, remote signals or barrier semaphores. Data moves between devices by JAX's collectives and lax.ppermute only.
A program may use at most 64 MiB of HBM per device.

v0:
```python
import functools

import jax
import jax.numpy as jnp
from jax import lax
from jax.experimental import pallas as pl
from jax.experimental.pallas import tpu as pltpu
from jax.sharding import PartitionSpec as P

MIB = 1024 * 1024
COLS = 256


def shape_of(shape, dtype=jnp.float32):
    return jax.ShapeDtypeStruct(shape, dtype)


def exchange(value, leaf_mask, front_mask, parity=None):
    fronts = lax.axis_size("front")
    pairs = [
        (leaf * fronts + front, (leaf ^ leaf_mask) * fronts + (front ^ front_mask))
        for leaf in range(lax.axis_size("leaf"))
        for front in range(fronts)
        if parity is None or (leaf ^ front) & 1 == parity
    ]
    return lax.ppermute(value, ("leaf", "front"), pairs)


def cross(value):
    fronts = lax.axis_size("front")
    pairs = []
    for leaf in range(lax.axis_size("leaf")):
        for front in range(fronts):
            flip = (leaf ^ front) & 1
            pairs.append((leaf * fronts + front, (leaf ^ flip) * fronts + (front ^ flip)))
    return lax.ppermute(value, ("leaf", "front"), pairs)


def after(value, *others):
    return lax.optimization_barrier((value, *others))[0]


def kids_of(parent_ref, owner):
    partner = owner ^ 1
    pool = [2 * owner, 2 * owner + 1, 2 * partner, 2 * partner + 1]
    member = [parent_ref[kid] == owner for kid in pool]
    first = jnp.where(member[0], 0, jnp.where(member[1], 1, 2))
    second = jnp.where(member[3], 3, jnp.where(member[2], 2, 1))
    ids = [2 * jnp.where(slot < 2, owner, partner) + (slot & 1) for slot in (first, second)]
    return (first, second), ids


def place_of():
    front, leaf = lax.axis_index("front"), lax.axis_index("leaf")
    owner = (leaf & -2) | (front & 1)
    block = (front & -2) | (leaf & 1)
    return owner, block


def keeps():
    return ((lax.axis_index("leaf") ^ lax.axis_index("front")) & 1) == 0


def store(pair, action):
    for ref, chosen in zip(pair, (keeps(), jnp.logical_not(keeps()))):
        pl.when(chosen)(functools.partial(action, ref))


def rounded(value):
    return value.astype(jnp.bfloat16)


def halves(value):
    high = rounded(value)
    return high, rounded(value - high.astype(jnp.float32))


def dot(left, right):
    return jnp.dot(left, right, preferred_element_type=jnp.float32)


def product(left, right):
    (left_high, left_low), (right_high, right_low) = left, right
    return dot(left_high, right_high) + (dot(left_high, right_low) + dot(left_low, right_high))


def column_sum(value):
    return jnp.sum(value, axis=0, keepdims=True)


def spans(width):
    return [slice(start, start + COLS) for start in range(0, width, COLS)]


def select_kernel(parent_ref, index_ref, own_rows, own_inverse, other_rows, other_inverse, kid_out, index_out):
    leaf = lax.axis_index("leaf")
    slots, _ = kids_of(parent_ref, leaf)
    split = own_rows.shape[1]
    for place, slot in enumerate(slots):
        for source in range(4):
            rows, inverse = (own_rows, own_inverse) if source < 2 else (other_rows, other_inverse)

            @pl.when(slot == source)
            def _(rows=rows, inverse=inverse, place=place, source=source):
                kid_out[place, :split] = rows[source % 2]
                kid_out[place, split:] = inverse[source % 2]

    owner, block = place_of()
    _, ids = kids_of(parent_ref, owner)
    pieces, width = index_out.shape[1:]
    for place, kid in enumerate(ids):
        row = index_ref[pl.ds(kid, 1), :]
        parts = [row[:, start : start + width] for start in range(0, pieces * width, width)]
        for mask in range(pieces):
            part = parts[0]
            for at in range(1, pieces):
                part = jnp.where((block ^ mask) == at, parts[at], part)
            index_out[place, mask : mask + 1, :] = part


def picks(index, first, rows):
    position = lax.broadcasted_iota(jnp.int32, (rows, index.shape[1]), 0) + first
    return rounded(jnp.where(position == index, 1.0, 0.0))


def unpacked(pieces, refs):
    pairs = [(refs[0], refs[0]), (refs[1], refs[1])]
    for at in range(2, 2 * pieces - 2, 4):
        near_keep, near_swap, far_keep, far_swap = refs[at : at + 4]
        pairs += [(near_keep, near_swap), (far_keep, far_swap)]
    return pairs


def diagonal_kernel(pieces, index, factor, *refs):
    diagonal = refs[:pieces]
    diag_high, diag_low, pick_high, pick_low, weights, parent_sum = refs[pieces:]
    _, block = place_of()
    own_rows, size = diagonal[0].shape
    parent_sum[...] = column_sum(diagonal[0][...] * diagonal[0][...])
    for mask in range(pieces):
        start = pl.multiple_of((block ^ mask) * own_rows, 16)
        high, low = halves(diagonal[mask][...])
        diag_high[pl.ds(start, own_rows), :] = high
        diag_low[pl.ds(start, own_rows), :] = low
    for kid in range(2):
        for mask in range(pieces):
            pick = picks(index[kid, mask : mask + 1, :], 0, size)
            pick_high[kid, mask] = rounded(dot(diag_high[...], pick))
            pick_low[kid, mask] = rounded(dot(diag_low[...], pick))
    factor_halves = halves(factor[...])
    for span in spans(size):
        weights[:, span] = product(factor_halves, (diag_high[:, span], diag_low[:, span]))


def kid_kernel(pieces, index, pick_high, pick_low, factor, *refs):
    kids = refs[:pieces]
    reduced, lift_high, lower_high, kid_sum, inv_high, inv_low, lifted, lower = refs[pieces:]
    _, block = place_of()
    size, own_border, border_size = lifted.shape[0], factor.shape[0], lower.shape[0]
    kid_block = index.shape[2]
    inv_block, own_rows = kids[0].shape[1] - kid_block, size // pieces
    factor_high = rounded(factor[...])
    for kid in range(2):
        own_inverse = kids[0][kid, kid_block:]
        for mask in range(pieces):
            start = pl.multiple_of((block ^ mask) * inv_block, 16)
            high, low = halves(kids[mask][kid, kid_block:])
            inv_high[pl.ds(start, inv_block), :] = high
            inv_low[pl.ds(start, inv_block), :] = low
        inverse = inv_high[...], inv_low[...]
        for mask in range(pieces):
            high, low = halves(product(halves(kids[mask][kid, :kid_block]), inverse))
            lifted_part = dot(pick_high[kid, mask], high) + dot(pick_low[kid, mask], high)
            places = index[kid, mask : mask + 1, :]
            low_part = dot(picks(places, size + block * own_border, own_border), low)
            part = dot(picks(places, size, border_size), high)
            lifted[...] = lifted_part if mask == 0 else lifted[...] + lifted_part
            reduced[kid] = low_part if mask == 0 else reduced[kid] + low_part
            lower[...] = part if mask == 0 else lower[...] + part
        own = lifted[pl.ds(pl.multiple_of(block * own_rows, 16), own_rows), :]
        kid_sum[kid : kid + 1] = column_sum(own_inverse * own_inverse) + column_sum(own * own)
        lift_high[kid] = rounded(lifted[...])
        lower_high[kid] = rounded(lower[...])
        own_lower = lower[pl.ds(pl.multiple_of(block * own_border, 8), own_border), :]
        reduced[kid] = own_lower + reduced[kid] - dot(factor_high, lift_high[kid])


def border_kernel(border, lower_high, border_high, border_lower):
    border_high[...] = rounded(border[...])
    for kid in range(2):
        for span in spans(lower_high.shape[2]):
            border_lower[kid, :, span] = dot(border_high[...], lower_high[kid, :, span])


def image_kernel(pieces, *refs):
    factor = unpacked(pieces, refs)
    border_high, border_lower, weights, reduced, lift_high, diag_high, diag_low, parent_sum, kid_sum, out = refs[
        2 * pieces - 2 : 2 * pieces + 8
    ]
    factor_high, fold_high, fold_low = refs[2 * pieces + 8 :]
    _, block = place_of()
    own_border, size = refs[0].shape
    kid_size = reduced.shape[2]
    for mask, pair in enumerate(factor):
        start = pl.multiple_of((block ^ mask) * own_border, 16)

        def put(ref, start=start):
            factor_high[pl.ds(start, own_border), :] = rounded(ref[...])

        if mask < 2:
            put(pair[0])
        else:
            store(pair, put)
    for span in spans(size):
        fold_high[:, span], fold_low[:, span] = halves(dot(border_high[...], factor_high[:, span]))
    fold = fold_high[...], fold_low[...]
    for span in spans(size):
        image = product(fold, (diag_high[:, span], diag_low[:, span]))
        out[:, span] = parent_sum[:, span] + column_sum(weights[:, span] * image)
    for kid in range(2):
        for span in spans(kid_size):
            image = border_lower[kid, :, span] - dot(fold[0], lift_high[kid, :, span])
            target = size + kid * kid_size + span.start
            out[:, target : target + COLS] = kid_sum[kid : kid + 1, span] + column_sum(reduced[kid, :, span] * image)


def finish_kernel(parent_ref, *refs):
    partials, (parent_out, kid_out) = refs[:-2], refs[-2:]
    leaf = lax.axis_index("leaf")
    size, kid_size = parent_out.shape[1], kid_out.shape[1]
    half = len(partials) // 2
    sums = [functools.reduce(jnp.add, [ref[...] for ref in group]) for group in (partials[:half], partials[half:])]
    owner, _ = place_of()
    parent_out[...] = jnp.where(owner == leaf, sums[0][:, :size], sums[1][:, :size])
    for parent, total in ((owner, sums[0]), (owner ^ 1, sums[1])):
        _, ids = kids_of(parent_ref, parent)
        for place in range(2):
            for kid in range(2):

                @pl.when(ids[place] == 2 * leaf + kid)
                def _(total=total, place=place, kid=kid):
                    start = size + place * kid_size
                    kid_out[kid : kid + 1] = total[:, start : start + kid_size]


def call(kernel, out_shape, limit, scalars=0, loose=0, keep=True, scratch=(), moved=1_000):
    def run(*args):
        specs = [pl.BlockSpec(memory_space=pltpu.SMEM if at < scalars else pltpu.VMEM) for at in range(len(args))]
        args = [
            pltpu.with_memory_space_constraint(value, pltpu.HBM if at < loose else pltpu.VMEM)
            for at, value in enumerate(args)
        ]
        results = out_shape
        if keep:
            results = jax.tree.map(lambda leaf: pltpu.VMEM(leaf.shape, leaf.dtype), results)
        return pl.pallas_call(
            kernel,
            out_shape=results,
            in_specs=specs,
            out_specs=jax.tree.map(lambda _: pl.BlockSpec(memory_space=pltpu.VMEM), out_shape),
            scratch_shapes=scratch,
            compiler_params=pltpu.CompilerParams(vmem_limit_bytes=limit * MIB),
            cost_estimate=pl.CostEstimate(flops=0, bytes_accessed=moved, transcendentals=0),
        )(*args)

    return run


def shards(border, factor, diagonal, kid_rows, kid_inverse, child_index, child_parent):
    border, factor, diagonal = border[0], factor[0], diagonal[0]
    pieces = lax.axis_size("front")
    size, kid_size, border_size = diagonal.shape[1], kid_rows.shape[2], border.shape[1]
    own_border = border.shape[0]
    kid_block = kid_rows.shape[1]
    half = jnp.bfloat16

    def over_fronts(value, parity=None):
        parts = {0: value}
        bit = 2
        while bit < pieces:
            for mask in list(parts):
                parts[mask | bit] = exchange(parts[mask], 0, bit, parity)
            bit *= 2
        return parts

    def spread(parts, gate_own, gate_rest):
        others = {mask | 1: exchange(after(part, *(gate_rest if mask else gate_own)), 1, 0) for mask, part in parts.items()}
        parts = parts | others
        return [parts[mask] for mask in range(pieces)]

    last = pieces - 2
    keep_factor = over_fronts(factor, 0)
    own_diagonal = cross(diagonal)
    kid_shape = (2, kid_block + kid_inverse.shape[1], kid_size)
    own_kids, index = call(
        select_kernel, (shape_of(kid_shape), shape_of((2, pieces, kid_block), jnp.int32)), 6, scalars=1, loose=4
    )(child_parent, child_index, kid_rows, kid_inverse, exchange(kid_rows, 1, 0), exchange(kid_inverse, 1, 0))
    own_kids = cross(after(own_kids, own_diagonal, keep_factor[last]))
    diagonal_parts = over_fronts(own_diagonal)
    kid_parts = over_fronts(after(own_kids, diagonal_parts[last]))
    own_factor = cross(after(factor, own_diagonal))
    diagonal_parts = spread(diagonal_parts, [own_kids], [own_kids])

    diag_high, diag_low, pick_high, pick_low, weights, parent_sum = call(
        functools.partial(diagonal_kernel, pieces),
        (
            shape_of((size, size), half),
            shape_of((size, size), half),
            shape_of((2, pieces, size, kid_block), half),
            shape_of((2, pieces, size, kid_block), half),
            shape_of((own_border, size)),
            shape_of((1, size)),
        ),
        10,
    )(index, own_factor, *diagonal_parts)
    own_border_rows = cross(after(border, own_kids))
    kids_here = kid_parts[last]
    swap_factor = over_fronts(after(own_factor, kids_here), 1)
    kid_parts = spread(kid_parts, [own_kids], [pick_high])

    reduced, lift_high, lower_high, kid_sum = call(
        functools.partial(kid_kernel, pieces),
        (
            shape_of((2, own_border, kid_size)),
            shape_of((2, size, kid_size), half),
            shape_of((2, border_size, kid_size), half),
            shape_of((2, kid_size)),
        ),
        20,
        scratch=[
            pltpu.VMEM((kid_size, kid_size), half),
            pltpu.VMEM((kid_size, kid_size), half),
            pltpu.VMEM((size, kid_size), jnp.float32),
            pltpu.VMEM((border_size, kid_size), jnp.float32),
        ],
    )(index, pick_high, pick_low, own_factor, *kid_parts)

    border_high, border_lower = call(
        border_kernel, (shape_of(border.shape, half), shape_of((2, own_border, kid_size))), 8
    )(own_border_rows, lower_high)

    factor_parts = [own_factor, exchange(after(own_factor, kids_here), 1, 0)]
    for mask in list(keep_factor)[1:]:
        far_swap = exchange(after(keep_factor[mask], kids_here), 1, 0, 0)
        far_keep = exchange(after(swap_factor[mask], border_lower), 1, 0, 1)
        factor_parts += [keep_factor[mask], swap_factor[mask], far_keep, far_swap]
    total = call(
        functools.partial(image_kernel, pieces),
        shape_of((1, size + 2 * kid_size)),
        12,
        scratch=[
            pltpu.VMEM((border_size, size), half),
            pltpu.VMEM((own_border, size), half),
            pltpu.VMEM((own_border, size), half),
        ],
    )(
        *factor_parts,
        border_high,
        border_lower,
        weights,
        reduced,
        lift_high,
        diag_high,
        diag_low,
        parent_sum,
        kid_sum,
    )

    total = total + exchange(total, 1, 0)
    bit = 4
    while bit < pieces:
        total = total + exchange(total, 0, bit)
        bit *= 2
    near = range(min(pieces, 4))
    order = [mask for parity in (0, 1) for mask in near if mask % 2 == parity]
    partials = [exchange(total, 0, mask) if mask else total for mask in order]
    return call(finish_kernel, (shape_of((1, size)), shape_of((2, kid_size))), 2, scalars=1, loose=1, keep=False)(
        child_parent, *partials
    )


def solution(mesh):
    whole = P("leaf", "front", None)
    return jax.shard_map(
        shards,
        mesh=mesh,
        in_specs=(whole,) * 5 + (P(), P()),
        out_specs=(P("leaf", None), P("leaf", None)),
        check_vma=False,
    )
```

profile of v0, /device:TPU:0, one launch (start us, length us, event | category | flops | bytes accessed | tf_op | source)
XLA Modules:
  0.0 109.5 jit_solution(10864442381841976387)
XLA Ops:
  0.6 4.9 %collective-permute-start.4 = (f32[384,768]{1,0:T(8,128)}, f32[384,768]{1,0:T(8,128)S(1)}, u32[]{:S(2)}, u32[]{:S(2)}) collective-permute-start(f32[384,768]{1,0:T(8,128)} %bitcast.4), channel_id=1, source_target_pairs={{0,2},{2,0},{5,7},{7,5},{8,10},{10,8},{13,15},{15,13},{16,18},{18,... | collective-permute-start | bytes 3538952 | tf_op jit(solution)/shard_map/ppermute | solution.py:26
  5.5 0.1 collective-permute-start.2
  5.6 0.0 copy-start
  5.6 1.9 %collective-permute-start = (f32[192,768]{1,0:T(8,128)}, f32[192,768]{1,0:T(8,128)S(1)}, u32[]{:S(2)}, u32[]{:S(2)}) collective-permute-start(f32[192,768]{1,0:T(8,128)} %bitcast.6), channel_id=1, source_target_pairs={{0,0},{1,4},{2,2},{3,6},{4,1},{5,5},{6,3},{7,7},{8,8},{9,12},{10,1... | collective-permute-start | bytes 1769480 | tf_op jit(solution)/shard_map/ppermute | solution.py:36
  7.5 1.4 %collective-permute-start.3 = (f32[2,128,512]{2,1,0:T(8,128)}, f32[2,128,512]{2,1,0:T(8,128)S(1)}, u32[]{:S(2)}, u32[]{:S(2)}) collective-permute-start(f32[2,128,512]{2,1,0:T(8,128)} %own_inverse.1), channel_id=1, source_target_pairs={{0,4},{1,5},{2,6},{3,7},{4,0},{5,1},{6,2},{7,3},{8,12},{9,13},{10,... | collective-permute-start | bytes 1572872 | tf_op jit(solution)/shard_map/ppermute | solution.py:26
  8.8 1.7 %collective-permute-done.3.other_inverse = f32[2,128,512]{2,1,0:T(8,128)S(1)} collective-permute-done((f32[2,128,512]{2,1,0:T(8,128)}, f32[2,128,512]{2,1,0:T(8,128)S(1)}, u32[]{:S(2)}, u32[]{:S(2)}) %collective-permute-start.3) | collective-permute-done | bytes 524320 | tf_op jit(solution)/shard_map/ppermute | solution.py:26
  10.6 0.0 collective-permute-done.2.other_rows
  10.6 1.6 %shard_map.86 = (f32[2,384,512]{2,1,0:T(8,128)S(1)}, s32[2,4,256]{2,1,0:T(4,128)S(1)}) custom-call(s32[16]{0:T(128)} %parent_ref.3, s32[16,1024]{1,0:T(8,128)} %index_ref.1, f32[2,256,512]{2,1,0:T(8,128)} %own_rows.1, f32[2,128,512]{2,1,0:T(8,128)} %own_inverse.1, f32[2,256,512]{2,1,0:T(8,128)S(1)} %collective-permute-done.2.other_rows, ...), custom_call_target="tpu_custom_call" | custom-call | bytes 1000 | tf_op jit(solution)/shard_map/pallas_call | solution.py:256
  12.2 0.0 collective-permute-done.refs_0_
  12.2 7.7 %collective-permute-done.4.refs_2_ = f32[384,768]{1,0:T(8,128)S(1)} collective-permute-done((f32[384,768]{1,0:T(8,128)}, f32[384,768]{1,0:T(8,128)S(1)}, u32[]{:S(2)}, u32[]{:S(2)}) %collective-permute-start.4) | collective-permute-done | bytes 1179680 | tf_op jit(solution)/shard_map/ppermute | solution.py:26
  19.9 0.8 collective-permute-start.5
  20.7 2.1 %collective-permute-start.6 = (f32[192,768]{1,0:T(8,128)S(1)}, f32[192,768]{1,0:T(8,128)S(1)}, u32[]{:S(2)}, u32[]{:S(2)}) collective-permute-start(f32[192,768]{1,0:T(8,128)S(1)} %collective-permute-done.refs_0_), channel_id=1, source_target_pairs={{0,2},{1,3},{2,0},{3,1},{4,6},{5,7},{6,4},{7,5},{8,10},{9,11},{10,... | collective-permute-start | bytes 1769480 | tf_op jit(solution)/shard_map/ppermute | solution.py:26
  22.7 12.8 %collective-permute-done.6.refs_2_ = f32[192,768]{1,0:T(8,128)S(1)} collective-permute-done((f32[192,768]{1,0:T(8,128)S(1)}, f32[192,768]{1,0:T(8,128)S(1)}, u32[]{:S(2)}, u32[]{:S(2)}) %collective-permute-start.6) | collective-permute-done | bytes 589856 | tf_op jit(solution)/shard_map/ppermute | solution.py:26
  35.5 0.0 collective-permute-done.5.refs_0_
  35.5 0.5 collective-permute-start.7
  36.0 1.9 %collective-permute-start.1 = (f32[384,768]{1,0:T(8,128)}, f32[384,768]{1,0:T(8,128)S(1)}, u32[]{:S(2)}, u32[]{:S(2)}) collective-permute-start(f32[384,768]{1,0:T(8,128)} %bitcast.5), channel_id=1, source_target_pairs={{0,0},{1,4},{2,2},{3,6},{4,1},{5,5},{6,3},{7,7},{8,8},{9,12},{10,1... | collective-permute-start | bytes 3538952 | tf_op jit(solution)/shard_map/ppermute | solution.py:36
  37.9 0.0 copy-done
  37.9 0.8 collective-permute-start.10
  38.7 6.9 %collective-permute-start.12 = (f32[192,768]{1,0:T(8,128)S(1)}, f32[192,768]{1,0:T(8,128)S(1)}, u32[]{:S(2)}, u32[]{:S(2)}) collective-permute-start(f32[192,768]{1,0:T(8,128)S(1)} %collective-permute-done.6.refs_2_), channel_id=1, source_target_pairs={{0,4},{1,5},{2,6},{3,7},{4,0},{5,1},{6,2},{7,3},{8,12},{9,13},{10,... | collective-permute-start | bytes 1769480 | tf_op jit(solution)/shard_map/ppermute | solution.py:26
  45.6 0.1 collective-permute-start.11
  45.7 0.0 collective-permute-done.1.factor.refs_0_
  45.7 12.3 %collective-permute-start.13 = (f32[2,384,512]{2,1,0:T(8,128)S(1)}, f32[2,384,512]{2,1,0:T(8,128)S(1)}, u32[]{:S(2)}, u32[]{:S(2)}) collective-permute-start(f32[2,384,512]{2,1,0:T(8,128)S(1)} %collective-permute-done.5.refs_0_), channel_id=1, source_target_pairs={{0,4},{1,5},{2,6},{3,7},{4,0},{5,1},{6,2},{7,3},{8,12},{9,13},{10,... | collective-permute-start | bytes 4718600 | tf_op jit(solution)/shard_map/ppermute | solution.py:26
  58.0 0.0 collective-permute-done.12.refs_3_
  58.0 0.0 collective-permute-done.11.refs_1_
  58.0 7.2 %shard_map.87 = (bf16[768,768]{1,0:T(8,128)(2,1)S(1)}, bf16[768,768]{1,0:T(8,128)(2,1)S(1)}, bf16[2,4,768,256]{3,2,1,0:T(8,128)(2,1)S(1)}, bf16[2,4,768,256]{3,2...) custom-call(s32[2,4,256]{2,1,0:T(4,128)S(1)} %get-tuple-element.33.index, ...), custom_call_target="tpu_custom_call" | custom-call | bytes 1000 | tf_op jit(solution)/shard_map/pallas_call | solution.py:256
  65.1 4.1 %collective-permute-done.7.refs_2_ = f32[2,384,512]{2,1,0:T(8,128)S(1)} collective-permute-done((f32[2,384,512]{2,1,0:T(8,128)S(1)}, f32[2,384,512]{2,1,0:T(8,128)S(1)}, u32[]{:S(2)}, u32[]{:S(2)}) %collective-permute-start.7) | collective-permute-done | bytes 1572896 | tf_op jit(solution)/shard_map/ppermute | solution.py:26
  69.2 3.4 %collective-permute-start.14 = (f32[2,384,512]{2,1,0:T(8,128)S(1)}, f32[2,384,512]{2,1,0:T(8,128)S(1)}, u32[]{:S(2)}, u32[]{:S(2)}) collective-permute-start(f32[2,384,512]{2,1,0:T(8,128)S(1)} %collective-permute-done.7.refs_2_), channel_id=1, source_target_pairs={{0,4},{1,5},{2,6},{3,7},{4,0},{5,1},{6,2},{7,3},{8,12},{9,13},{10,... | collective-permute-start | bytes 4718600 | tf_op jit(solution)/shard_map/ppermute | solution.py:26
  72.6 0.7 collective-permute-start.9
  73.3 1.5 %collective-permute-start.8 = (f32[384,768]{1,0:T(8,128)S(1)}, f32[384,768]{1,0:T(8,128)S(1)}, u32[]{:S(2)}, u32[]{:S(2)}) collective-permute-start(f32[384,768]{1,0:T(8,128)S(1)} %collective-permute-done.1.factor.refs_0_), channel_id=1, source_target_pairs={{0,4},{1,5},{2,6},{3,7},{4,0},{5,1},{6,2},{7,3},{8,12},{9,13},{10,... | collective-permute-start | bytes 3538952 | tf_op jit(solution)/shard_map/ppermute | solution.py:26
  74.8 0.0 collective-permute-done.13.refs_1_
  74.8 2.2 %collective-permute-start.16 = (f32[384,768]{1,0:T(8,128)S(1)}, f32[384,768]{1,0:T(8,128)S(1)}, u32[]{:S(2)}, u32[]{:S(2)}) collective-permute-start(f32[384,768]{1,0:T(8,128)S(1)} %collective-permute-done.4.refs_2_), channel_id=1, source_target_pairs={{0,4},{2,6},{5,1},{7,3},{8,12},{10,14},{13,9},{15,11},{16,20},{18,... | collective-permute-start | bytes 3538952 | tf_op jit(solution)/shard_map/ppermute | solution.py:26
  77.0 0.0 collective-permute-done.14.refs_3_
  77.0 13.6 %shard_map.88 = (f32[2,384,512]{2,1,0:T(8,128)S(1)}, bf16[2,768,512]{2,1,0:T(8,128)(2,1)S(1)}, bf16[2,1536,512]{2,1,0:T(8,128)(2,1)S(1)}, f32[2,512]{1,0:T(2,128)S(1)}) custom-call(s32[2,4,256]{2,1,0:T(4,128)S(1)} %get-tuple-element.33.index, bf16[2,4,768,256]{3,2,1,0:T(8,128)(2,1)S(1)} %get-tuple-element.36.pick_high, ...), custom_call_target="tpu_custom_call" | custom-call | bytes 1000 | tf_op jit(solution)/shard_map/pallas_call | solution.py:256
  90.6 0.0 collective-permute-done.10.border
  90.6 1.4 %shard_map.89 = (bf16[384,1536]{1,0:T(8,128)(2,1)S(1)}, f32[2,384,512]{2,1,0:T(8,128)S(1)}) custom-call(f32[384,1536]{1,0:T(8,128)S(1)} %collective-permute-done.10.border, bf16[2,1536,512]{2,1,0:T(8,128)(2,1)S(1)} %get-tuple-element.40.lower_high), custom_call_target="tpu_custom_call" | custom-call | bytes 1000 | tf_op jit(solution)/shard_map/pallas_call | solution.py:256
  92.0 0.0 collective-permute-done.9.refs_3_
  92.0 1.3 %collective-permute-start.15 = (f32[384,768]{1,0:T(8,128)S(1)}, f32[384,768]{1,0:T(8,128)S(1)}, u32[]{:S(2)}, u32[]{:S(2)}) collective-permute-start(f32[384,768]{1,0:T(8,128)S(1)} %collective-permute-done.9.refs_3_), channel_id=1, source_target_pairs={{1,5},{3,7},{4,0},{6,2},{9,13},{11,15},{12,8},{14,10},{17,21},{19,... | collective-permute-start | bytes 3538952 | tf_op jit(solution)/shard_map/ppermute | solution.py:26
  93.3 0.0 collective-permute-done.8.refs_1_
  93.3 0.0 collective-permute-done.16.refs_5_
  93.3 3.4 %collective-permute-done.15.refs_4_ = f32[384,768]{1,0:T(8,128)S(1)} collective-permute-done((f32[384,768]{1,0:T(8,128)S(1)}, f32[384,768]{1,0:T(8,128)S(1)}, u32[]{:S(2)}, u32[]{:S(2)}) %collective-permute-start.15) | collective-permute-done | bytes 1179680 | tf_op jit(solution)/shard_map/ppermute | solution.py:26
  96.8 3.7 %shard_map.90 = f32[1,1792]{1,0:T(1,128)S(1)} custom-call(f32[384,768]{1,0:T(8,128)S(1)} %collective-permute-done.1.factor.refs_0_, f32[384,768]{1,0:T(8,128)S(1)} %collective-permute-done.8.refs_1_, f32[384,768]{1,0:T(8,128)S(1)} %collective-permute-done.4.refs_2_, f32[384,768]{1,0:T(8,128)S(1)} %collective-permute-done.9.refs_3_, ...), custom_call_target="tpu_custom_call" | custom-call | bytes 1000 | tf_op jit(solution)/shard_map/pallas_call | solution.py:256
  100.5 0.2 collective-permute-start.17
  100.7 1.0 collective-permute-done.17
  101.7 1.6 %collective-permute-start.18 = (f32[1,1792]{1,0:T(1,128)S(1)}, f32[1,1792]{1,0:T(1,128)S(1)}, u32[]{:S(2)}, u32[]{:S(2)}) collective-permute-start(f32[1,1792]{1,0:T(1,128)S(1)} %add.3.refs_0_), channel_id=1, source_target_pairs={{0,2},{1,3},{2,0},{3,1},{4,6},{5,7},{6,4},{7,5},{8,10},{9,11},{10,... | collective-permute-start | bytes 21512 | tf_op jit(solution)/shard_map/ppermute | solution.py:26
  103.3 0.3 collective-permute-start.19
  103.6 1.7 %collective-permute-start.20 = (f32[1,1792]{1,0:T(1,128)S(1)}, f32[1,1792]{1,0:T(1,128)S(1)}, u32[]{:S(2)}, u32[]{:S(2)}) collective-permute-start(f32[1,1792]{1,0:T(1,128)S(1)} %add.3.refs_0_), channel_id=1, source_target_pairs={{0,3},{1,2},{2,1},{3,0},{4,7},{5,6},{6,5},{7,4},{8,11},{9,10},{10,... | collective-permute-start | bytes 21512 | tf_op jit(solution)/shard_map/ppermute | solution.py:26
  105.3 0.2 collective-permute-done.18.refs_1_
  105.4 1.5 %collective-permute-done.19.refs_2_ = f32[1,1792]{1,0:T(1,128)S(1)} collective-permute-done((f32[1,1792]{1,0:T(1,128)S(1)}, f32[1,1792]{1,0:T(1,128)S(1)}, u32[]{:S(2)}, u32[]{:S(2)}) %collective-permute-start.19) | collective-permute-done | bytes 7200 | tf_op jit(solution)/shard_map/ppermute | solution.py:26
  107.0 1.2 %collective-permute-done.20.refs_3_ = f32[1,1792]{1,0:T(1,128)S(1)} collective-permute-done((f32[1,1792]{1,0:T(1,128)S(1)}, f32[1,1792]{1,0:T(1,128)S(1)}, u32[]{:S(2)}, u32[]{:S(2)}) %collective-permute-start.20) | collective-permute-done | bytes 7200 | tf_op jit(solution)/shard_map/ppermute | solution.py:26
  108.2 1.3 %shard_map.91 = (f32[1,768]{1,0:T(1,128)}, f32[2,512]{1,0:T(2,128)}) custom-call(s32[16]{0:T(128)} %parent_ref.3, f32[1,1792]{1,0:T(1,128)S(1)} %add.3.refs_0_, f32[1,1792]{1,0:T(1,128)S(1)} %collective-permute-done.18.refs_1_, f32[1,1792]{1,0:T(1,128)S(1)} %collective-permute-done.19.refs_2_, f32[1,1792]{1,0:T(1,128)S(1)} %collective-permute-done.20.refs_3_), custom_call_target="tpu_custom_call" | custom-call | bytes 1000 | tf_op jit(solution)/shard_map/pallas_call | solution.py:256
  (1 shorter events, 0.0 us)
Async XLA Ops:
  0.6 19.3 %collective-permute-start.4 = (f32[384,768]{1,0:T(8,128)}, f32[384,768]{1,0:T(8,128)S(1)}, u32[]{:S(2)}, u32[]{:S(2)}) collective-permute-start(f32[384,768]{1,0:T(8,128)} %bitcast.4), channel_id=1, source_target_pairs={{0,2},{2,0},{5,7},{7,5},{8,10},{10,8},{13,15},{15,13},{16,18},{18,... | collective-permute-start | bytes 3538952 | tf_op jit(solution)/shard_map/ppermute | solution.py:26
  5.5 5.1 %collective-permute-start.2 = (f32[2,256,512]{2,1,0:T(8,128)}, f32[2,256,512]{2,1,0:T(8,128)S(1)}, u32[]{:S(2)}, u32[]{:S(2)}) collective-permute-start(f32[2,256,512]{2,1,0:T(8,128)} %own_rows.1), channel_id=1, source_target_pairs={{0,4},{1,5},{2,6},{3,7},{4,0},{5,1},{6,2},{7,3},{8,12},{9,13},{10,... | collective-permute-start | bytes 3145736 | tf_op jit(solution)/shard_map/ppermute | solution.py:26
  5.6 32.3 %copy-start = (f32[1,384,1536]{2,1,0:T(8,128)S(1)}, f32[1,384,1536]{2,1,0:T(8,128)}, u32[]{:S(2)}) copy-start(f32[1,384,1536]{2,1,0:T(8,128)} %param.7) | copy-start | bytes 7077892
  5.6 6.6 %collective-permute-start = (f32[192,768]{1,0:T(8,128)}, f32[192,768]{1,0:T(8,128)S(1)}, u32[]{:S(2)}, u32[]{:S(2)}) collective-permute-start(f32[192,768]{1,0:T(8,128)} %bitcast.6), channel_id=1, source_target_pairs={{0,0},{1,4},{2,2},{3,6},{4,1},{5,5},{6,3},{7,7},{8,8},{9,12},{10,1... | collective-permute-start | bytes 1769480 | tf_op jit(solution)/shard_map/ppermute | solution.py:36
  7.5 3.1 %collective-permute-start.3 = (f32[2,128,512]{2,1,0:T(8,128)}, f32[2,128,512]{2,1,0:T(8,128)S(1)}, u32[]{:S(2)}, u32[]{:S(2)}) collective-permute-start(f32[2,128,512]{2,1,0:T(8,128)} %own_inverse.1), channel_id=1, source_target_pairs={{0,4},{1,5},{2,6},{3,7},{4,0},{5,1},{6,2},{7,3},{8,12},{9,13},{10,... | collective-permute-start | bytes 1572872 | tf_op jit(solution)/shard_map/ppermute | solution.py:26
  19.9 15.6 %collective-permute-start.5 = (f32[2,384,512]{2,1,0:T(8,128)S(1)}, f32[2,384,512]{2,1,0:T(8,128)S(1)}, u32[]{:S(2)}, u32[]{:S(2)}) collective-permute-start(f32[2,384,512]{2,1,0:T(8,128)S(1)} %get-tuple-element.29), channel_id=1, source_target_pairs={{0,0},{1,4},{2,2},{3,6},{4,1},{5,5},{6,3},{7,7},{8,8},{9,12},{10,1... | collective-permute-start | bytes 4718600 | tf_op jit(solution)/shard_map/ppermute | solution.py:36
  20.7 14.8 %collective-permute-start.6 = (f32[192,768]{1,0:T(8,128)S(1)}, f32[192,768]{1,0:T(8,128)S(1)}, u32[]{:S(2)}, u32[]{:S(2)}) collective-permute-start(f32[192,768]{1,0:T(8,128)S(1)} %collective-permute-done.refs_0_), channel_id=1, source_target_pairs={{0,2},{1,3},{2,0},{3,1},{4,6},{5,7},{6,4},{7,5},{8,10},{9,11},{10,... | collective-permute-start | bytes 1769480 | tf_op jit(solution)/shard_map/ppermute | solution.py:26
  35.5 33.7 %collective-permute-start.7 = (f32[2,384,512]{2,1,0:T(8,128)S(1)}, f32[2,384,512]{2,1,0:T(8,128)S(1)}, u32[]{:S(2)}, u32[]{:S(2)}) collective-permute-start(f32[2,384,512]{2,1,0:T(8,128)S(1)} %collective-permute-done.5.refs_0_), channel_id=1, source_target_pairs={{0,2},{1,3},{2,0},{3,1},{4,6},{5,7},{6,4},{7,5},{8,10},{9,11},{10,... | collective-permute-start | bytes 4718600 | tf_op jit(solution)/shard_map/ppermute | solution.py:26
  36.0 9.7 %collective-permute-start.1 = (f32[384,768]{1,0:T(8,128)}, f32[384,768]{1,0:T(8,128)S(1)}, u32[]{:S(2)}, u32[]{:S(2)}) collective-permute-start(f32[384,768]{1,0:T(8,128)} %bitcast.5), channel_id=1, source_target_pairs={{0,0},{1,4},{2,2},{3,6},{4,1},{5,5},{6,3},{7,7},{8,8},{9,12},{10,1... | collective-permute-start | bytes 3538952 | tf_op jit(solution)/shard_map/ppermute | solution.py:36
  37.9 52.7 %collective-permute-start.10 = (f32[384,1536]{1,0:T(8,128)S(1)}, f32[384,1536]{1,0:T(8,128)S(1)}, u32[]{:S(2)}, u32[]{:S(2)}) collective-permute-start(f32[384,1536]{1,0:T(8,128)S(1)} %bitcast.3), channel_id=1, source_target_pairs={{0,0},{1,4},{2,2},{3,6},{4,1},{5,5},{6,3},{7,7},{8,8},{9,12},{10,1... | collective-permute-start | bytes 7077896 | tf_op jit(solution)/shard_map/ppermute | solution.py:36
  38.7 19.2 %collective-permute-start.12 = (f32[192,768]{1,0:T(8,128)S(1)}, f32[192,768]{1,0:T(8,128)S(1)}, u32[]{:S(2)}, u32[]{:S(2)}) collective-permute-start(f32[192,768]{1,0:T(8,128)S(1)} %collective-permute-done.6.refs_2_), channel_id=1, source_target_pairs={{0,4},{1,5},{2,6},{3,7},{4,0},{5,1},{6,2},{7,3},{8,12},{9,13},{10,... | collective-permute-start | bytes 1769480 | tf_op jit(solution)/shard_map/ppermute | solution.py:26
  45.6 12.4 %collective-permute-start.11 = (f32[192,768]{1,0:T(8,128)S(1)}, f32[192,768]{1,0:T(8,128)S(1)}, u32[]{:S(2)}, u32[]{:S(2)}) collective-permute-start(f32[192,768]{1,0:T(8,128)S(1)} %collective-permute-done.refs_0_), channel_id=1, source_target_pairs={{0,4},{1,5},{2,6},{3,7},{4,0},{5,1},{6,2},{7,3},{8,12},{9,13},{10,... | collective-permute-start | bytes 1769480 | tf_op jit(solution)/shard_map/ppermute | solution.py:26
  45.7 29.1 %collective-permute-start.13 = (f32[2,384,512]{2,1,0:T(8,128)S(1)}, f32[2,384,512]{2,1,0:T(8,128)S(1)}, u32[]{:S(2)}, u32[]{:S(2)}) collective-permute-start(f32[2,384,512]{2,1,0:T(8,128)S(1)} %collective-permute-done.5.refs_0_), channel_id=1, source_target_pairs={{0,4},{1,5},{2,6},{3,7},{4,0},{5,1},{6,2},{7,3},{8,12},{9,13},{10,... | collective-permute-start | bytes 4718600 | tf_op jit(solution)/shard_map/ppermute | solution.py:26
  69.2 7.8 %collective-permute-start.14 = (f32[2,384,512]{2,1,0:T(8,128)S(1)}, f32[2,384,512]{2,1,0:T(8,128)S(1)}, u32[]{:S(2)}, u32[]{:S(2)}) collective-permute-start(f32[2,384,512]{2,1,0:T(8,128)S(1)} %collective-permute-done.7.refs_2_), channel_id=1, source_target_pairs={{0,4},{1,5},{2,6},{3,7},{4,0},{5,1},{6,2},{7,3},{8,12},{9,13},{10,... | collective-permute-start | bytes 4718600 | tf_op jit(solution)/shard_map/ppermute | solution.py:26
  72.6 19.4 %collective-permute-start.9 = (f32[384,768]{1,0:T(8,128)S(1)}, f32[384,768]{1,0:T(8,128)S(1)}, u32[]{:S(2)}, u32[]{:S(2)}) collective-permute-start(f32[384,768]{1,0:T(8,128)S(1)} %collective-permute-done.1.factor.refs_0_), channel_id=1, source_target_pairs={{1,3},{3,1},{4,6},{6,4},{9,11},{11,9},{12,14},{14,12},{17,19},{19,... | collective-permute-start | bytes 3538952 | tf_op jit(solution)/shard_map/ppermute | solution.py:26
  73.3 20.0 %collective-permute-start.8 = (f32[384,768]{1,0:T(8,128)S(1)}, f32[384,768]{1,0:T(8,128)S(1)}, u32[]{:S(2)}, u32[]{:S(2)}) collective-permute-start(f32[384,768]{1,0:T(8,128)S(1)} %collective-permute-done.1.factor.refs_0_), channel_id=1, source_target_pairs={{0,4},{1,5},{2,6},{3,7},{4,0},{5,1},{6,2},{7,3},{8,12},{9,13},{10,... | collective-permute-start | bytes 3538952 | tf_op jit(solution)/shard_map/ppermute | solution.py:26
  74.8 18.5 %collective-permute-start.16 = (f32[384,768]{1,0:T(8,128)S(1)}, f32[384,768]{1,0:T(8,128)S(1)}, u32[]{:S(2)}, u32[]{:S(2)}) collective-permute-start(f32[384,768]{1,0:T(8,128)S(1)} %collective-permute-done.4.refs_2_), channel_id=1, source_target_pairs={{0,4},{2,6},{5,1},{7,3},{8,12},{10,14},{13,9},{15,11},{16,20},{18,... | collective-permute-start | bytes 3538952 | tf_op jit(solution)/shard_map/ppermute | solution.py:26
  92.0 4.7 %collective-permute-start.15 = (f32[384,768]{1,0:T(8,128)S(1)}, f32[384,768]{1,0:T(8,128)S(1)}, u32[]{:S(2)}, u32[]{:S(2)}) collective-permute-start(f32[384,768]{1,0:T(8,128)S(1)} %collective-permute-done.9.refs_3_), channel_id=1, source_target_pairs={{1,5},{3,7},{4,0},{6,2},{9,13},{11,15},{12,8},{14,10},{17,21},{19,... | collective-permute-start | bytes 3538952 | tf_op jit(solution)/shard_map/ppermute | solution.py:26
  100.5 1.2 %collective-permute-start.17 = (f32[1,1792]{1,0:T(1,128)S(1)}, f32[1,1792]{1,0:T(1,128)S(1)}, u32[]{:S(2)}, u32[]{:S(2)}) collective-permute-start(f32[1,1792]{1,0:T(1,128)S(1)} %shard_map.90), channel_id=1, source_target_pairs={{0,4},{1,5},{2,6},{3,7},{4,0},{5,1},{6,2},{7,3},{8,12},{9,13},{10,... | collective-permute-start | bytes 21512 | tf_op jit(solution)/shard_map/ppermute | solution.py:26
  101.7 3.7 %collective-permute-start.18 = (f32[1,1792]{1,0:T(1,128)S(1)}, f32[1,1792]{1,0:T(1,128)S(1)}, u32[]{:S(2)}, u32[]{:S(2)}) collective-permute-start(f32[1,1792]{1,0:T(1,128)S(1)} %add.3.refs_0_), channel_id=1, source_target_pairs={{0,2},{1,3},{2,0},{3,1},{4,6},{5,7},{6,4},{7,5},{8,10},{9,11},{10,... | collective-permute-start | bytes 21512 | tf_op jit(solution)/shard_map/ppermute | solution.py:26
  103.3 3.6 %collective-permute-start.19 = (f32[1,1792]{1,0:T(1,128)S(1)}, f32[1,1792]{1,0:T(1,128)S(1)}, u32[]{:S(2)}, u32[]{:S(2)}) collective-permute-start(f32[1,1792]{1,0:T(1,128)S(1)} %add.3.refs_0_), channel_id=1, source_target_pairs={{0,1},{1,0},{2,3},{3,2},{4,5},{5,4},{6,7},{7,6},{8,9},{9,8},{10,11... | collective-permute-start | bytes 21512 | tf_op jit(solution)/shard_map/ppermute | solution.py:26
  103.6 4.5 %collective-permute-start.20 = (f32[1,1792]{1,0:T(1,128)S(1)}, f32[1,1792]{1,0:T(1,128)S(1)}, u32[]{:S(2)}, u32[]{:S(2)}) collective-permute-start(f32[1,1792]{1,0:T(1,128)S(1)} %add.3.refs_0_), channel_id=1, source_target_pairs={{0,3},{1,2},{2,1},{3,0},{4,7},{5,6},{6,5},{7,4},{8,11},{9,10},{10,... | collective-permute-start | bytes 21512 | tf_op jit(solution)/shard_map/ppermute | solution.py:26
where the time goes:
time: 110 us; the launch traced here: 109 us
  starting transfers between devices  46.3 us (42%)
  waiting for transfers between devices  33.6 us (31%)
  Pallas kernels  28.8 us (26%)
    ppermute x17, starting transfers between devices, exchange(): return lax.ppermute(value, ('leaf', 'front'), pairs)  40.9 us
    ppermute x17, waiting for transfers between devices, exchange(): return lax.ppermute(value, ('leaf', 'front'), pairs)  33.6 us
    pallas_call x6, Pallas kernels, run(): pl.pallas_call(kernel, out_shape=results, in_specs=specs, out_specs=jax.t...  28.8 us
    ppermute x4, starting transfers between devices, cross(): return lax.ppermute(value, ('leaf', 'front'), pairs)  5.32 us
  transfers between devices with their start and end apart: 21, of which 9 were waited for; matrix products, arithmetic and copies ran while one was open for 0% of the time, Pallas kernels for 22%

commit v1 on v0

--- a/solution.py
+++ b/solution.py
@@ -131,37 +131,16 @@
     return pairs
 
 
-def diagonal_kernel(pieces, index, factor, *refs):
-    diagonal = refs[:pieces]
-    diag_high, diag_low, pick_high, pick_low, weights, parent_sum = refs[pieces:]
+def kid_kernel(pieces, index, *refs):
+    kids = refs[:pieces]
+    up_high, lower_high, own_lower, inv_sum, inv_high, inv_low, upper, lower = refs[pieces:]
     _, block = place_of()
-    own_rows, size = diagonal[0].shape
-    parent_sum[...] = column_sum(diagonal[0][...] * diagonal[0][...])
-    for mask in range(pieces):
-        start = pl.multiple_of((block ^ mask) * own_rows, 16)
-        high, low = halves(diagonal[mask][...])
-        diag_high[pl.ds(start, own_rows), :] = high
-        diag_low[pl.ds(start, own_rows), :] = low
-    for kid in range(2):
-        for mask in range(pieces):
-            pick = picks(index[kid, mask : mask + 1, :], 0, size)
-            pick_high[kid, mask] = rounded(dot(diag_high[...], pick))
-            pick_low[kid, mask] = rounded(dot(diag_low[...], pick))
-    factor_halves = halves(factor[...])
-    for span in spans(size):
-        weights[:, span] = product(factor_halves, (diag_high[:, span], diag_low[:, span]))
-
-
-def kid_kernel(pieces, index, pick_high, pick_low, factor, *refs):
-    kids = refs[:pieces]
-    reduced, lift_high, lower_high, kid_sum, inv_high, inv_low, lifted, lower = refs[pieces:]
-    _, block = place_of()
-    size, own_border, border_size = lifted.shape[0], factor.shape[0], lower.shape[0]
+    size, border_size, own_border = upper.shape[0], lower.shape[0], own_lower.shape[1]
     kid_block = index.shape[2]
-    inv_block, own_rows = kids[0].shape[1] - kid_block, size // pieces
-    factor_high = rounded(factor[...])
+    inv_block = kids[0].shape[1] - kid_block
     for kid in range(2):
         own_inverse = kids[0][kid, kid_block:]
+        inv_sum[kid : kid + 1] = column_sum(own_inverse * own_inverse)
         for mask in range(pieces):
             start = pl.multiple_of((block ^ mask) * inv_block, 16)
             high, low = halves(kids[mask][kid, kid_block:])
@@ -170,23 +149,49 @@
         inverse = inv_high[...], inv_low[...]
         for mask in range(pieces):
             high, low = halves(product(halves(kids[mask][kid, :kid_block]), inverse))
-            lifted_part = dot(pick_high[kid, mask], high) + dot(pick_low[kid, mask], high)
             places = index[kid, mask : mask + 1, :]
+            up_part = dot(picks(places, 0, size), high)
+            part = dot(picks(places, size, border_size), high)
             low_part = dot(picks(places, size + block * own_border, own_border), low)
-            part = dot(picks(places, size, border_size), high)
-            lifted[...] = lifted_part if mask == 0 else lifted[...] + lifted_part
-            reduced[kid] = low_part if mask == 0 else reduced[kid] + low_part
+            upper[...] = up_part if mask == 0 else upper[...] + up_part
             lower[...] = part if mask == 0 else lower[...] + part
+            own_lower[kid] = low_part if mask == 0 else own_lower[kid] + low_part
+        up_high[kid] = rounded(upper[...])
+        lower_high[kid] = rounded(lower[...])
+        own_lower[kid] = own_lower[kid] + lower[pl.ds(pl.multiple_of(block * own_border, 8), own_border), :]
+
+
+def lift_kernel(pieces, factor, up_high, own_lower, inv_sum, *refs):
+    reduced, lift_high, diag_high, diag_low, weights, parent_sum, kid_sum, lifted = refs[2 * pieces - 2 :]
+    _, block = place_of()
+    own_rows, size = refs[0].shape
+    parent_sum[...] = column_sum(refs[0][...] * refs[0][...])
+    for mask, pair in enumerate(unpacked(pieces, refs)):
+        start = pl.multiple_of((block ^ mask) * own_rows, 16)
+
+        def put(ref, start=start):
+            diag_high[pl.ds(start, own_rows), :], diag_low[pl.ds(start, own_rows), :] = halves(ref[...])
+
+        if mask < 2:
+            put(pair[0])
+        else:
+            store(pair, put)
+    factor_halves = halves(factor[...])
+    for kid in range(2):
+        lifted[...] = dot(diag_high[...], up_high[kid]) + dot(diag_low[...], up_high[kid])
         own = lifted[pl.ds(pl.multiple_of(block * own_rows, 16), own_rows), :]
-        kid_sum[kid : kid + 1] = column_sum(own_inverse * own_inverse) + column_sum(own * own)
+        kid_sum[kid : kid + 1] = inv_sum[kid : kid + 1] + column_sum(own * own)
         lift_high[kid] = rounded(lifted[...])
-        lower_high[kid] = rounded(lower[...])
-        own_lower = lower[pl.ds(pl.multiple_of(block * own_border, 8), own_border), :]
-        reduced[kid] = own_lower + reduced[kid] - dot(factor_high, lift_high[kid])
-
-
-def border_kernel(border, lower_high, border_high, border_lower):
-    border_high[...] = rounded(border[...])
+        reduced[kid] = own_lower[kid] - dot(factor_halves[0], lift_high[kid])
+    for span in spans(size):
+        weights[:, span] = product(factor_halves, (diag_high[:, span], diag_low[:, span]))
+
+
+def border_kernel(top, rest, lower_high, border_high, border_lower):
+    start = 0
+    for part in (top, rest):
+        border_high[start : start + part.shape[0]] = rounded(part[...])
+        start += part.shape[0]
     for kid in range(2):
         for span in spans(lower_high.shape[2]):
             border_lower[kid, :, span] = dot(border_high[...], lower_high[kid, :, span])
@@ -288,42 +293,40 @@
         parts = parts | others
         return [parts[mask] for mask in range(pieces)]
 
+    def gathered(own, keep, swap, gate_own, gate_keep, gate_swap):
+        result = [own, exchange(after(own, *gate_own), 1, 0)]
+        for mask in list(keep)[1:]:
+            far_swap = exchange(after(keep[mask], *gate_keep), 1, 0, 0)
+            far_keep = exchange(after(swap[mask], *gate_swap), 1, 0, 1)
+            result += [keep[mask], swap[mask], far_keep, far_swap]
+        return result
+
     last = pieces - 2
+    top = -(-own_border // 48) * 16
+    border_top, border_rest = border[:top], border[top:]
     keep_factor = over_fronts(factor, 0)
-    own_diagonal = cross(diagonal)
     kid_shape = (2, kid_block + kid_inverse.shape[1], kid_size)
     own_kids, index = call(
         select_kernel, (shape_of(kid_shape), shape_of((2, pieces, kid_block), jnp.int32)), 6, scalars=1, loose=4
     )(child_parent, child_index, kid_rows, kid_inverse, exchange(kid_rows, 1, 0), exchange(kid_inverse, 1, 0))
-    own_kids = cross(after(own_kids, own_diagonal, keep_factor[last]))
-    diagonal_parts = over_fronts(own_diagonal)
-    kid_parts = over_fronts(after(own_kids, diagonal_parts[last]))
-    own_factor = cross(after(factor, own_diagonal))
-    diagonal_parts = spread(diagonal_parts, [own_kids], [own_kids])
-
-    diag_high, diag_low, pick_high, pick_low, weights, parent_sum = call(
-        functools.partial(diagonal_kernel, pieces),
-        (
-            shape_of((size, size), half),
-            shape_of((size, size), half),
-            shape_of((2, pieces, size, kid_block), half),
-            shape_of((2, pieces, size, kid_block), half),
-            shape_of((own_border, size)),
-            shape_of((1, size)),
-        ),
-        10,
-    )(index, own_factor, *diagonal_parts)
-    own_border_rows = cross(after(border, own_kids))
+    own_kids = cross(own_kids)
+    kid_parts = over_fronts(own_kids)
     kids_here = kid_parts[last]
+    own_top = cross(after(border_top, own_kids))
+    own_diagonal = cross(after(diagonal, own_kids, keep_factor[last]))
+    own_factor = cross(after(factor, own_kids))
+    own_rest = cross(after(border_rest, own_top))
+    keep_diagonal = over_fronts(own_diagonal, 0)
+    swap_diagonal = over_fronts(own_diagonal, 1)
     swap_factor = over_fronts(after(own_factor, kids_here), 1)
-    kid_parts = spread(kid_parts, [own_kids], [pick_high])
-
-    reduced, lift_high, lower_high, kid_sum = call(
+    kid_parts = spread(kid_parts, [own_diagonal], [keep_diagonal[last], own_factor, own_top])
+
+    up_high, lower_high, own_lower, inv_sum = call(
         functools.partial(kid_kernel, pieces),
         (
-            shape_of((2, own_border, kid_size)),
             shape_of((2, size, kid_size), half),
             shape_of((2, border_size, kid_size), half),
+            shape_of((2, own_border, kid_size)),
             shape_of((2, kid_size)),
         ),
         20,
@@ -333,17 +336,29 @@
             pltpu.VMEM((size, kid_size), jnp.float32),
             pltpu.VMEM((border_size, kid_size), jnp.float32),
         ],
-    )(index, pick_high, pick_low, own_factor, *kid_parts)
+    )(index, *kid_parts)
+    diagonal_parts = gathered(own_diagonal, keep_diagonal, swap_diagonal, [up_high], [up_high], [up_high])
+
+    reduced, lift_high, diag_high, diag_low, weights, parent_sum, kid_sum = call(
+        functools.partial(lift_kernel, pieces),
+        (
+            shape_of((2, own_border, kid_size)),
+            shape_of((2, size, kid_size), half),
+            shape_of((size, size), half),
+            shape_of((size, size), half),
+            shape_of((own_border, size)),
+            shape_of((1, size)),
+            shape_of((2, kid_size)),
+        ),
+        12,
+        scratch=[pltpu.VMEM((size, kid_size), jnp.float32)],
+    )(own_factor, up_high, own_lower, inv_sum, *diagonal_parts)
 
     border_high, border_lower = call(
         border_kernel, (shape_of(border.shape, half), shape_of((2, own_border, kid_size))), 8
-    )(own_border_rows, lower_high)
-
-    factor_parts = [own_factor, exchange(after(own_factor, kids_here), 1, 0)]
-    for mask in list(keep_factor)[1:]:
-        far_swap = exchange(after(keep_factor[mask], kids_here), 1, 0, 0)
-        far_keep = exchange(after(swap_factor[mask], border_lower), 1, 0, 1)
-        factor_parts += [keep_factor[mask], swap_factor[mask], far_keep, far_swap]
+    )(own_top, own_rest, lower_high)
+
+    factor_parts = gathered(own_factor, keep_factor, swap_factor, [kids_here], [kids_here], [lift_high, own_rest])
     total = call(
         functools.partial(image_kernel, pieces),
         shape_of((1, size + 2 * kid_size)),

time: 110 us -> 118 us (1.073)
  waiting for transfers between devices: 33.6 us -> 50.2 us
  Pallas kernels: 28.8 us -> 23.9 us
  starting transfers between devices: 46.3 us -> 42.6 us
    ppermute x17 -> x19, waiting for transfers between devices: 33.6 us -> 50.2 us  [exchange(): return lax.ppermute(value, ('leaf', 'front'), pairs)]
    pallas_call x6, Pallas kernels: 28.8 us -> 23.9 us  [run(): pl.pallas_call(kernel, out_shape=results, in_specs=specs, out_specs=jax.t...]
    ppermute x17 -> x19, starting transfers between devices: 40.9 us -> 37.8 us  [exchange(): return lax.ppermute(value, ('leaf', 'front'), pairs)]
    ppermute x4 -> x5, starting transfers between devices: 5.32 us -> 4.85 us  [cross(): return lax.ppermute(value, ('leaf', 'front'), pairs)]
  transfers between devices with their start and end apart: 21 -> 24, of which waited for: 9 -> 9; matrix products, arithmetic and copies ran while one was open for 0% -> 0% of each run, Pallas kernels for 22% -> 15%
where the time goes in v1:
time: 118 us
  waiting for transfers between devices  50.2 us (43%)
  starting transfers between devices  42.6 us (36%)
  Pallas kernels  23.9 us (20%)
    ppermute x19, waiting for transfers between devices, exchange(): return lax.ppermute(value, ('leaf', 'front'), pairs)  50.2 us
    ppermute x19, starting transfers between devices, exchange(): return lax.ppermute(value, ('leaf', 'front'), pairs)  37.8 us
    pallas_call x6, Pallas kernels, run(): pl.pallas_call(kernel, out_shape=results, in_specs=specs, out_specs=jax.t...  23.9 us
    ppermute x5, starting transfers between devices, cross(): return lax.ppermute(value, ('leaf', 'front'), pairs)  4.85 us
  transfers between devices with their start and end apart: 24, of which 9 were waited for; matrix products, arithmetic and copies ran while one was open for 0% of the time, Pallas kernels for 15%

profile of v1, /device:TPU:0, one launch (start us, length us, event | category | flops | bytes accessed | tf_op | source)
XLA Modules:
  0.0 117.8 jit_solution(9513482748128062756)
XLA Ops:
  0.6 0.0 copy-start.1
  0.6 0.0 copy-start
  0.7 0.5 collective-permute-start
  1.2 0.1 collective-permute-start.1
  1.2 3.2 %collective-permute-done.1.other_inverse = f32[2,128,512]{2,1,0:T(8,128)S(1)} collective-permute-done((f32[2,128,512]{2,1,0:T(8,128)}, f32[2,128,512]{2,1,0:T(8,128)S(1)}, u32[]{:S(2)}, u32[]{:S(2)}) %collective-permute-start.1) | collective-permute-done | bytes 524320 | tf_op jit(solution)/shard_map/ppermute | solution.py:26
  4.4 0.0 collective-permute-done.other_rows
  4.4 1.6 %shard_map.86 = (f32[2,384,512]{2,1,0:T(8,128)S(1)}, s32[2,4,256]{2,1,0:T(4,128)S(1)}) custom-call(s32[16]{0:T(128)} %parent_ref.3, s32[16,1024]{1,0:T(8,128)} %index_ref.1, f32[2,256,512]{2,1,0:T(8,128)} %own_rows.1, f32[2,128,512]{2,1,0:T(8,128)} %own_inverse.1, f32[2,256,512]{2,1,0:T(8,128)S(1)} %collective-permute-done.other_rows, ...), custom_call_target="tpu_custom_call" | custom-call | bytes 1000 | tf_op jit(solution)/shard_map/pallas_call | solution.py:261
  6.0 0.8 collective-permute-start.2
  6.8 4.8 %collective-permute-start.6 = (f32[384,768]{1,0:T(8,128)}, f32[384,768]{1,0:T(8,128)S(1)}, u32[]{:S(2)}, u32[]{:S(2)}) collective-permute-start(f32[384,768]{1,0:T(8,128)} %bitcast.6), channel_id=1, source_target_pairs={{0,2},{2,0},{5,7},{7,5},{8,10},{10,8},{13,15},{15,13},{16,18},{18,... | collective-permute-start | bytes 3538952 | tf_op jit(solution)/shard_map/ppermute | solution.py:26
  11.6 0.0 collective-permute-done.2.refs_0_
  11.6 0.1 collective-permute-start.4
  11.7 14.3 %collective-permute-done.6.refs_2_ = f32[384,768]{1,0:T(8,128)S(1)} collective-permute-done((f32[384,768]{1,0:T(8,128)}, f32[384,768]{1,0:T(8,128)S(1)}, u32[]{:S(2)}, u32[]{:S(2)}) %collective-permute-start.6) | collective-permute-done | bytes 1179680 | tf_op jit(solution)/shard_map/ppermute | solution.py:26
  25.9 0.0 copy-done.1
  25.9 0.7 collective-permute-start.8
  26.6 1.9 %collective-permute-start.3 = (f32[384,768]{1,0:T(8,128)}, f32[384,768]{1,0:T(8,128)S(1)}, u32[]{:S(2)}, u32[]{:S(2)}) collective-permute-start(f32[384,768]{1,0:T(8,128)} %bitcast.7), channel_id=1, source_target_pairs={{0,0},{1,4},{2,2},{3,6},{4,1},{5,5},{6,3},{7,7},{8,8},{9,12},{10,1... | collective-permute-start | bytes 3538952 | tf_op jit(solution)/shard_map/ppermute | solution.py:36
  28.6 0.0 copy-done
  28.6 0.1 slice_bitcast_fusion.1
  28.6 0.7 collective-permute-start.11
  29.4 0.0 collective-permute-done.8.refs_0_
  29.4 3.9 %collective-permute-start.10 = (f32[192,768]{1,0:T(8,128)S(1)}, f32[192,768]{1,0:T(8,128)S(1)}, u32[]{:S(2)}, u32[]{:S(2)}) collective-permute-start(f32[192,768]{1,0:T(8,128)S(1)} %collective-permute-done.8.refs_0_), channel_id=1, source_target_pairs={{0,2},{2,0},{5,7},{7,5},{8,10},{10,8},{13,15},{15,13},{16,18},{18,... | collective-permute-start | bytes 1769480 | tf_op jit(solution)/shard_map/ppermute | solution.py:26
  33.3 9.7 %collective-permute-start.9 = (f32[2,384,512]{2,1,0:T(8,128)S(1)}, f32[2,384,512]{2,1,0:T(8,128)S(1)}, u32[]{:S(2)}, u32[]{:S(2)}) collective-permute-start(f32[2,384,512]{2,1,0:T(8,128)S(1)} %collective-permute-done.2.refs_0_), channel_id=1, source_target_pairs={{0,4},{1,5},{2,6},{3,7},{4,0},{5,1},{6,2},{7,3},{8,12},{9,13},{10,... | collective-permute-start | bytes 4718600 | tf_op jit(solution)/shard_map/ppermute | solution.py:26
  43.0 0.0 collective-permute-done.11.top
  43.0 22.9 %collective-permute-done.10.refs_2_ = f32[192,768]{1,0:T(8,128)S(1)} collective-permute-done((f32[192,768]{1,0:T(8,128)S(1)}, f32[192,768]{1,0:T(8,128)S(1)}, u32[]{:S(2)}, u32[]{:S(2)}) %collective-permute-start.10) | collective-permute-done | bytes 589856 | tf_op jit(solution)/shard_map/ppermute | solution.py:26
  66.0 0.0 collective-permute-done.3.factor.refs_0_
  66.0 0.0 collective-permute-done.4.refs_2_
  66.0 0.0 collective-permute-start.12
  66.0 0.1 slice_bitcast_fusion
  66.1 0.8 collective-permute-start.17
  66.9 0.7 collective-permute-start.14
  67.6 0.7 collective-permute-start.7
  68.3 0.0 collective-permute-done.9.refs_1_
  68.3 1.1 collective-permute-done.12.refs_3_
  69.4 10.9 %shard_map.87 = (bf16[2,768,512]{2,1,0:T(8,128)(2,1)S(1)}, bf16[2,1536,512]{2,1,0:T(8,128)(2,1)S(1)}, f32[2,384,512]{2,1,0:T(8,128)S(1)}, f32[2,512]{1,0:T(2,128)S(1)}) custom-call(s32[2,4,256]{2,1,0:T(4,128)S(1)} %get-tuple-element.32.index, f32[2,384,512]{2,1,0:T(8,128)S(1)} %collective-permute-done.2.refs_0_, ...), custom_call_target="tpu_custom_call" | custom-call | bytes 1000 | tf_op jit(solution)/shard_map/pallas_call | solution.py:261
  80.3 7.1 %collective-permute-start.16 = (f32[192,768]{1,0:T(8,128)S(1)}, f32[192,768]{1,0:T(8,128)S(1)}, u32[]{:S(2)}, u32[]{:S(2)}) collective-permute-start(f32[192,768]{1,0:T(8,128)S(1)} %collective-permute-done.10.refs_2_), channel_id=1, source_target_pairs={{0,4},{2,6},{5,1},{7,3},{8,12},{10,14},{13,9},{15,11},{16,20},{18,... | collective-permute-start | bytes 1769480 | tf_op jit(solution)/shard_map/ppermute | solution.py:26
  87.4 0.0 collective-permute-done.14.refs_3_
  87.4 1.5 %collective-permute-start.15 = (f32[192,768]{1,0:T(8,128)S(1)}, f32[192,768]{1,0:T(8,128)S(1)}, u32[]{:S(2)}, u32[]{:S(2)}) collective-permute-start(f32[192,768]{1,0:T(8,128)S(1)} %collective-permute-done.14.refs_3_), channel_id=1, source_target_pairs={{1,5},{3,7},{4,0},{6,2},{9,13},{11,15},{12,8},{14,10},{17,21},{19,... | collective-permute-start | bytes 1769480 | tf_op jit(solution)/shard_map/ppermute | solution.py:26
  88.9 1.2 %collective-permute-start.13 = (f32[192,768]{1,0:T(8,128)S(1)}, f32[192,768]{1,0:T(8,128)S(1)}, u32[]{:S(2)}, u32[]{:S(2)}) collective-permute-start(f32[192,768]{1,0:T(8,128)S(1)} %collective-permute-done.8.refs_0_), channel_id=1, source_target_pairs={{0,4},{1,5},{2,6},{3,7},{4,0},{5,1},{6,2},{7,3},{8,12},{9,13},{10,... | collective-permute-start | bytes 1769480 | tf_op jit(solution)/shard_map/ppermute | solution.py:26
  90.1 0.0 collective-permute-done.16.refs_5_
  90.1 0.1 collective-permute-start.5
  90.2 1.1 collective-permute-done.15.refs_4_
  91.3 2.1 %collective-permute-start.19 = (f32[384,768]{1,0:T(8,128)S(1)}, f32[384,768]{1,0:T(8,128)S(1)}, u32[]{:S(2)}, u32[]{:S(2)}) collective-permute-start(f32[384,768]{1,0:T(8,128)S(1)} %collective-permute-done.6.refs_2_), channel_id=1, source_target_pairs={{0,4},{2,6},{5,1},{7,3},{8,12},{10,14},{13,9},{15,11},{16,20},{18,... | collective-permute-start | bytes 3538952 | tf_op jit(solution)/shard_map/ppermute | solution.py:26
  93.4 0.0 collective-permute-done.13.refs_1_
  93.4 5.2 %shard_map.88 = (f32[2,384,512]{2,1,0:T(8,128)S(1)}, bf16[2,768,512]{2,1,0:T(8,128)(2,1)S(1)}, bf16[768,768]{1,0:T(8,128)(2,1)S(1)}, bf16[768,768]{1,0:T(8,128)(...) custom-call(f32[384,768]{1,0:T(8,128)S(1)} %collective-permute-done.3.factor.refs_0_, ...), custom_call_target="tpu_custom_call" | custom-call | bytes 1000 | tf_op jit(solution)/shard_map/pallas_call | solution.py:261
  98.7 0.0 collective-permute-done.17.rest
  98.7 0.0 collective-permute-done.7.refs_3_
  98.7 1.3 %collective-permute-start.18 = (f32[384,768]{1,0:T(8,128)S(1)}, f32[384,768]{1,0:T(8,128)S(1)}, u32[]{:S(2)}, u32[]{:S(2)}) collective-permute-start(f32[384,768]{1,0:T(8,128)S(1)} %collective-permute-done.7.refs_3_), channel_id=1, source_target_pairs={{1,5},{3,7},{4,0},{6,2},{9,13},{11,15},{12,8},{14,10},{17,21},{19,... | collective-permute-start | bytes 3538952 | tf_op jit(solution)/shard_map/ppermute | solution.py:26
  100.0 1.4 %shard_map.89 = (bf16[384,1536]{1,0:T(8,128)(2,1)S(1)}, f32[2,384,512]{2,1,0:T(8,128)S(1)}) custom-call(f32[128,1536]{1,0:T(8,128)S(1)} %collective-permute-done.11.top, f32[256,1536]{1,0:T(8,128)S(1)} %collective-permute-done.17.rest, bf16[2,1536,512]{2,1,0:T(8,128)(2,1)S(1)} %get-tuple-element.47.lower_high), custom_call_target="tpu_custom_call" | custom-call | bytes 1000 | tf_op jit(solution)/shard_map/pallas_call | solution.py:261
  101.4 0.0 collective-permute-done.5.refs_1_
  101.4 0.0 collective-permute-done.19.refs_5_
  101.4 2.0 %collective-permute-done.18.refs_4_ = f32[384,768]{1,0:T(8,128)S(1)} collective-permute-done((f32[384,768]{1,0:T(8,128)S(1)}, f32[384,768]{1,0:T(8,128)S(1)}, u32[]{:S(2)}, u32[]{:S(2)}) %collective-permute-start.18) | collective-permute-done | bytes 1179680 | tf_op jit(solution)/shard_map/ppermute | solution.py:26
  103.4 3.6 %shard_map.90 = f32[1,1792]{1,0:T(1,128)S(1)} custom-call(f32[384,768]{1,0:T(8,128)S(1)} %collective-permute-done.3.factor.refs_0_, f32[384,768]{1,0:T(8,128)S(1)} %collective-permute-done.5.refs_1_, f32[384,768]{1,0:T(8,128)S(1)} %collective-permute-done.6.refs_2_, f32[384,768]{1,0:T(8,128)S(1)} %collective-permute-done.7.refs_3_, ...), custom_call_target="tpu_custom_call" | custom-call | bytes 1000 | tf_op jit(solution)/shard_map/pallas_call | solution.py:261
  107.0 0.2 collective-permute-start.20
  107.2 1.0 collective-permute-done.20
  108.3 1.6 %collective-permute-start.21 = (f32[1,1792]{1,0:T(1,128)S(1)}, f32[1,1792]{1,0:T(1,128)S(1)}, u32[]{:S(2)}, u32[]{:S(2)}) collective-permute-start(f32[1,1792]{1,0:T(1,128)S(1)} %add.3.refs_0_), channel_id=1, source_target_pairs={{0,2},{1,3},{2,0},{3,1},{4,6},{5,7},{6,4},{7,5},{8,10},{9,11},{10,... | collective-permute-start | bytes 21512 | tf_op jit(solution)/shard_map/ppermute | solution.py:26
  109.8 2.1 %collective-permute-start.22 = (f32[1,1792]{1,0:T(1,128)S(1)}, f32[1,1792]{1,0:T(1,128)S(1)}, u32[]{:S(2)}, u32[]{:S(2)}) collective-permute-start(f32[1,1792]{1,0:T(1,128)S(1)} %add.3.refs_0_), channel_id=1, source_target_pairs={{0,1},{1,0},{2,3},{3,2},{4,5},{5,4},{6,7},{7,6},{8,9},{9,8},{10,11... | collective-permute-start | bytes 21512 | tf_op jit(solution)/shard_map/ppermute | solution.py:26
  111.9 0.0 collective-permute-start.23
  111.9 0.0 collective-permute-done.21.refs_1_
  112.0 1.6 %collective-permute-done.22.refs_2_ = f32[1,1792]{1,0:T(1,128)S(1)} collective-permute-done((f32[1,1792]{1,0:T(1,128)S(1)}, f32[1,1792]{1,0:T(1,128)S(1)}, u32[]{:S(2)}, u32[]{:S(2)}) %collective-permute-start.22) | collective-permute-done | bytes 7200 | tf_op jit(solution)/shard_map/ppermute | solution.py:26
  113.6 2.9 %collective-permute-done.23.refs_3_ = f32[1,1792]{1,0:T(1,128)S(1)} collective-permute-done((f32[1,1792]{1,0:T(1,128)S(1)}, f32[1,1792]{1,0:T(1,128)S(1)}, u32[]{:S(2)}, u32[]{:S(2)}) %collective-permute-start.23) | collective-permute-done | bytes 7200 | tf_op jit(solution)/shard_map/ppermute | solution.py:26
  116.5 1.3 %shard_map.91 = (f32[1,768]{1,0:T(1,128)}, f32[2,512]{1,0:T(2,128)}) custom-call(s32[16]{0:T(128)} %parent_ref.3, f32[1,1792]{1,0:T(1,128)S(1)} %add.3.refs_0_, f32[1,1792]{1,0:T(1,128)S(1)} %collective-permute-done.21.refs_1_, f32[1,1792]{1,0:T(1,128)S(1)} %collective-permute-done.22.refs_2_, f32[1,1792]{1,0:T(1,128)S(1)} %collective-permute-done.23.refs_3_), custom_call_target="tpu_custom_call" | custom-call | bytes 1000 | tf_op jit(solution)/shard_map/pallas_call | solution.py:261
  (1 shorter events, 0.0 us)
Async XLA Ops:
  0.6 25.3 %copy-start.1 = (f32[1,192,768]{2,1,0:T(8,128)S(1)}, f32[1,192,768]{2,1,0:T(8,128)}, u32[]{:S(2)}) copy-start(f32[1,192,768]{2,1,0:T(8,128)} %param.9) | copy-start | bytes 1769476
  0.6 27.9 %copy-start = (f32[1,384,1536]{2,1,0:T(8,128)S(1)}, f32[1,384,1536]{2,1,0:T(8,128)}, u32[]{:S(2)}) copy-start(f32[1,384,1536]{2,1,0:T(8,128)} %param.7) | copy-start | bytes 7077892
  0.7 3.8 %collective-permute-start = (f32[2,256,512]{2,1,0:T(8,128)}, f32[2,256,512]{2,1,0:T(8,128)S(1)}, u32[]{:S(2)}, u32[]{:S(2)}) collective-permute-start(f32[2,256,512]{2,1,0:T(8,128)} %own_rows.1), channel_id=1, source_target_pairs={{0,4},{1,5},{2,6},{3,7},{4,0},{5,1},{6,2},{7,3},{8,12},{9,13},{10,... | collective-permute-start | bytes 3145736 | tf_op jit(solution)/shard_map/ppermute | solution.py:26
  1.2 3.2 %collective-permute-start.1 = (f32[2,128,512]{2,1,0:T(8,128)}, f32[2,128,512]{2,1,0:T(8,128)S(1)}, u32[]{:S(2)}, u32[]{:S(2)}) collective-permute-start(f32[2,128,512]{2,1,0:T(8,128)} %own_inverse.1), channel_id=1, source_target_pairs={{0,4},{1,5},{2,6},{3,7},{4,0},{5,1},{6,2},{7,3},{8,12},{9,13},{10,... | collective-permute-start | bytes 1572872 | tf_op jit(solution)/shard_map/ppermute | solution.py:26
  6.0 5.6 %collective-permute-start.2 = (f32[2,384,512]{2,1,0:T(8,128)S(1)}, f32[2,384,512]{2,1,0:T(8,128)S(1)}, u32[]{:S(2)}, u32[]{:S(2)}) collective-permute-start(f32[2,384,512]{2,1,0:T(8,128)S(1)} %get-tuple-element.29), channel_id=1, source_target_pairs={{0,0},{1,4},{2,2},{3,6},{4,1},{5,5},{6,3},{7,7},{8,8},{9,12},{10,1... | collective-permute-start | bytes 4718600 | tf_op jit(solution)/shard_map/ppermute | solution.py:36
  6.8 19.2 %collective-permute-start.6 = (f32[384,768]{1,0:T(8,128)}, f32[384,768]{1,0:T(8,128)S(1)}, u32[]{:S(2)}, u32[]{:S(2)}) collective-permute-start(f32[384,768]{1,0:T(8,128)} %bitcast.6), channel_id=1, source_target_pairs={{0,2},{2,0},{5,7},{7,5},{8,10},{10,8},{13,15},{15,13},{16,18},{18,... | collective-permute-start | bytes 3538952 | tf_op jit(solution)/shard_map/ppermute | solution.py:26
  11.6 54.4 %collective-permute-start.4 = (f32[2,384,512]{2,1,0:T(8,128)S(1)}, f32[2,384,512]{2,1,0:T(8,128)S(1)}, u32[]{:S(2)}, u32[]{:S(2)}) collective-permute-start(f32[2,384,512]{2,1,0:T(8,128)S(1)} %collective-permute-done.2.refs_0_), channel_id=1, source_target_pairs={{0,2},{1,3},{2,0},{3,1},{4,6},{5,7},{6,4},{7,5},{8,10},{9,11},{10,... | collective-permute-start | bytes 4718600 | tf_op jit(solution)/shard_map/ppermute | solution.py:26
  25.9 3.4 %collective-permute-start.8 = (f32[192,768]{1,0:T(8,128)S(1)}, f32[192,768]{1,0:T(8,128)S(1)}, u32[]{:S(2)}, u32[]{:S(2)}) collective-permute-start(f32[192,768]{1,0:T(8,128)S(1)} %bitcast.8), channel_id=1, source_target_pairs={{0,0},{1,4},{2,2},{3,6},{4,1},{5,5},{6,3},{7,7},{8,8},{9,12},{10,1... | collective-permute-start | bytes 1769480 | tf_op jit(solution)/shard_map/ppermute | solution.py:36
  26.6 39.3 %collective-permute-start.3 = (f32[384,768]{1,0:T(8,128)}, f32[384,768]{1,0:T(8,128)S(1)}, u32[]{:S(2)}, u32[]{:S(2)}) collective-permute-start(f32[384,768]{1,0:T(8,128)} %bitcast.7), channel_id=1, source_target_pairs={{0,0},{1,4},{2,2},{3,6},{4,1},{5,5},{6,3},{7,7},{8,8},{9,12},{10,1... | collective-permute-start | bytes 3538952 | tf_op jit(solution)/shard_map/ppermute | solution.py:36
  28.6 14.4 %collective-permute-start.11 = (f32[128,1536]{1,0:T(8,128)S(1)}, f32[128,1536]{1,0:T(8,128)S(1)}, u32[]{:S(2)}, u32[]{:S(2)}) collective-permute-start(f32[128,1536]{1,0:T(8,128)S(1)} %slice_bitcast_fusion.1), channel_id=1, source_target_pairs={{0,0},{1,4},{2,2},{3,6},{4,1},{5,5},{6,3},{7,7},{8,8},{9,12},{10,1... | collective-permute-start | bytes 2359304 | tf_op jit(solution)/shard_map/ppermute | solution.py:36
  29.4 36.6 %collective-permute-start.10 = (f32[192,768]{1,0:T(8,128)S(1)}, f32[192,768]{1,0:T(8,128)S(1)}, u32[]{:S(2)}, u32[]{:S(2)}) collective-permute-start(f32[192,768]{1,0:T(8,128)S(1)} %collective-permute-done.8.refs_0_), channel_id=1, source_target_pairs={{0,2},{2,0},{5,7},{7,5},{8,10},{10,8},{13,15},{15,13},{16,18},{18,... | collective-permute-start | bytes 1769480 | tf_op jit(solution)/shard_map/ppermute | solution.py:26
  33.3 35.0 %collective-permute-start.9 = (f32[2,384,512]{2,1,0:T(8,128)S(1)}, f32[2,384,512]{2,1,0:T(8,128)S(1)}, u32[]{:S(2)}, u32[]{:S(2)}) collective-permute-start(f32[2,384,512]{2,1,0:T(8,128)S(1)} %collective-permute-done.2.refs_0_), channel_id=1, source_target_pairs={{0,4},{1,5},{2,6},{3,7},{4,0},{5,1},{6,2},{7,3},{8,12},{9,13},{10,... | collective-permute-start | bytes 4718600 | tf_op jit(solution)/shard_map/ppermute | solution.py:26
  66.0 3.4 %collective-permute-start.12 = (f32[2,384,512]{2,1,0:T(8,128)S(1)}, f32[2,384,512]{2,1,0:T(8,128)S(1)}, u32[]{:S(2)}, u32[]{:S(2)}) collective-permute-start(f32[2,384,512]{2,1,0:T(8,128)S(1)} %collective-permute-done.4.refs_2_), channel_id=1, source_target_pairs={{0,4},{1,5},{2,6},{3,7},{4,0},{5,1},{6,2},{7,3},{8,12},{9,13},{10,... | collective-permute-start | bytes 4718600 | tf_op jit(solution)/shard_map/ppermute | solution.py:26
  66.1 32.6 %collective-permute-start.17 = (f32[256,1536]{1,0:T(8,128)S(1)}, f32[256,1536]{1,0:T(8,128)S(1)}, u32[]{:S(2)}, u32[]{:S(2)}) collective-permute-start(f32[256,1536]{1,0:T(8,128)S(1)} %slice_bitcast_fusion), channel_id=1, source_target_pairs={{0,0},{1,4},{2,2},{3,6},{4,1},{5,5},{6,3},{7,7},{8,8},{9,12},{10,1... | collective-permute-start | bytes 4718600 | tf_op jit(solution)/shard_map/ppermute | solution.py:36
  66.9 20.5 %collective-permute-start.14 = (f32[192,768]{1,0:T(8,128)S(1)}, f32[192,768]{1,0:T(8,128)S(1)}, u32[]{:S(2)}, u32[]{:S(2)}) collective-permute-start(f32[192,768]{1,0:T(8,128)S(1)} %collective-permute-done.8.refs_0_), channel_id=1, source_target_pairs={{1,3},{3,1},{4,6},{6,4},{9,11},{11,9},{12,14},{14,12},{17,19},{19,... | collective-permute-start | bytes 1769480 | tf_op jit(solution)/shard_map/ppermute | solution.py:26
  67.6 31.1 %collective-permute-start.7 = (f32[384,768]{1,0:T(8,128)S(1)}, f32[384,768]{1,0:T(8,128)S(1)}, u32[]{:S(2)}, u32[]{:S(2)}) collective-permute-start(f32[384,768]{1,0:T(8,128)S(1)} %collective-permute-done.3.factor.refs_0_), channel_id=1, source_target_pairs={{1,3},{3,1},{4,6},{6,4},{9,11},{11,9},{12,14},{14,12},{17,19},{19,... | collective-permute-start | bytes 3538952 | tf_op jit(solution)/shard_map/ppermute | solution.py:26
  80.3 9.9 %collective-permute-start.16 = (f32[192,768]{1,0:T(8,128)S(1)}, f32[192,768]{1,0:T(8,128)S(1)}, u32[]{:S(2)}, u32[]{:S(2)}) collective-permute-start(f32[192,768]{1,0:T(8,128)S(1)} %collective-permute-done.10.refs_2_), channel_id=1, source_target_pairs={{0,4},{2,6},{5,1},{7,3},{8,12},{10,14},{13,9},{15,11},{16,20},{18,... | collective-permute-start | bytes 1769480 | tf_op jit(solution)/shard_map/ppermute | solution.py:26
  87.4 3.9 %collective-permute-start.15 = (f32[192,768]{1,0:T(8,128)S(1)}, f32[192,768]{1,0:T(8,128)S(1)}, u32[]{:S(2)}, u32[]{:S(2)}) collective-permute-start(f32[192,768]{1,0:T(8,128)S(1)} %collective-permute-done.14.refs_3_), channel_id=1, source_target_pairs={{1,5},{3,7},{4,0},{6,2},{9,13},{11,15},{12,8},{14,10},{17,21},{19,... | collective-permute-start | bytes 1769480 | tf_op jit(solution)/shard_map/ppermute | solution.py:26
  88.9 4.5 %collective-permute-start.13 = (f32[192,768]{1,0:T(8,128)S(1)}, f32[192,768]{1,0:T(8,128)S(1)}, u32[]{:S(2)}, u32[]{:S(2)}) collective-permute-start(f32[192,768]{1,0:T(8,128)S(1)} %collective-permute-done.8.refs_0_), channel_id=1, source_target_pairs={{0,4},{1,5},{2,6},{3,7},{4,0},{5,1},{6,2},{7,3},{8,12},{9,13},{10,... | collective-permute-start | bytes 1769480 | tf_op jit(solution)/shard_map/ppermute | solution.py:26
  90.1 11.3 %collective-permute-start.5 = (f32[384,768]{1,0:T(8,128)S(1)}, f32[384,768]{1,0:T(8,128)S(1)}, u32[]{:S(2)}, u32[]{:S(2)}) collective-permute-start(f32[384,768]{1,0:T(8,128)S(1)} %collective-permute-done.3.factor.refs_0_), channel_id=1, source_target_pairs={{0,4},{1,5},{2,6},{3,7},{4,0},{5,1},{6,2},{7,3},{8,12},{9,13},{10,... | collective-permute-start | bytes 3538952 | tf_op jit(solution)/shard_map/ppermute | solution.py:26
  91.3 10.1 %collective-permute-start.19 = (f32[384,768]{1,0:T(8,128)S(1)}, f32[384,768]{1,0:T(8,128)S(1)}, u32[]{:S(2)}, u32[]{:S(2)}) collective-permute-start(f32[384,768]{1,0:T(8,128)S(1)} %collective-permute-done.6.refs_2_), channel_id=1, source_target_pairs={{0,4},{2,6},{5,1},{7,3},{8,12},{10,14},{13,9},{15,11},{16,20},{18,... | collective-permute-start | bytes 3538952 | tf_op jit(solution)/shard_map/ppermute | solution.py:26
  98.7 4.7 %collective-permute-start.18 = (f32[384,768]{1,0:T(8,128)S(1)}, f32[384,768]{1,0:T(8,128)S(1)}, u32[]{:S(2)}, u32[]{:S(2)}) collective-permute-start(f32[384,768]{1,0:T(8,128)S(1)} %collective-permute-done.7.refs_3_), channel_id=1, source_target_pairs={{1,5},{3,7},{4,0},{6,2},{9,13},{11,15},{12,8},{14,10},{17,21},{19,... | collective-permute-start | bytes 3538952 | tf_op jit(solution)/shard_map/ppermute | solution.py:26
  107.0 1.2 %collective-permute-start.20 = (f32[1,1792]{1,0:T(1,128)S(1)}, f32[1,1792]{1,0:T(1,128)S(1)}, u32[]{:S(2)}, u32[]{:S(2)}) collective-permute-start(f32[1,1792]{1,0:T(1,128)S(1)} %shard_map.90), channel_id=1, source_target_pairs={{0,4},{1,5},{2,6},{3,7},{4,0},{5,1},{6,2},{7,3},{8,12},{9,13},{10,... | collective-permute-start | bytes 21512 | tf_op jit(solution)/shard_map/ppermute | solution.py:26
  108.3 3.7 %collective-permute-start.21 = (f32[1,1792]{1,0:T(1,128)S(1)}, f32[1,1792]{1,0:T(1,128)S(1)}, u32[]{:S(2)}, u32[]{:S(2)}) collective-permute-start(f32[1,1792]{1,0:T(1,128)S(1)} %add.3.refs_0_), channel_id=1, source_target_pairs={{0,2},{1,3},{2,0},{3,1},{4,6},{5,7},{6,4},{7,5},{8,10},{9,11},{10,... | collective-permute-start | bytes 21512 | tf_op jit(solution)/shard_map/ppermute | solution.py:26
  109.8 3.7 %collective-permute-start.22 = (f32[1,1792]{1,0:T(1,128)S(1)}, f32[1,1792]{1,0:T(1,128)S(1)}, u32[]{:S(2)}, u32[]{:S(2)}) collective-permute-start(f32[1,1792]{1,0:T(1,128)S(1)} %add.3.refs_0_), channel_id=1, source_target_pairs={{0,1},{1,0},{2,3},{3,2},{4,5},{5,4},{6,7},{7,6},{8,9},{9,8},{10,11... | collective-permute-start | bytes 21512 | tf_op jit(solution)/shard_map/ppermute | solution.py:26
  111.9 4.5 %collective-permute-start.23 = (f32[1,1792]{1,0:T(1,128)S(1)}, f32[1,1792]{1,0:T(1,128)S(1)}, u32[]{:S(2)}, u32[]{:S(2)}) collective-permute-start(f32[1,1792]{1,0:T(1,128)S(1)} %add.3.refs_0_), channel_id=1, source_target_pairs={{0,3},{1,2},{2,1},{3,0},{4,7},{5,6},{6,5},{7,4},{8,11},{9,10},{10,... | collective-permute-start | bytes 21512 | tf_op jit(solution)/shard_map/ppermute | solution.py:26

commit v2 on v0

--- a/solution.py
+++ b/solution.py
@@ -132,16 +132,20 @@
 
 
 def diagonal_kernel(pieces, index, factor, *refs):
-    diagonal = refs[:pieces]
-    diag_high, diag_low, pick_high, pick_low, weights, parent_sum = refs[pieces:]
+    diag_high, diag_low, pick_high, pick_low, weights, parent_sum = refs[2 * pieces - 2 :]
     _, block = place_of()
-    own_rows, size = diagonal[0].shape
-    parent_sum[...] = column_sum(diagonal[0][...] * diagonal[0][...])
-    for mask in range(pieces):
+    own_rows, size = refs[0].shape
+    parent_sum[...] = column_sum(refs[0][...] * refs[0][...])
+    for mask, pair in enumerate(unpacked(pieces, refs)):
         start = pl.multiple_of((block ^ mask) * own_rows, 16)
-        high, low = halves(diagonal[mask][...])
-        diag_high[pl.ds(start, own_rows), :] = high
-        diag_low[pl.ds(start, own_rows), :] = low
+
+        def put(ref, start=start):
+            diag_high[pl.ds(start, own_rows), :], diag_low[pl.ds(start, own_rows), :] = halves(ref[...])
+
+        if mask < 2:
+            put(pair[0])
+        else:
+            store(pair, put)
     for kid in range(2):
         for mask in range(pieces):
             pick = picks(index[kid, mask : mask + 1, :], 0, size)
@@ -288,18 +292,27 @@
         parts = parts | others
         return [parts[mask] for mask in range(pieces)]
 
+    def gathered(own, keep, swap, gate_own, gate_keep, gate_swap):
+        result = [own, exchange(after(own, *gate_own), 1, 0)]
+        for mask in list(keep)[1:]:
+            far_swap = exchange(after(keep[mask], *gate_keep), 1, 0, 0)
+            far_keep = exchange(after(swap[mask], *gate_swap), 1, 0, 1)
+            result += [keep[mask], swap[mask], far_keep, far_swap]
+        return result
+
     last = pieces - 2
+    keep_diagonal = over_fronts(diagonal, 0)
     keep_factor = over_fronts(factor, 0)
     own_diagonal = cross(diagonal)
     kid_shape = (2, kid_block + kid_inverse.shape[1], kid_size)
     own_kids, index = call(
         select_kernel, (shape_of(kid_shape), shape_of((2, pieces, kid_block), jnp.int32)), 6, scalars=1, loose=4
     )(child_parent, child_index, kid_rows, kid_inverse, exchange(kid_rows, 1, 0), exchange(kid_inverse, 1, 0))
-    own_kids = cross(after(own_kids, own_diagonal, keep_factor[last]))
-    diagonal_parts = over_fronts(own_diagonal)
-    kid_parts = over_fronts(after(own_kids, diagonal_parts[last]))
-    own_factor = cross(after(factor, own_diagonal))
-    diagonal_parts = spread(diagonal_parts, [own_kids], [own_kids])
+    own_kids = cross(after(own_kids, own_diagonal, keep_diagonal[last], keep_factor[last]))
+    swap_diagonal = over_fronts(own_diagonal, 1)
+    kid_parts = over_fronts(after(own_kids, swap_diagonal[last]))
+    own_factor = cross(after(factor, own_kids))
+    diagonal_parts = gathered(own_diagonal, keep_diagonal, swap_diagonal, [own_kids], [own_kids], [own_kids])
 
     diag_high, diag_low, pick_high, pick_low, weights, parent_sum = call(
         functools.partial(diagonal_kernel, pieces),
@@ -339,11 +352,7 @@
         border_kernel, (shape_of(border.shape, half), shape_of((2, own_border, kid_size))), 8
     )(own_border_rows, lower_high)
 
-    factor_parts = [own_factor, exchange(after(own_factor, kids_here), 1, 0)]
-    for mask in list(keep_factor)[1:]:
-        far_swap = exchange(after(keep_factor[mask], kids_here), 1, 0, 0)
-        far_keep = exchange(after(swap_factor[mask], border_lower), 1, 0, 1)
-        factor_parts += [keep_factor[mask], swap_factor[mask], far_keep, far_swap]
+    factor_parts = gathered(own_factor, keep_factor, swap_factor, [kids_here], [kids_here], [lift_high, own_border_rows])
     total = call(
         functools.partial(image_kernel, pieces),
         shape_of((1, size + 2 * kid_size)),

time: 110 us -> 104 us (0.945)
  waiting for transfers between devices: 33.6 us -> 27.4 us
    ppermute x17 -> x19, waiting for transfers between devices: 33.6 us -> 27.4 us  [exchange(): return lax.ppermute(value, ('leaf', 'front'), pairs)]
    ppermute x17 -> x19, starting transfers between devices: 40.9 us -> 41.4 us  [exchange(): return lax.ppermute(value, ('leaf', 'front'), pairs)]
  transfers between devices with their start and end apart: 21 -> 23, of which waited for: 9 -> 9; matrix products, arithmetic and copies ran while one was open for 0% -> 0% of each run, Pallas kernels for 22% -> 23%
where the time goes in v2:
time: 104 us
  starting transfers between devices  46.7 us (45%)
  Pallas kernels  28.7 us (28%)
  waiting for transfers between devices  27.4 us (26%)
    ppermute x19, starting transfers between devices, exchange(): return lax.ppermute(value, ('leaf', 'front'), pairs)  41.4 us
    pallas_call x6, Pallas kernels, run(): pl.pallas_call(kernel, out_shape=results, in_specs=specs, out_specs=jax.t...  28.7 us
    ppermute x19, waiting for transfers between devices, exchange(): return lax.ppermute(value, ('leaf', 'front'), pairs)  27.4 us
    ppermute x4, starting transfers between devices, cross(): return lax.ppermute(value, ('leaf', 'front'), pairs)  5.34 us
  transfers between devices with their start and end apart: 23, of which 9 were waited for; matrix products, arithmetic and copies ran while one was open for 0% of the time, Pallas kernels for 23%

profile of v2, /device:TPU:0, one launch (start us, length us, event | category | flops | bytes accessed | tf_op | source)
XLA Modules:
  0.0 103.7 jit_solution(9165915547897615284)
XLA Ops:
  0.6 4.9 %collective-permute-start.4 = (f32[384,768]{1,0:T(8,128)}, f32[384,768]{1,0:T(8,128)S(1)}, u32[]{:S(2)}, u32[]{:S(2)}) collective-permute-start(f32[384,768]{1,0:T(8,128)} %bitcast.4), channel_id=1, source_target_pairs={{0,2},{2,0},{5,7},{7,5},{8,10},{10,8},{13,15},{15,13},{16,18},{18,... | collective-permute-start | bytes 3538952 | tf_op jit(solution)/shard_map/ppermute | solution.py:26
  5.5 0.1 collective-permute-start
  5.6 0.0 copy-start
  5.6 1.9 %collective-permute-start.2 = (f32[192,768]{1,0:T(8,128)}, f32[192,768]{1,0:T(8,128)S(1)}, u32[]{:S(2)}, u32[]{:S(2)}) collective-permute-start(f32[192,768]{1,0:T(8,128)} %bitcast.6), channel_id=1, source_target_pairs={{0,0},{1,4},{2,2},{3,6},{4,1},{5,5},{6,3},{7,7},{8,8},{9,12},{10,1... | collective-permute-start | bytes 1769480 | tf_op jit(solution)/shard_map/ppermute | solution.py:36
  7.5 1.9 %collective-permute-start.3 = (f32[192,768]{1,0:T(8,128)}, f32[192,768]{1,0:T(8,128)S(1)}, u32[]{:S(2)}, u32[]{:S(2)}) collective-permute-start(f32[192,768]{1,0:T(8,128)} %bitcast.7), channel_id=1, source_target_pairs={{0,2},{2,0},{5,7},{7,5},{8,10},{10,8},{13,15},{15,13},{16,18},{18,... | collective-permute-start | bytes 1769480 | tf_op jit(solution)/shard_map/ppermute | solution.py:26
  9.4 0.2 collective-permute-start.1
  9.6 2.0 %collective-permute-done.1.other_inverse = f32[2,128,512]{2,1,0:T(8,128)S(1)} collective-permute-done((f32[2,128,512]{2,1,0:T(8,128)}, f32[2,128,512]{2,1,0:T(8,128)S(1)}, u32[]{:S(2)}, u32[]{:S(2)}) %collective-permute-start.1) | collective-permute-done | bytes 524320 | tf_op jit(solution)/shard_map/ppermute | solution.py:26
  11.6 0.0 collective-permute-done.other_rows
  11.6 1.6 %shard_map.86 = (f32[2,384,512]{2,1,0:T(8,128)S(1)}, s32[2,4,256]{2,1,0:T(4,128)S(1)}) custom-call(s32[16]{0:T(128)} %parent_ref.3, s32[16,1024]{1,0:T(8,128)} %index_ref.1, f32[2,256,512]{2,1,0:T(8,128)} %own_rows.1, f32[2,128,512]{2,1,0:T(8,128)} %own_inverse.1, f32[2,256,512]{2,1,0:T(8,128)S(1)} %collective-permute-done.other_rows, ...), custom_call_target="tpu_custom_call" | custom-call | bytes 1000 | tf_op jit(solution)/shard_map/pallas_call | solution.py:260
  13.1 0.0 collective-permute-done.2.refs_0_
  13.1 15.7 %collective-permute-done.3.refs_2_ = f32[192,768]{1,0:T(8,128)S(1)} collective-permute-done((f32[192,768]{1,0:T(8,128)}, f32[192,768]{1,0:T(8,128)S(1)}, u32[]{:S(2)}, u32[]{:S(2)}) %collective-permute-start.3) | collective-permute-done | bytes 589856 | tf_op jit(solution)/shard_map/ppermute | solution.py:26
  28.8 0.0 collective-permute-done.4.refs_2_
  28.8 0.8 collective-permute-start.5
  29.6 0.7 collective-permute-start.7
  30.3 0.0 collective-permute-done.7.refs_3_
  30.3 0.0 collective-permute-done.5.refs_0_
  30.3 2.4 %collective-permute-start.8 = (f32[2,384,512]{2,1,0:T(8,128)S(1)}, f32[2,384,512]{2,1,0:T(8,128)S(1)}, u32[]{:S(2)}, u32[]{:S(2)}) collective-permute-start(f32[2,384,512]{2,1,0:T(8,128)S(1)} %collective-permute-done.5.refs_0_), channel_id=1, source_target_pairs={{0,2},{1,3},{2,0},{3,1},{4,6},{5,7},{6,4},{7,5},{8,10},{9,11},{10,... | collective-permute-start | bytes 4718600 | tf_op jit(solution)/shard_map/ppermute | solution.py:26
  32.8 1.3 %collective-permute-start.12 = (f32[192,768]{1,0:T(8,128)S(1)}, f32[192,768]{1,0:T(8,128)S(1)}, u32[]{:S(2)}, u32[]{:S(2)}) collective-permute-start(f32[192,768]{1,0:T(8,128)S(1)} %collective-permute-done.7.refs_3_), channel_id=1, source_target_pairs={{1,5},{3,7},{4,0},{6,2},{9,13},{11,15},{12,8},{14,10},{17,21},{19,... | collective-permute-start | bytes 1769480 | tf_op jit(solution)/shard_map/ppermute | solution.py:26
  34.0 1.9 %collective-permute-start.6 = (f32[384,768]{1,0:T(8,128)}, f32[384,768]{1,0:T(8,128)S(1)}, u32[]{:S(2)}, u32[]{:S(2)}) collective-permute-start(f32[384,768]{1,0:T(8,128)} %bitcast.5), channel_id=1, source_target_pairs={{0,0},{1,4},{2,2},{3,6},{4,1},{5,5},{6,3},{7,7},{8,8},{9,12},{10,1... | collective-permute-start | bytes 3538952 | tf_op jit(solution)/shard_map/ppermute | solution.py:36
  36.0 0.0 copy-done
  36.0 0.8 collective-permute-start.16
  36.8 10.1 %collective-permute-start.11 = (f32[192,768]{1,0:T(8,128)S(1)}, f32[192,768]{1,0:T(8,128)S(1)}, u32[]{:S(2)}, u32[]{:S(2)}) collective-permute-start(f32[192,768]{1,0:T(8,128)S(1)} %collective-permute-done.2.refs_0_), channel_id=1, source_target_pairs={{0,4},{1,5},{2,6},{3,7},{4,0},{5,1},{6,2},{7,3},{8,12},{9,13},{10,... | collective-permute-start | bytes 1769480 | tf_op jit(solution)/shard_map/ppermute | solution.py:26
  46.9 0.0 collective-permute-done.12.refs_4_
  46.9 2.0 %collective-permute-start.13 = (f32[192,768]{1,0:T(8,128)S(1)}, f32[192,768]{1,0:T(8,128)S(1)}, u32[]{:S(2)}, u32[]{:S(2)}) collective-permute-start(f32[192,768]{1,0:T(8,128)S(1)} %collective-permute-done.3.refs_2_), channel_id=1, source_target_pairs={{0,4},{2,6},{5,1},{7,3},{8,12},{10,14},{13,9},{15,11},{16,20},{18,... | collective-permute-start | bytes 1769480 | tf_op jit(solution)/shard_map/ppermute | solution.py:26
  48.9 0.0 collective-permute-done.11.refs_1_
  48.9 0.1 collective-permute-start.14
  49.0 1.5 %collective-permute-done.13.refs_5_ = f32[192,768]{1,0:T(8,128)S(1)} collective-permute-done((f32[192,768]{1,0:T(8,128)S(1)}, f32[192,768]{1,0:T(8,128)S(1)}, u32[]{:S(2)}, u32[]{:S(2)}) %collective-permute-start.13) | collective-permute-done | bytes 589856 | tf_op jit(solution)/shard_map/ppermute | solution.py:26
  50.5 0.0 collective-permute-done.6.factor.refs_0_
  50.5 7.0 %shard_map.87 = (bf16[768,768]{1,0:T(8,128)(2,1)S(1)}, bf16[768,768]{1,0:T(8,128)(2,1)S(1)}, bf16[2,4,768,256]{3,2,1,0:T(8,128)(2,1)S(1)}, bf16[2,4,768,256]{3,2...) custom-call(s32[2,4,256]{2,1,0:T(4,128)S(1)} %get-tuple-element.33.index, ...), custom_call_target="tpu_custom_call" | custom-call | bytes 1000 | tf_op jit(solution)/shard_map/pallas_call | solution.py:260
  57.5 3.4 %collective-permute-done.8.refs_2_ = f32[2,384,512]{2,1,0:T(8,128)S(1)} collective-permute-done((f32[2,384,512]{2,1,0:T(8,128)S(1)}, f32[2,384,512]{2,1,0:T(8,128)S(1)}, u32[]{:S(2)}, u32[]{:S(2)}) %collective-permute-start.8) | collective-permute-done | bytes 1572896 | tf_op jit(solution)/shard_map/ppermute | solution.py:26
  61.0 6.9 %collective-permute-start.15 = (f32[2,384,512]{2,1,0:T(8,128)S(1)}, f32[2,384,512]{2,1,0:T(8,128)S(1)}, u32[]{:S(2)}, u32[]{:S(2)}) collective-permute-start(f32[2,384,512]{2,1,0:T(8,128)S(1)} %collective-permute-done.8.refs_2_), channel_id=1, source_target_pairs={{0,4},{1,5},{2,6},{3,7},{4,0},{5,1},{6,2},{7,3},{8,12},{9,13},{10,... | collective-permute-start | bytes 4718600 | tf_op jit(solution)/shard_map/ppermute | solution.py:26
  67.8 0.7 collective-permute-start.10
  68.6 3.0 %collective-permute-start.9 = (f32[384,768]{1,0:T(8,128)S(1)}, f32[384,768]{1,0:T(8,128)S(1)}, u32[]{:S(2)}, u32[]{:S(2)}) collective-permute-start(f32[384,768]{1,0:T(8,128)S(1)} %collective-permute-done.6.factor.refs_0_), channel_id=1, source_target_pairs={{0,4},{1,5},{2,6},{3,7},{4,0},{5,1},{6,2},{7,3},{8,12},{9,13},{10,... | collective-permute-start | bytes 3538952 | tf_op jit(solution)/shard_map/ppermute | solution.py:26
  71.5 0.0 collective-permute-done.14.refs_1_
  71.5 2.2 %collective-permute-start.18 = (f32[384,768]{1,0:T(8,128)S(1)}, f32[384,768]{1,0:T(8,128)S(1)}, u32[]{:S(2)}, u32[]{:S(2)}) collective-permute-start(f32[384,768]{1,0:T(8,128)S(1)} %collective-permute-done.4.refs_2_), channel_id=1, source_target_pairs={{0,4},{2,6},{5,1},{7,3},{8,12},{10,14},{13,9},{15,11},{16,20},{18,... | collective-permute-start | bytes 3538952 | tf_op jit(solution)/shard_map/ppermute | solution.py:26
  73.7 0.0 collective-permute-done.15.refs_3_
  73.7 13.6 %shard_map.88 = (f32[2,384,512]{2,1,0:T(8,128)S(1)}, bf16[2,768,512]{2,1,0:T(8,128)(2,1)S(1)}, bf16[2,1536,512]{2,1,0:T(8,128)(2,1)S(1)}, f32[2,512]{1,0:T(2,128)S(1)}) custom-call(s32[2,4,256]{2,1,0:T(4,128)S(1)} %get-tuple-element.33.index, bf16[2,4,768,256]{3,2,1,0:T(8,128)(2,1)S(1)} %get-tuple-element.37.pick_high, ...), custom_call_target="tpu_custom_call" | custom-call | bytes 1000 | tf_op jit(solution)/shard_map/pallas_call | solution.py:260
  87.3 0.0 collective-permute-done.16.border
  87.3 0.0 collective-permute-done.10.refs_3_
  87.4 1.3 %collective-permute-start.17 = (f32[384,768]{1,0:T(8,128)S(1)}, f32[384,768]{1,0:T(8,128)S(1)}, u32[]{:S(2)}, u32[]{:S(2)}) collective-permute-start(f32[384,768]{1,0:T(8,128)S(1)} %collective-permute-done.10.refs_3_), channel_id=1, source_target_pairs={{1,5},{3,7},{4,0},{6,2},{9,13},{11,15},{12,8},{14,10},{17,21},{19,... | collective-permute-start | bytes 3538952 | tf_op jit(solution)/shard_map/ppermute | solution.py:26
  88.7 1.4 %shard_map.89 = (bf16[384,1536]{1,0:T(8,128)(2,1)S(1)}, f32[2,384,512]{2,1,0:T(8,128)S(1)}) custom-call(f32[384,1536]{1,0:T(8,128)S(1)} %collective-permute-done.16.border, bf16[2,1536,512]{2,1,0:T(8,128)(2,1)S(1)} %get-tuple-element.45.lower_high), custom_call_target="tpu_custom_call" | custom-call | bytes 1000 | tf_op jit(solution)/shard_map/pallas_call | solution.py:260
  90.0 0.0 collective-permute-done.9.refs_1_
  90.1 0.0 collective-permute-done.18.refs_5_
  90.1 2.0 %collective-permute-done.17.refs_4_ = f32[384,768]{1,0:T(8,128)S(1)} collective-permute-done((f32[384,768]{1,0:T(8,128)S(1)}, f32[384,768]{1,0:T(8,128)S(1)}, u32[]{:S(2)}, u32[]{:S(2)}) %collective-permute-start.17) | collective-permute-done | bytes 1179680 | tf_op jit(solution)/shard_map/ppermute | solution.py:26
  92.1 3.8 %shard_map.90 = f32[1,1792]{1,0:T(1,128)S(1)} custom-call(f32[384,768]{1,0:T(8,128)S(1)} %collective-permute-done.6.factor.refs_0_, f32[384,768]{1,0:T(8,128)S(1)} %collective-permute-done.9.refs_1_, f32[384,768]{1,0:T(8,128)S(1)} %collective-permute-done.4.refs_2_, f32[384,768]{1,0:T(8,128)S(1)} %collective-permute-done.10.refs_3_, ...), custom_call_target="tpu_custom_call" | custom-call | bytes 1000 | tf_op jit(solution)/shard_map/pallas_call | solution.py:260
  95.9 0.2 collective-permute-start.19
  96.1 1.0 %collective-permute-done.19 = f32[1,1792]{1,0:T(1,128)S(1)} collective-permute-done((f32[1,1792]{1,0:T(1,128)S(1)}, f32[1,1792]{1,0:T(1,128)S(1)}, u32[]{:S(2)}, u32[]{:S(2)}) %collective-permute-start.19) | collective-permute-done | bytes 7200 | tf_op jit(solution)/shard_map/ppermute | solution.py:26
  97.1 0.4 collective-permute-start.20
  97.5 0.0 collective-permute-start.21
  97.5 3.2 %collective-permute-start.22 = (f32[1,1792]{1,0:T(1,128)S(1)}, f32[1,1792]{1,0:T(1,128)S(1)}, u32[]{:S(2)}, u32[]{:S(2)}) collective-permute-start(f32[1,1792]{1,0:T(1,128)S(1)} %add.3.refs_0_), channel_id=1, source_target_pairs={{0,3},{1,2},{2,1},{3,0},{4,7},{5,6},{6,5},{7,4},{8,11},{9,10},{10,... | collective-permute-start | bytes 21512 | tf_op jit(solution)/shard_map/ppermute | solution.py:26
  100.7 0.2 collective-permute-done.20.refs_1_
  100.8 0.3 collective-permute-done.21.refs_2_
  101.1 1.2 %collective-permute-done.22.refs_3_ = f32[1,1792]{1,0:T(1,128)S(1)} collective-permute-done((f32[1,1792]{1,0:T(1,128)S(1)}, f32[1,1792]{1,0:T(1,128)S(1)}, u32[]{:S(2)}, u32[]{:S(2)}) %collective-permute-start.22) | collective-permute-done | bytes 7200 | tf_op jit(solution)/shard_map/ppermute | solution.py:26
  102.4 1.3 %shard_map.91 = (f32[1,768]{1,0:T(1,128)}, f32[2,512]{1,0:T(2,128)}) custom-call(s32[16]{0:T(128)} %parent_ref.3, f32[1,1792]{1,0:T(1,128)S(1)} %add.3.refs_0_, f32[1,1792]{1,0:T(1,128)S(1)} %collective-permute-done.20.refs_1_, f32[1,1792]{1,0:T(1,128)S(1)} %collective-permute-done.21.refs_2_, f32[1,1792]{1,0:T(1,128)S(1)} %collective-permute-done.22.refs_3_), custom_call_target="tpu_custom_call" | custom-call | bytes 1000 | tf_op jit(solution)/shard_map/pallas_call | solution.py:260
  (1 shorter events, 0.0 us)
Async XLA Ops:
  0.6 28.2 %collective-permute-start.4 = (f32[384,768]{1,0:T(8,128)}, f32[384,768]{1,0:T(8,128)S(1)}, u32[]{:S(2)}, u32[]{:S(2)}) collective-permute-start(f32[384,768]{1,0:T(8,128)} %bitcast.4), channel_id=1, source_target_pairs={{0,2},{2,0},{5,7},{7,5},{8,10},{10,8},{13,15},{15,13},{16,18},{18,... | collective-permute-start | bytes 3538952 | tf_op jit(solution)/shard_map/ppermute | solution.py:26
  5.5 6.0 %collective-permute-start = (f32[2,256,512]{2,1,0:T(8,128)}, f32[2,256,512]{2,1,0:T(8,128)S(1)}, u32[]{:S(2)}, u32[]{:S(2)}) collective-permute-start(f32[2,256,512]{2,1,0:T(8,128)} %own_rows.1), channel_id=1, source_target_pairs={{0,4},{1,5},{2,6},{3,7},{4,0},{5,1},{6,2},{7,3},{8,12},{9,13},{10,... | collective-permute-start | bytes 3145736 | tf_op jit(solution)/shard_map/ppermute | solution.py:26
  5.6 30.4 %copy-start = (f32[1,384,1536]{2,1,0:T(8,128)S(1)}, f32[1,384,1536]{2,1,0:T(8,128)}, u32[]{:S(2)}) copy-start(f32[1,384,1536]{2,1,0:T(8,128)} %param.7) | copy-start | bytes 7077892
  5.6 7.5 %collective-permute-start.2 = (f32[192,768]{1,0:T(8,128)}, f32[192,768]{1,0:T(8,128)S(1)}, u32[]{:S(2)}, u32[]{:S(2)}) collective-permute-start(f32[192,768]{1,0:T(8,128)} %bitcast.6), channel_id=1, source_target_pairs={{0,0},{1,4},{2,2},{3,6},{4,1},{5,5},{6,3},{7,7},{8,8},{9,12},{10,1... | collective-permute-start | bytes 1769480 | tf_op jit(solution)/shard_map/ppermute | solution.py:36
  7.5 21.4 %collective-permute-start.3 = (f32[192,768]{1,0:T(8,128)}, f32[192,768]{1,0:T(8,128)S(1)}, u32[]{:S(2)}, u32[]{:S(2)}) collective-permute-start(f32[192,768]{1,0:T(8,128)} %bitcast.7), channel_id=1, source_target_pairs={{0,2},{2,0},{5,7},{7,5},{8,10},{10,8},{13,15},{15,13},{16,18},{18,... | collective-permute-start | bytes 1769480 | tf_op jit(solution)/shard_map/ppermute | solution.py:26
  9.4 2.2 %collective-permute-start.1 = (f32[2,128,512]{2,1,0:T(8,128)}, f32[2,128,512]{2,1,0:T(8,128)S(1)}, u32[]{:S(2)}, u32[]{:S(2)}) collective-permute-start(f32[2,128,512]{2,1,0:T(8,128)} %own_inverse.1), channel_id=1, source_target_pairs={{0,4},{1,5},{2,6},{3,7},{4,0},{5,1},{6,2},{7,3},{8,12},{9,13},{10,... | collective-permute-start | bytes 1572872 | tf_op jit(solution)/shard_map/ppermute | solution.py:26
  28.8 1.5 %collective-permute-start.5 = (f32[2,384,512]{2,1,0:T(8,128)S(1)}, f32[2,384,512]{2,1,0:T(8,128)S(1)}, u32[]{:S(2)}, u32[]{:S(2)}) collective-permute-start(f32[2,384,512]{2,1,0:T(8,128)S(1)} %get-tuple-element.29), channel_id=1, source_target_pairs={{0,0},{1,4},{2,2},{3,6},{4,1},{5,5},{6,3},{7,7},{8,8},{9,12},{10,1... | collective-permute-start | bytes 4718600 | tf_op jit(solution)/shard_map/ppermute | solution.py:36
  29.6 0.7 collective-permute-start.7
  30.3 30.7 %collective-permute-start.8 = (f32[2,384,512]{2,1,0:T(8,128)S(1)}, f32[2,384,512]{2,1,0:T(8,128)S(1)}, u32[]{:S(2)}, u32[]{:S(2)}) collective-permute-start(f32[2,384,512]{2,1,0:T(8,128)S(1)} %collective-permute-done.5.refs_0_), channel_id=1, source_target_pairs={{0,2},{1,3},{2,0},{3,1},{4,6},{5,7},{6,4},{7,5},{8,10},{9,11},{10,... | collective-permute-start | bytes 4718600 | tf_op jit(solution)/shard_map/ppermute | solution.py:26
  32.8 14.2 %collective-permute-start.12 = (f32[192,768]{1,0:T(8,128)S(1)}, f32[192,768]{1,0:T(8,128)S(1)}, u32[]{:S(2)}, u32[]{:S(2)}) collective-permute-start(f32[192,768]{1,0:T(8,128)S(1)} %collective-permute-done.7.refs_3_), channel_id=1, source_target_pairs={{1,5},{3,7},{4,0},{6,2},{9,13},{11,15},{12,8},{14,10},{17,21},{19,... | collective-permute-start | bytes 1769480 | tf_op jit(solution)/shard_map/ppermute | solution.py:26
  34.0 16.4 %collective-permute-start.6 = (f32[384,768]{1,0:T(8,128)}, f32[384,768]{1,0:T(8,128)S(1)}, u32[]{:S(2)}, u32[]{:S(2)}) collective-permute-start(f32[384,768]{1,0:T(8,128)} %bitcast.5), channel_id=1, source_target_pairs={{0,0},{1,4},{2,2},{3,6},{4,1},{5,5},{6,3},{7,7},{8,8},{9,12},{10,1... | collective-permute-start | bytes 3538952 | tf_op jit(solution)/shard_map/ppermute | solution.py:36
  36.0 51.4 %collective-permute-start.16 = (f32[384,1536]{1,0:T(8,128)S(1)}, f32[384,1536]{1,0:T(8,128)S(1)}, u32[]{:S(2)}, u32[]{:S(2)}) collective-permute-start(f32[384,1536]{1,0:T(8,128)S(1)} %bitcast.3), channel_id=1, source_target_pairs={{0,0},{1,4},{2,2},{3,6},{4,1},{5,5},{6,3},{7,7},{8,8},{9,12},{10,1... | collective-permute-start | bytes 7077896 | tf_op jit(solution)/shard_map/ppermute | solution.py:36
  36.8 12.1 %collective-permute-start.11 = (f32[192,768]{1,0:T(8,128)S(1)}, f32[192,768]{1,0:T(8,128)S(1)}, u32[]{:S(2)}, u32[]{:S(2)}) collective-permute-start(f32[192,768]{1,0:T(8,128)S(1)} %collective-permute-done.2.refs_0_), channel_id=1, source_target_pairs={{0,4},{1,5},{2,6},{3,7},{4,0},{5,1},{6,2},{7,3},{8,12},{9,13},{10,... | collective-permute-start | bytes 1769480 | tf_op jit(solution)/shard_map/ppermute | solution.py:26
  46.9 3.5 %collective-permute-start.13 = (f32[192,768]{1,0:T(8,128)S(1)}, f32[192,768]{1,0:T(8,128)S(1)}, u32[]{:S(2)}, u32[]{:S(2)}) collective-permute-start(f32[192,768]{1,0:T(8,128)S(1)} %collective-permute-done.3.refs_2_), channel_id=1, source_target_pairs={{0,4},{2,6},{5,1},{7,3},{8,12},{10,14},{13,9},{15,11},{16,20},{18,... | collective-permute-start | bytes 1769480 | tf_op jit(solution)/shard_map/ppermute | solution.py:26
  48.9 22.6 %collective-permute-start.14 = (f32[2,384,512]{2,1,0:T(8,128)S(1)}, f32[2,384,512]{2,1,0:T(8,128)S(1)}, u32[]{:S(2)}, u32[]{:S(2)}) collective-permute-start(f32[2,384,512]{2,1,0:T(8,128)S(1)} %collective-permute-done.5.refs_0_), channel_id=1, source_target_pairs={{0,4},{1,5},{2,6},{3,7},{4,0},{5,1},{6,2},{7,3},{8,12},{9,13},{10,... | collective-permute-start | bytes 4718600 | tf_op jit(solution)/shard_map/ppermute | solution.py:26
  61.0 12.8 %collective-permute-start.15 = (f32[2,384,512]{2,1,0:T(8,128)S(1)}, f32[2,384,512]{2,1,0:T(8,128)S(1)}, u32[]{:S(2)}, u32[]{:S(2)}) collective-permute-start(f32[2,384,512]{2,1,0:T(8,128)S(1)} %collective-permute-done.8.refs_2_), channel_id=1, source_target_pairs={{0,4},{1,5},{2,6},{3,7},{4,0},{5,1},{6,2},{7,3},{8,12},{9,13},{10,... | collective-permute-start | bytes 4718600 | tf_op jit(solution)/shard_map/ppermute | solution.py:26
  67.8 19.5 %collective-permute-start.10 = (f32[384,768]{1,0:T(8,128)S(1)}, f32[384,768]{1,0:T(8,128)S(1)}, u32[]{:S(2)}, u32[]{:S(2)}) collective-permute-start(f32[384,768]{1,0:T(8,128)S(1)} %collective-permute-done.6.factor.refs_0_), channel_id=1, source_target_pairs={{1,3},{3,1},{4,6},{6,4},{9,11},{11,9},{12,14},{14,12},{17,19},{19,... | collective-permute-start | bytes 3538952 | tf_op jit(solution)/shard_map/ppermute | solution.py:26
  68.6 21.5 %collective-permute-start.9 = (f32[384,768]{1,0:T(8,128)S(1)}, f32[384,768]{1,0:T(8,128)S(1)}, u32[]{:S(2)}, u32[]{:S(2)}) collective-permute-start(f32[384,768]{1,0:T(8,128)S(1)} %collective-permute-done.6.factor.refs_0_), channel_id=1, source_target_pairs={{0,4},{1,5},{2,6},{3,7},{4,0},{5,1},{6,2},{7,3},{8,12},{9,13},{10,... | collective-permute-start | bytes 3538952 | tf_op jit(solution)/shard_map/ppermute | solution.py:26
  71.5 18.5 %collective-permute-start.18 = (f32[384,768]{1,0:T(8,128)S(1)}, f32[384,768]{1,0:T(8,128)S(1)}, u32[]{:S(2)}, u32[]{:S(2)}) collective-permute-start(f32[384,768]{1,0:T(8,128)S(1)} %collective-permute-done.4.refs_2_), channel_id=1, source_target_pairs={{0,4},{2,6},{5,1},{7,3},{8,12},{10,14},{13,9},{15,11},{16,20},{18,... | collective-permute-start | bytes 3538952 | tf_op jit(solution)/shard_map/ppermute | solution.py:26
  87.4 4.7 %collective-permute-start.17 = (f32[384,768]{1,0:T(8,128)S(1)}, f32[384,768]{1,0:T(8,128)S(1)}, u32[]{:S(2)}, u32[]{:S(2)}) collective-permute-start(f32[384,768]{1,0:T(8,128)S(1)} %collective-permute-done.10.refs_3_), channel_id=1, source_target_pairs={{1,5},{3,7},{4,0},{6,2},{9,13},{11,15},{12,8},{14,10},{17,21},{19,... | collective-permute-start | bytes 3538952 | tf_op jit(solution)/shard_map/ppermute | solution.py:26
  95.9 1.2 %collective-permute-start.19 = (f32[1,1792]{1,0:T(1,128)S(1)}, f32[1,1792]{1,0:T(1,128)S(1)}, u32[]{:S(2)}, u32[]{:S(2)}) collective-permute-start(f32[1,1792]{1,0:T(1,128)S(1)} %shard_map.90), channel_id=1, source_target_pairs={{0,4},{1,5},{2,6},{3,7},{4,0},{5,1},{6,2},{7,3},{8,12},{9,13},{10,... | collective-permute-start | bytes 21512 | tf_op jit(solution)/shard_map/ppermute | solution.py:26
  97.1 3.7 %collective-permute-start.20 = (f32[1,1792]{1,0:T(1,128)S(1)}, f32[1,1792]{1,0:T(1,128)S(1)}, u32[]{:S(2)}, u32[]{:S(2)}) collective-permute-start(f32[1,1792]{1,0:T(1,128)S(1)} %add.3.refs_0_), channel_id=1, source_target_pairs={{0,2},{1,3},{2,0},{3,1},{4,6},{5,7},{6,4},{7,5},{8,10},{9,11},{10,... | collective-permute-start | bytes 21512 | tf_op jit(solution)/shard_map/ppermute | solution.py:26
  97.5 3.6 %collective-permute-start.21 = (f32[1,1792]{1,0:T(1,128)S(1)}, f32[1,1792]{1,0:T(1,128)S(1)}, u32[]{:S(2)}, u32[]{:S(2)}) collective-permute-start(f32[1,1792]{1,0:T(1,128)S(1)} %add.3.refs_0_), channel_id=1, source_target_pairs={{0,1},{1,0},{2,3},{3,2},{4,5},{5,4},{6,7},{7,6},{8,9},{9,8},{10,11... | collective-permute-start | bytes 21512 | tf_op jit(solution)/shard_map/ppermute | solution.py:26
  97.5 4.9 %collective-permute-start.22 = (f32[1,1792]{1,0:T(1,128)S(1)}, f32[1,1792]{1,0:T(1,128)S(1)}, u32[]{:S(2)}, u32[]{:S(2)}) collective-permute-start(f32[1,1792]{1,0:T(1,128)S(1)} %add.3.refs_0_), channel_id=1, source_target_pairs={{0,3},{1,2},{2,1},{3,0},{4,7},{5,6},{6,5},{7,4},{8,11},{9,10},{10,... | collective-permute-start | bytes 21512 | tf_op jit(solution)/shard_map/ppermute | solution.py:26

commit v3 on v2

--- a/solution.py
+++ b/solution.py
@@ -132,7 +132,7 @@
 
 
 def diagonal_kernel(pieces, index, factor, *refs):
-    diag_high, diag_low, pick_high, pick_low, weights, parent_sum = refs[2 * pieces - 2 :]
+    diag_high, diag_low, pick_high, weights, parent_sum = refs[2 * pieces - 2 :]
     _, block = place_of()
     own_rows, size = refs[0].shape
     parent_sum[...] = column_sum(refs[0][...] * refs[0][...])
@@ -146,17 +146,20 @@
             put(pair[0])
         else:
             store(pair, put)
+    kid_block = index.shape[2]
     for kid in range(2):
         for mask in range(pieces):
-            pick = picks(index[kid, mask : mask + 1, :], 0, size)
-            pick_high[kid, mask] = rounded(dot(diag_high[...], pick))
-            pick_low[kid, mask] = rounded(dot(diag_low[...], pick))
+
+            @pl.when((block ^ mask) * kid_block < size)
+            def _(kid=kid, mask=mask):
+                pick_high[kid, mask] = rounded(dot(diag_high[...], picks(index[kid, mask : mask + 1, :], 0, size)))
+
     factor_halves = halves(factor[...])
     for span in spans(size):
         weights[:, span] = product(factor_halves, (diag_high[:, span], diag_low[:, span]))
 
 
-def kid_kernel(pieces, index, pick_high, pick_low, factor, *refs):
+def kid_kernel(pieces, index, pick_high, factor, *refs):
     kids = refs[:pieces]
     reduced, lift_high, lower_high, kid_sum, inv_high, inv_low, lifted, lower = refs[pieces:]
     _, block = place_of()
@@ -164,6 +167,7 @@
     kid_block = index.shape[2]
     inv_block, own_rows = kids[0].shape[1] - kid_block, size // pieces
     factor_high = rounded(factor[...])
+    middle, kid_size = border_size // 2, lifted.shape[1]
     for kid in range(2):
         own_inverse = kids[0][kid, kid_block:]
         for mask in range(pieces):
@@ -172,15 +176,26 @@
             inv_high[pl.ds(start, inv_block), :] = high
             inv_low[pl.ds(start, inv_block), :] = low
         inverse = inv_high[...], inv_low[...]
+        lifted[...] = jnp.zeros(lifted.shape, jnp.float32)
+        lower[middle:] = jnp.zeros((border_size - middle, kid_size), jnp.float32)
         for mask in range(pieces):
             high, low = halves(product(halves(kids[mask][kid, :kid_block]), inverse))
-            lifted_part = dot(pick_high[kid, mask], high) + dot(pick_low[kid, mask], high)
             places = index[kid, mask : mask + 1, :]
+            first_row = (block ^ mask) * kid_block
+
+            @pl.when(first_row < size)
+            def _(kid=kid, mask=mask, high=high):
+                lifted[...] += dot(pick_high[kid, mask], high)
+
             low_part = dot(picks(places, size + block * own_border, own_border), low)
-            part = dot(picks(places, size, border_size), high)
-            lifted[...] = lifted_part if mask == 0 else lifted[...] + lifted_part
             reduced[kid] = low_part if mask == 0 else reduced[kid] + low_part
-            lower[...] = part if mask == 0 else lower[...] + part
+            part = dot(picks(places, size, middle), high)
+            lower[:middle] = part if mask == 0 else lower[:middle] + part
+
+            @pl.when(first_row + kid_block - 1 + border_size - pieces * kid_block >= middle)
+            def _(places=places, high=high):
+                lower[middle:] += dot(picks(places, size + middle, border_size - middle), high)
+
         own = lifted[pl.ds(pl.multiple_of(block * own_rows, 16), own_rows), :]
         kid_sum[kid : kid + 1] = column_sum(own_inverse * own_inverse) + column_sum(own * own)
         lift_high[kid] = rounded(lifted[...])
@@ -301,25 +316,25 @@
         return result
 
     last = pieces - 2
-    keep_diagonal = over_fronts(diagonal, 0)
-    keep_factor = over_fronts(factor, 0)
-    own_diagonal = cross(diagonal)
+    raw_rows, raw_inverse = exchange(kid_rows, 1, 0), exchange(kid_inverse, 1, 0)
+    keep_diagonal = over_fronts(after(diagonal, raw_rows, raw_inverse), 0)
+    keep_factor = over_fronts(after(factor, raw_rows, raw_inverse), 0)
+    own_diagonal = cross(after(diagonal, raw_rows, raw_inverse))
     kid_shape = (2, kid_block + kid_inverse.shape[1], kid_size)
     own_kids, index = call(
         select_kernel, (shape_of(kid_shape), shape_of((2, pieces, kid_block), jnp.int32)), 6, scalars=1, loose=4
-    )(child_parent, child_index, kid_rows, kid_inverse, exchange(kid_rows, 1, 0), exchange(kid_inverse, 1, 0))
+    )(child_parent, child_index, kid_rows, kid_inverse, raw_rows, raw_inverse)
     own_kids = cross(after(own_kids, own_diagonal, keep_diagonal[last], keep_factor[last]))
     swap_diagonal = over_fronts(own_diagonal, 1)
     kid_parts = over_fronts(after(own_kids, swap_diagonal[last]))
     own_factor = cross(after(factor, own_kids))
     diagonal_parts = gathered(own_diagonal, keep_diagonal, swap_diagonal, [own_kids], [own_kids], [own_kids])
 
-    diag_high, diag_low, pick_high, pick_low, weights, parent_sum = call(
+    diag_high, diag_low, pick_high, weights, parent_sum = call(
         functools.partial(diagonal_kernel, pieces),
         (
             shape_of((size, size), half),
             shape_of((size, size), half),
-            shape_of((2, pieces, size, kid_block), half),
             shape_of((2, pieces, size, kid_block), half),
             shape_of((own_border, size)),
             shape_of((1, size)),
@@ -346,7 +361,7 @@
             pltpu.VMEM((size, kid_size), jnp.float32),
             pltpu.VMEM((border_size, kid_size), jnp.float32),
         ],
-    )(index, pick_high, pick_low, own_factor, *kid_parts)
+    )(index, pick_high, own_factor, *kid_parts)
 
     border_high, border_lower = call(
         border_kernel, (shape_of(border.shape, half), shape_of((2, own_border, kid_size))), 8

time: 104 us -> 110 us (1.058)
  waiting for transfers between devices: 27.4 us -> 40.6 us
  starting transfers between devices: 46.7 us -> 40.3 us
    ppermute x19, waiting for transfers between devices: 27.4 us -> 40.6 us  [exchange(): return lax.ppermute(value, ('leaf', 'front'), pairs)]
    ppermute x19, starting transfers between devices: 41.4 us -> 35 us  [exchange(): return lax.ppermute(value, ('leaf', 'front'), pairs)]
  transfers between devices with their start and end apart: 23 -> 23, of which waited for: 9 -> 9; matrix products, arithmetic and copies ran while one was open for 0% -> 0% of each run, Pallas kernels for 23% -> 21%
where the time goes in v3:
time: 110 us
  waiting for transfers between devices  40.6 us (37%)
  starting transfers between devices  40.3 us (37%)
  Pallas kernels  28 us (25%)
    ppermute x19, waiting for transfers between devices, exchange(): return lax.ppermute(value, ('leaf', 'front'), pairs)  40.6 us
    ppermute x19, starting transfers between devices, exchange(): return lax.ppermute(value, ('leaf', 'front'), pairs)  35 us
    pallas_call x6, Pallas kernels, run(): pl.pallas_call(kernel, out_shape=results, in_specs=specs, out_specs=jax.t...  28 us
    ppermute x4, starting transfers between devices, cross(): return lax.ppermute(value, ('leaf', 'front'), pairs)  5.34 us
  transfers between devices with their start and end apart: 23, of which 9 were waited for; matrix products, arithmetic and copies ran while one was open for 0% of the time, Pallas kernels for 21%

profile of v3, /device:TPU:0, one launch (start us, length us, event | category | flops | bytes accessed | tf_op | source)
XLA Modules:
  0.0 109.9 jit_solution(5771789060354608884)
XLA Ops:
  0.6 0.5 collective-permute-start
  1.1 0.1 collective-permute-start.1
  1.2 3.2 %collective-permute-done.1.other_inverse = f32[2,128,512]{2,1,0:T(8,128)S(1)} collective-permute-done((f32[2,128,512]{2,1,0:T(8,128)}, f32[2,128,512]{2,1,0:T(8,128)S(1)}, u32[]{:S(2)}, u32[]{:S(2)}) %collective-permute-start.1) | collective-permute-done | bytes 524320 | tf_op jit(solution)/shard_map/ppermute | solution.py:26
  4.4 0.0 collective-permute-done.other_rows
  4.4 4.8 %collective-permute-start.4 = (f32[384,768]{1,0:T(8,128)}, f32[384,768]{1,0:T(8,128)S(1)}, u32[]{:S(2)}, u32[]{:S(2)}) collective-permute-start(f32[384,768]{1,0:T(8,128)} %bitcast.4), channel_id=1, source_target_pairs={{0,2},{2,0},{5,7},{7,5},{8,10},{10,8},{13,15},{15,13},{16,18},{18,... | collective-permute-start | bytes 3538952 | tf_op jit(solution)/shard_map/ppermute | solution.py:26
  9.2 0.0 copy-start
  9.2 1.9 %collective-permute-start.2 = (f32[192,768]{1,0:T(8,128)}, f32[192,768]{1,0:T(8,128)S(1)}, u32[]{:S(2)}, u32[]{:S(2)}) collective-permute-start(f32[192,768]{1,0:T(8,128)} %bitcast.6), channel_id=1, source_target_pairs={{0,0},{1,4},{2,2},{3,6},{4,1},{5,5},{6,3},{7,7},{8,8},{9,12},{10,1... | collective-permute-start | bytes 1769480 | tf_op jit(solution)/shard_map/ppermute | solution.py:36
  11.1 1.9 %collective-permute-start.3 = (f32[192,768]{1,0:T(8,128)}, f32[192,768]{1,0:T(8,128)S(1)}, u32[]{:S(2)}, u32[]{:S(2)}) collective-permute-start(f32[192,768]{1,0:T(8,128)} %bitcast.7), channel_id=1, source_target_pairs={{0,2},{2,0},{5,7},{7,5},{8,10},{10,8},{13,15},{15,13},{16,18},{18,... | collective-permute-start | bytes 1769480 | tf_op jit(solution)/shard_map/ppermute | solution.py:26
  13.0 1.6 %shard_map.86 = (f32[2,384,512]{2,1,0:T(8,128)S(1)}, s32[2,4,256]{2,1,0:T(4,128)S(1)}) custom-call(s32[16]{0:T(128)} %parent_ref.3, s32[16,1024]{1,0:T(8,128)} %index_ref.1, f32[2,256,512]{2,1,0:T(8,128)} %own_rows.1, f32[2,128,512]{2,1,0:T(8,128)} %own_inverse.1, f32[2,256,512]{2,1,0:T(8,128)S(1)} %collective-permute-done.other_rows, ...), custom_call_target="tpu_custom_call" | custom-call | bytes 1000 | tf_op jit(solution)/shard_map/pallas_call | solution.py:275
  14.5 0.0 collective-permute-done.2.refs_0_
  14.6 19.2 %collective-permute-done.3.refs_2_ = f32[192,768]{1,0:T(8,128)S(1)} collective-permute-done((f32[192,768]{1,0:T(8,128)}, f32[192,768]{1,0:T(8,128)S(1)}, u32[]{:S(2)}, u32[]{:S(2)}) %collective-permute-start.3) | collective-permute-done | bytes 589856 | tf_op jit(solution)/shard_map/ppermute | solution.py:26
  33.8 0.0 collective-permute-done.4.refs_2_
  33.8 0.8 collective-permute-start.5
  34.5 0.7 collective-permute-start.7
  35.3 0.0 collective-permute-done.7.refs_3_
  35.3 0.0 collective-permute-done.5.refs_0_
  35.3 2.4 %collective-permute-start.8 = (f32[2,384,512]{2,1,0:T(8,128)S(1)}, f32[2,384,512]{2,1,0:T(8,128)S(1)}, u32[]{:S(2)}, u32[]{:S(2)}) collective-permute-start(f32[2,384,512]{2,1,0:T(8,128)S(1)} %collective-permute-done.5.refs_0_), channel_id=1, source_target_pairs={{0,2},{1,3},{2,0},{3,1},{4,6},{5,7},{6,4},{7,5},{8,10},{9,11},{10,... | collective-permute-start | bytes 4718600 | tf_op jit(solution)/shard_map/ppermute | solution.py:26
  37.7 1.3 %collective-permute-start.12 = (f32[192,768]{1,0:T(8,128)S(1)}, f32[192,768]{1,0:T(8,128)S(1)}, u32[]{:S(2)}, u32[]{:S(2)}) collective-permute-start(f32[192,768]{1,0:T(8,128)S(1)} %collective-permute-done.7.refs_3_), channel_id=1, source_target_pairs={{1,5},{3,7},{4,0},{6,2},{9,13},{11,15},{12,8},{14,10},{17,21},{19,... | collective-permute-start | bytes 1769480 | tf_op jit(solution)/shard_map/ppermute | solution.py:26
  39.0 1.9 %collective-permute-start.6 = (f32[384,768]{1,0:T(8,128)}, f32[384,768]{1,0:T(8,128)S(1)}, u32[]{:S(2)}, u32[]{:S(2)}) collective-permute-start(f32[384,768]{1,0:T(8,128)} %bitcast.5), channel_id=1, source_target_pairs={{0,0},{1,4},{2,2},{3,6},{4,1},{5,5},{6,3},{7,7},{8,8},{9,12},{10,1... | collective-permute-start | bytes 3538952 | tf_op jit(solution)/shard_map/ppermute | solution.py:36
  40.9 0.0 copy-done
  40.9 0.8 collective-permute-start.16
  41.7 7.0 %collective-permute-start.11 = (f32[192,768]{1,0:T(8,128)S(1)}, f32[192,768]{1,0:T(8,128)S(1)}, u32[]{:S(2)}, u32[]{:S(2)}) collective-permute-start(f32[192,768]{1,0:T(8,128)S(1)} %collective-permute-done.2.refs_0_), channel_id=1, source_target_pairs={{0,4},{1,5},{2,6},{3,7},{4,0},{5,1},{6,2},{7,3},{8,12},{9,13},{10,... | collective-permute-start | bytes 1769480 | tf_op jit(solution)/shard_map/ppermute | solution.py:26
  48.7 0.0 collective-permute-done.12.refs_4_
  48.7 2.0 %collective-permute-start.13 = (f32[192,768]{1,0:T(8,128)S(1)}, f32[192,768]{1,0:T(8,128)S(1)}, u32[]{:S(2)}, u32[]{:S(2)}) collective-permute-start(f32[192,768]{1,0:T(8,128)S(1)} %collective-permute-done.3.refs_2_), channel_id=1, source_target_pairs={{0,4},{2,6},{5,1},{7,3},{8,12},{10,14},{13,9},{15,11},{16,20},{18,... | collective-permute-start | bytes 1769480 | tf_op jit(solution)/shard_map/ppermute | solution.py:26
  50.7 0.0 collective-permute-done.11.refs_1_
  50.7 0.1 collective-permute-start.14
  50.8 1.5 %collective-permute-done.13.refs_5_ = f32[192,768]{1,0:T(8,128)S(1)} collective-permute-done((f32[192,768]{1,0:T(8,128)S(1)}, f32[192,768]{1,0:T(8,128)S(1)}, u32[]{:S(2)}, u32[]{:S(2)}) %collective-permute-start.13) | collective-permute-done | bytes 589856 | tf_op jit(solution)/shard_map/ppermute | solution.py:26
  52.3 0.0 collective-permute-done.6.factor.refs_0_
  52.3 5.0 %shard_map.87 = (bf16[768,768]{1,0:T(8,128)(2,1)S(1)}, bf16[768,768]{1,0:T(8,128)(2,1)S(1)}, bf16[2,4,768,256]{3,2,1,0:T(8,128)(2,1)S(1)}, f32[384,768]{1,0:T(8,128)S(1)}, f32[1,768]{1,0:T(1,128)S(1)}) custom-call(s32[2,4,256]{2,1,0:T(4,128)S(1)} %get-tuple-element.36.index, f32[384,768]{1,0:T(8,128)S(1)} %collective-permute-done.6.factor.refs_0_, ...), custom_call_target="tpu_custom_call" | custom-call | bytes 1000 | tf_op jit(solution)/shard_map/pallas_call | solution.py:275
  57.3 12.0 %collective-permute-done.8.refs_2_ = f32[2,384,512]{2,1,0:T(8,128)S(1)} collective-permute-done((f32[2,384,512]{2,1,0:T(8,128)S(1)}, f32[2,384,512]{2,1,0:T(8,128)S(1)}, u32[]{:S(2)}, u32[]{:S(2)}) %collective-permute-start.8) | collective-permute-done | bytes 1572896 | tf_op jit(solution)/shard_map/ppermute | solution.py:26
  69.3 3.5 %collective-permute-start.15 = (f32[2,384,512]{2,1,0:T(8,128)S(1)}, f32[2,384,512]{2,1,0:T(8,128)S(1)}, u32[]{:S(2)}, u32[]{:S(2)}) collective-permute-start(f32[2,384,512]{2,1,0:T(8,128)S(1)} %collective-permute-done.8.refs_2_), channel_id=1, source_target_pairs={{0,4},{1,5},{2,6},{3,7},{4,0},{5,1},{6,2},{7,3},{8,12},{9,13},{10,... | collective-permute-start | bytes 4718600 | tf_op jit(solution)/shard_map/ppermute | solution.py:26
  72.8 0.7 collective-permute-start.10
  73.5 3.0 %collective-permute-start.9 = (f32[384,768]{1,0:T(8,128)S(1)}, f32[384,768]{1,0:T(8,128)S(1)}, u32[]{:S(2)}, u32[]{:S(2)}) collective-permute-start(f32[384,768]{1,0:T(8,128)S(1)} %collective-permute-done.6.factor.refs_0_), channel_id=1, source_target_pairs={{0,4},{1,5},{2,6},{3,7},{4,0},{5,1},{6,2},{7,3},{8,12},{9,13},{10,... | collective-permute-start | bytes 3538952 | tf_op jit(solution)/shard_map/ppermute | solution.py:26
  76.5 0.0 collective-permute-done.14.refs_1_
  76.5 2.0 %collective-permute-start.18 = (f32[384,768]{1,0:T(8,128)S(1)}, f32[384,768]{1,0:T(8,128)S(1)}, u32[]{:S(2)}, u32[]{:S(2)}) collective-permute-start(f32[384,768]{1,0:T(8,128)S(1)} %collective-permute-done.4.refs_2_), channel_id=1, source_target_pairs={{0,4},{2,6},{5,1},{7,3},{8,12},{10,14},{13,9},{15,11},{16,20},{18,... | collective-permute-start | bytes 3538952 | tf_op jit(solution)/shard_map/ppermute | solution.py:26
  78.5 0.0 collective-permute-done.15.refs_3_
  78.5 15.0 %shard_map.88 = (f32[2,384,512]{2,1,0:T(8,128)S(1)}, bf16[2,768,512]{2,1,0:T(8,128)(2,1)S(1)}, bf16[2,1536,512]{2,1,0:T(8,128)(2,1)S(1)}, f32[2,512]{1,0:T(2,128)S(1)}) custom-call(s32[2,4,256]{2,1,0:T(4,128)S(1)} %get-tuple-element.36.index, bf16[2,4,768,256]{3,2,1,0:T(8,128)(2,1)S(1)} %get-tuple-element.40.pick_high, ...), custom_call_target="tpu_custom_call" | custom-call | bytes 1000 | tf_op jit(solution)/shard_map/pallas_call | solution.py:275
  93.5 0.0 collective-permute-done.16.border
  93.6 0.0 collective-permute-done.10.refs_3_
  93.6 1.3 %collective-permute-start.17 = (f32[384,768]{1,0:T(8,128)S(1)}, f32[384,768]{1,0:T(8,128)S(1)}, u32[]{:S(2)}, u32[]{:S(2)}) collective-permute-start(f32[384,768]{1,0:T(8,128)S(1)} %collective-permute-done.10.refs_3_), channel_id=1, source_target_pairs={{1,5},{3,7},{4,0},{6,2},{9,13},{11,15},{12,8},{14,10},{17,21},{19,... | collective-permute-start | bytes 3538952 | tf_op jit(solution)/shard_map/ppermute | solution.py:26
  94.9 1.4 %shard_map.89 = (bf16[384,1536]{1,0:T(8,128)(2,1)S(1)}, f32[2,384,512]{2,1,0:T(8,128)S(1)}) custom-call(f32[384,1536]{1,0:T(8,128)S(1)} %collective-permute-done.16.border, bf16[2,1536,512]{2,1,0:T(8,128)(2,1)S(1)} %get-tuple-element.47.lower_high), custom_call_target="tpu_custom_call" | custom-call | bytes 1000 | tf_op jit(solution)/shard_map/pallas_call | solution.py:275
  96.3 0.0 collective-permute-done.9.refs_1_
  96.3 0.0 collective-permute-done.18.refs_5_
  96.3 2.0 %collective-permute-done.17.refs_4_ = f32[384,768]{1,0:T(8,128)S(1)} collective-permute-done((f32[384,768]{1,0:T(8,128)S(1)}, f32[384,768]{1,0:T(8,128)S(1)}, u32[]{:S(2)}, u32[]{:S(2)}) %collective-permute-start.17) | collective-permute-done | bytes 1179680 | tf_op jit(solution)/shard_map/ppermute | solution.py:26
  98.3 3.7 %shard_map.90 = f32[1,1792]{1,0:T(1,128)S(1)} custom-call(f32[384,768]{1,0:T(8,128)S(1)} %collective-permute-done.6.factor.refs_0_, f32[384,768]{1,0:T(8,128)S(1)} %collective-permute-done.9.refs_1_, f32[384,768]{1,0:T(8,128)S(1)} %collective-permute-done.4.refs_2_, f32[384,768]{1,0:T(8,128)S(1)} %collective-permute-done.10.refs_3_, ...), custom_call_target="tpu_custom_call" | custom-call | bytes 1000 | tf_op jit(solution)/shard_map/pallas_call | solution.py:275
  102.0 0.2 collective-permute-start.19
  102.2 1.0 collective-permute-done.19
  103.3 0.3 collective-permute-start.20
  103.6 0.2 collective-permute-start.21
  103.8 3.1 %collective-permute-start.22 = (f32[1,1792]{1,0:T(1,128)S(1)}, f32[1,1792]{1,0:T(1,128)S(1)}, u32[]{:S(2)}, u32[]{:S(2)}) collective-permute-start(f32[1,1792]{1,0:T(1,128)S(1)} %add.3.refs_0_), channel_id=1, source_target_pairs={{0,3},{1,2},{2,1},{3,0},{4,7},{5,6},{6,5},{7,4},{8,11},{9,10},{10,... | collective-permute-start | bytes 21512 | tf_op jit(solution)/shard_map/ppermute | solution.py:26
  106.8 0.2 collective-permute-done.20.refs_1_
  107.0 0.3 collective-permute-done.21.refs_2_
  107.3 1.3 %collective-permute-done.22.refs_3_ = f32[1,1792]{1,0:T(1,128)S(1)} collective-permute-done((f32[1,1792]{1,0:T(1,128)S(1)}, f32[1,1792]{1,0:T(1,128)S(1)}, u32[]{:S(2)}, u32[]{:S(2)}) %collective-permute-start.22) | collective-permute-done | bytes 7200 | tf_op jit(solution)/shard_map/ppermute | solution.py:26
  108.5 1.3 %shard_map.91 = (f32[1,768]{1,0:T(1,128)}, f32[2,512]{1,0:T(2,128)}) custom-call(s32[16]{0:T(128)} %parent_ref.3, f32[1,1792]{1,0:T(1,128)S(1)} %add.3.refs_0_, f32[1,1792]{1,0:T(1,128)S(1)} %collective-permute-done.20.refs_1_, f32[1,1792]{1,0:T(1,128)S(1)} %collective-permute-done.21.refs_2_, f32[1,1792]{1,0:T(1,128)S(1)} %collective-permute-done.22.refs_3_), custom_call_target="tpu_custom_call" | custom-call | bytes 1000 | tf_op jit(solution)/shard_map/pallas_call | solution.py:275
  (1 shorter events, 0.0 us)
Async XLA Ops:
  0.6 3.8 %collective-permute-start = (f32[2,256,512]{2,1,0:T(8,128)}, f32[2,256,512]{2,1,0:T(8,128)S(1)}, u32[]{:S(2)}, u32[]{:S(2)}) collective-permute-start(f32[2,256,512]{2,1,0:T(8,128)} %own_rows.1), channel_id=1, source_target_pairs={{0,4},{1,5},{2,6},{3,7},{4,0},{5,1},{6,2},{7,3},{8,12},{9,13},{10,... | collective-permute-start | bytes 3145736 | tf_op jit(solution)/shard_map/ppermute | solution.py:26
  1.1 3.2 %collective-permute-start.1 = (f32[2,128,512]{2,1,0:T(8,128)}, f32[2,128,512]{2,1,0:T(8,128)S(1)}, u32[]{:S(2)}, u32[]{:S(2)}) collective-permute-start(f32[2,128,512]{2,1,0:T(8,128)} %own_inverse.1), channel_id=1, source_target_pairs={{0,4},{1,5},{2,6},{3,7},{4,0},{5,1},{6,2},{7,3},{8,12},{9,13},{10,... | collective-permute-start | bytes 1572872 | tf_op jit(solution)/shard_map/ppermute | solution.py:26
  4.4 29.4 %collective-permute-start.4 = (f32[384,768]{1,0:T(8,128)}, f32[384,768]{1,0:T(8,128)S(1)}, u32[]{:S(2)}, u32[]{:S(2)}) collective-permute-start(f32[384,768]{1,0:T(8,128)} %bitcast.4), channel_id=1, source_target_pairs={{0,2},{2,0},{5,7},{7,5},{8,10},{10,8},{13,15},{15,13},{16,18},{18,... | collective-permute-start | bytes 3538952 | tf_op jit(solution)/shard_map/ppermute | solution.py:26
  9.2 31.7 %copy-start = (f32[1,384,1536]{2,1,0:T(8,128)S(1)}, f32[1,384,1536]{2,1,0:T(8,128)}, u32[]{:S(2)}) copy-start(f32[1,384,1536]{2,1,0:T(8,128)} %param.7) | copy-start | bytes 7077892
  9.2 5.3 %collective-permute-start.2 = (f32[192,768]{1,0:T(8,128)}, f32[192,768]{1,0:T(8,128)S(1)}, u32[]{:S(2)}, u32[]{:S(2)}) collective-permute-start(f32[192,768]{1,0:T(8,128)} %bitcast.6), channel_id=1, source_target_pairs={{0,0},{1,4},{2,2},{3,6},{4,1},{5,5},{6,3},{7,7},{8,8},{9,12},{10,1... | collective-permute-start | bytes 1769480 | tf_op jit(solution)/shard_map/ppermute | solution.py:36
  11.1 22.7 %collective-permute-start.3 = (f32[192,768]{1,0:T(8,128)}, f32[192,768]{1,0:T(8,128)S(1)}, u32[]{:S(2)}, u32[]{:S(2)}) collective-permute-start(f32[192,768]{1,0:T(8,128)} %bitcast.7), channel_id=1, source_target_pairs={{0,2},{2,0},{5,7},{7,5},{8,10},{10,8},{13,15},{15,13},{16,18},{18,... | collective-permute-start | bytes 1769480 | tf_op jit(solution)/shard_map/ppermute | solution.py:26
  33.8 1.5 %collective-permute-start.5 = (f32[2,384,512]{2,1,0:T(8,128)S(1)}, f32[2,384,512]{2,1,0:T(8,128)S(1)}, u32[]{:S(2)}, u32[]{:S(2)}) collective-permute-start(f32[2,384,512]{2,1,0:T(8,128)S(1)} %get-tuple-element.32), channel_id=1, source_target_pairs={{0,0},{1,4},{2,2},{3,6},{4,1},{5,5},{6,3},{7,7},{8,8},{9,12},{10,1... | collective-permute-start | bytes 4718600 | tf_op jit(solution)/shard_map/ppermute | solution.py:36
  34.5 0.7 collective-permute-start.7
  35.3 34.0 %collective-permute-start.8 = (f32[2,384,512]{2,1,0:T(8,128)S(1)}, f32[2,384,512]{2,1,0:T(8,128)S(1)}, u32[]{:S(2)}, u32[]{:S(2)}) collective-permute-start(f32[2,384,512]{2,1,0:T(8,128)S(1)} %collective-permute-done.5.refs_0_), channel_id=1, source_target_pairs={{0,2},{1,3},{2,0},{3,1},{4,6},{5,7},{6,4},{7,5},{8,10},{9,11},{10,... | collective-permute-start | bytes 4718600 | tf_op jit(solution)/shard_map/ppermute | solution.py:26
  37.7 11.0 %collective-permute-start.12 = (f32[192,768]{1,0:T(8,128)S(1)}, f32[192,768]{1,0:T(8,128)S(1)}, u32[]{:S(2)}, u32[]{:S(2)}) collective-permute-start(f32[192,768]{1,0:T(8,128)S(1)} %collective-permute-done.7.refs_3_), channel_id=1, source_target_pairs={{1,5},{3,7},{4,0},{6,2},{9,13},{11,15},{12,8},{14,10},{17,21},{19,... | collective-permute-start | bytes 1769480 | tf_op jit(solution)/shard_map/ppermute | solution.py:26
  39.0 13.3 %collective-permute-start.6 = (f32[384,768]{1,0:T(8,128)}, f32[384,768]{1,0:T(8,128)S(1)}, u32[]{:S(2)}, u32[]{:S(2)}) collective-permute-start(f32[384,768]{1,0:T(8,128)} %bitcast.5), channel_id=1, source_target_pairs={{0,0},{1,4},{2,2},{3,6},{4,1},{5,5},{6,3},{7,7},{8,8},{9,12},{10,1... | collective-permute-start | bytes 3538952 | tf_op jit(solution)/shard_map/ppermute | solution.py:36
  40.9 52.6 %collective-permute-start.16 = (f32[384,1536]{1,0:T(8,128)S(1)}, f32[384,1536]{1,0:T(8,128)S(1)}, u32[]{:S(2)}, u32[]{:S(2)}) collective-permute-start(f32[384,1536]{1,0:T(8,128)S(1)} %bitcast.3), channel_id=1, source_target_pairs={{0,0},{1,4},{2,2},{3,6},{4,1},{5,5},{6,3},{7,7},{8,8},{9,12},{10,1... | collective-permute-start | bytes 7077896 | tf_op jit(solution)/shard_map/ppermute | solution.py:36
  41.7 9.0 %collective-permute-start.11 = (f32[192,768]{1,0:T(8,128)S(1)}, f32[192,768]{1,0:T(8,128)S(1)}, u32[]{:S(2)}, u32[]{:S(2)}) collective-permute-start(f32[192,768]{1,0:T(8,128)S(1)} %collective-permute-done.2.refs_0_), channel_id=1, source_target_pairs={{0,4},{1,5},{2,6},{3,7},{4,0},{5,1},{6,2},{7,3},{8,12},{9,13},{10,... | collective-permute-start | bytes 1769480 | tf_op jit(solution)/shard_map/ppermute | solution.py:26
  48.7 3.5 %collective-permute-start.13 = (f32[192,768]{1,0:T(8,128)S(1)}, f32[192,768]{1,0:T(8,128)S(1)}, u32[]{:S(2)}, u32[]{:S(2)}) collective-permute-start(f32[192,768]{1,0:T(8,128)S(1)} %collective-permute-done.3.refs_2_), channel_id=1, source_target_pairs={{0,4},{2,6},{5,1},{7,3},{8,12},{10,14},{13,9},{15,11},{16,20},{18,... | collective-permute-start | bytes 1769480 | tf_op jit(solution)/shard_map/ppermute | solution.py:26
  50.7 25.8 %collective-permute-start.14 = (f32[2,384,512]{2,1,0:T(8,128)S(1)}, f32[2,384,512]{2,1,0:T(8,128)S(1)}, u32[]{:S(2)}, u32[]{:S(2)}) collective-permute-start(f32[2,384,512]{2,1,0:T(8,128)S(1)} %collective-permute-done.5.refs_0_), channel_id=1, source_target_pairs={{0,4},{1,5},{2,6},{3,7},{4,0},{5,1},{6,2},{7,3},{8,12},{9,13},{10,... | collective-permute-start | bytes 4718600 | tf_op jit(solution)/shard_map/ppermute | solution.py:26
  69.3 9.2 %collective-permute-start.15 = (f32[2,384,512]{2,1,0:T(8,128)S(1)}, f32[2,384,512]{2,1,0:T(8,128)S(1)}, u32[]{:S(2)}, u32[]{:S(2)}) collective-permute-start(f32[2,384,512]{2,1,0:T(8,128)S(1)} %collective-permute-done.8.refs_2_), channel_id=1, source_target_pairs={{0,4},{1,5},{2,6},{3,7},{4,0},{5,1},{6,2},{7,3},{8,12},{9,13},{10,... | collective-permute-start | bytes 4718600 | tf_op jit(solution)/shard_map/ppermute | solution.py:26
  72.8 20.8 %collective-permute-start.10 = (f32[384,768]{1,0:T(8,128)S(1)}, f32[384,768]{1,0:T(8,128)S(1)}, u32[]{:S(2)}, u32[]{:S(2)}) collective-permute-start(f32[384,768]{1,0:T(8,128)S(1)} %collective-permute-done.6.factor.refs_0_), channel_id=1, source_target_pairs={{1,3},{3,1},{4,6},{6,4},{9,11},{11,9},{12,14},{14,12},{17,19},{19,... | collective-permute-start | bytes 3538952 | tf_op jit(solution)/shard_map/ppermute | solution.py:26
  73.5 22.8 %collective-permute-start.9 = (f32[384,768]{1,0:T(8,128)S(1)}, f32[384,768]{1,0:T(8,128)S(1)}, u32[]{:S(2)}, u32[]{:S(2)}) collective-permute-start(f32[384,768]{1,0:T(8,128)S(1)} %collective-permute-done.6.factor.refs_0_), channel_id=1, source_target_pairs={{0,4},{1,5},{2,6},{3,7},{4,0},{5,1},{6,2},{7,3},{8,12},{9,13},{10,... | collective-permute-start | bytes 3538952 | tf_op jit(solution)/shard_map/ppermute | solution.py:26
  76.5 19.8 %collective-permute-start.18 = (f32[384,768]{1,0:T(8,128)S(1)}, f32[384,768]{1,0:T(8,128)S(1)}, u32[]{:S(2)}, u32[]{:S(2)}) collective-permute-start(f32[384,768]{1,0:T(8,128)S(1)} %collective-permute-done.4.refs_2_), channel_id=1, source_target_pairs={{0,4},{2,6},{5,1},{7,3},{8,12},{10,14},{13,9},{15,11},{16,20},{18,... | collective-permute-start | bytes 3538952 | tf_op jit(solution)/shard_map/ppermute | solution.py:26
  93.6 4.7 %collective-permute-start.17 = (f32[384,768]{1,0:T(8,128)S(1)}, f32[384,768]{1,0:T(8,128)S(1)}, u32[]{:S(2)}, u32[]{:S(2)}) collective-permute-start(f32[384,768]{1,0:T(8,128)S(1)} %collective-permute-done.10.refs_3_), channel_id=1, source_target_pairs={{1,5},{3,7},{4,0},{6,2},{9,13},{11,15},{12,8},{14,10},{17,21},{19,... | collective-permute-start | bytes 3538952 | tf_op jit(solution)/shard_map/ppermute | solution.py:26
  102.0 1.2 %collective-permute-start.19 = (f32[1,1792]{1,0:T(1,128)S(1)}, f32[1,1792]{1,0:T(1,128)S(1)}, u32[]{:S(2)}, u32[]{:S(2)}) collective-permute-start(f32[1,1792]{1,0:T(1,128)S(1)} %shard_map.90), channel_id=1, source_target_pairs={{0,4},{1,5},{2,6},{3,7},{4,0},{5,1},{6,2},{7,3},{8,12},{9,13},{10,... | collective-permute-start | bytes 21512 | tf_op jit(solution)/shard_map/ppermute | solution.py:26
  103.3 3.7 %collective-permute-start.20 = (f32[1,1792]{1,0:T(1,128)S(1)}, f32[1,1792]{1,0:T(1,128)S(1)}, u32[]{:S(2)}, u32[]{:S(2)}) collective-permute-start(f32[1,1792]{1,0:T(1,128)S(1)} %add.3.refs_0_), channel_id=1, source_target_pairs={{0,2},{1,3},{2,0},{3,1},{4,6},{5,7},{6,4},{7,5},{8,10},{9,11},{10,... | collective-permute-start | bytes 21512 | tf_op jit(solution)/shard_map/ppermute | solution.py:26
  103.6 3.6 %collective-permute-start.21 = (f32[1,1792]{1,0:T(1,128)S(1)}, f32[1,1792]{1,0:T(1,128)S(1)}, u32[]{:S(2)}, u32[]{:S(2)}) collective-permute-start(f32[1,1792]{1,0:T(1,128)S(1)} %add.3.refs_0_), channel_id=1, source_target_pairs={{0,1},{1,0},{2,3},{3,2},{4,5},{5,4},{6,7},{7,6},{8,9},{9,8},{10,11... | collective-permute-start | bytes 21512 | tf_op jit(solution)/shard_map/ppermute | solution.py:26
  103.8 4.7 %collective-permute-start.22 = (f32[1,1792]{1,0:T(1,128)S(1)}, f32[1,1792]{1,0:T(1,128)S(1)}, u32[]{:S(2)}, u32[]{:S(2)}) collective-permute-start(f32[1,1792]{1,0:T(1,128)S(1)} %add.3.refs_0_), channel_id=1, source_target_pairs={{0,3},{1,2},{2,1},{3,0},{4,7},{5,6},{6,5},{7,4},{8,11},{9,10},{10,... | collective-permute-start | bytes 21512 | tf_op jit(solution)/shard_map/ppermute | solution.py:26

commit v4 on v2

--- a/solution.py
+++ b/solution.py
@@ -132,7 +132,7 @@
 
 
 def diagonal_kernel(pieces, index, factor, *refs):
-    diag_high, diag_low, pick_high, pick_low, weights, parent_sum = refs[2 * pieces - 2 :]
+    diag_high, diag_low, pick_high, weights, parent_sum = refs[2 * pieces - 2 :]
     _, block = place_of()
     own_rows, size = refs[0].shape
     parent_sum[...] = column_sum(refs[0][...] * refs[0][...])
@@ -150,13 +150,12 @@
         for mask in range(pieces):
             pick = picks(index[kid, mask : mask + 1, :], 0, size)
             pick_high[kid, mask] = rounded(dot(diag_high[...], pick))
-            pick_low[kid, mask] = rounded(dot(diag_low[...], pick))
     factor_halves = halves(factor[...])
     for span in spans(size):
         weights[:, span] = product(factor_halves, (diag_high[:, span], diag_low[:, span]))
 
 
-def kid_kernel(pieces, index, pick_high, pick_low, factor, *refs):
+def kid_kernel(pieces, index, pick_high, factor, *refs):
     kids = refs[:pieces]
     reduced, lift_high, lower_high, kid_sum, inv_high, inv_low, lifted, lower = refs[pieces:]
     _, block = place_of()
@@ -174,7 +173,7 @@
         inverse = inv_high[...], inv_low[...]
         for mask in range(pieces):
             high, low = halves(product(halves(kids[mask][kid, :kid_block]), inverse))
-            lifted_part = dot(pick_high[kid, mask], high) + dot(pick_low[kid, mask], high)
+            lifted_part = dot(pick_high[kid, mask], high)
             places = index[kid, mask : mask + 1, :]
             low_part = dot(picks(places, size + block * own_border, own_border), low)
             part = dot(picks(places, size, border_size), high)
@@ -314,12 +313,11 @@
     own_factor = cross(after(factor, own_kids))
     diagonal_parts = gathered(own_diagonal, keep_diagonal, swap_diagonal, [own_kids], [own_kids], [own_kids])
 
-    diag_high, diag_low, pick_high, pick_low, weights, parent_sum = call(
+    diag_high, diag_low, pick_high, weights, parent_sum = call(
         functools.partial(diagonal_kernel, pieces),
         (
             shape_of((size, size), half),
             shape_of((size, size), half),
-            shape_of((2, pieces, size, kid_block), half),
             shape_of((2, pieces, size, kid_block), half),
             shape_of((own_border, size)),
             shape_of((1, size)),
@@ -346,7 +344,7 @@
             pltpu.VMEM((size, kid_size), jnp.float32),
             pltpu.VMEM((border_size, kid_size), jnp.float32),
         ],
-    )(index, pick_high, pick_low, own_factor, *kid_parts)
+    )(index, pick_high, own_factor, *kid_parts)
 
     border_high, border_lower = call(
         border_kernel, (shape_of(border.shape, half), shape_of((2, own_border, kid_size))), 8

time: 104 us -> 102 us (0.981)
  Pallas kernels: 28.7 us -> 24.5 us
  waiting for transfers between devices: 27.4 us -> 29.9 us
    pallas_call x6, Pallas kernels: 28.7 us -> 24.5 us  [run(): pl.pallas_call(kernel, out_shape=results, in_specs=specs, out_specs=jax.t...]
    ppermute x19, waiting for transfers between devices: 27.4 us -> 29.9 us  [exchange(): return lax.ppermute(value, ('leaf', 'front'), pairs)]
  transfers between devices with their start and end apart: 23 -> 23, of which waited for: 9 -> 9; matrix products, arithmetic and copies ran while one was open for 0% -> 0% of each run, Pallas kernels for 23% -> 19%
where the time goes in v4:
time: 102 us
  starting transfers between devices  46.7 us (46%)
  waiting for transfers between devices  29.9 us (29%)
  Pallas kernels  24.5 us (24%)
    ppermute x19, starting transfers between devices, exchange(): return lax.ppermute(value, ('leaf', 'front'), pairs)  41.4 us
    ppermute x19, waiting for transfers between devices, exchange(): return lax.ppermute(value, ('leaf', 'front'), pairs)  29.9 us
    pallas_call x6, Pallas kernels, run(): pl.pallas_call(kernel, out_shape=results, in_specs=specs, out_specs=jax.t...  24.5 us
    ppermute x4, starting transfers between devices, cross(): return lax.ppermute(value, ('leaf', 'front'), pairs)  5.34 us
  transfers between devices with their start and end apart: 23, of which 9 were waited for; matrix products, arithmetic and copies ran while one was open for 0% of the time, Pallas kernels for 19%

profile of v4, /device:TPU:0, one launch (start us, length us, event | category | flops | bytes accessed | tf_op | source)
XLA Modules:
  0.0 102.1 jit_solution(4786497979175582811)
XLA Ops:
  0.6 4.9 %collective-permute-start.4 = (f32[384,768]{1,0:T(8,128)}, f32[384,768]{1,0:T(8,128)S(1)}, u32[]{:S(2)}, u32[]{:S(2)}) collective-permute-start(f32[384,768]{1,0:T(8,128)} %bitcast.4), channel_id=1, source_target_pairs={{0,2},{2,0},{5,7},{7,5},{8,10},{10,8},{13,15},{15,13},{16,18},{18,... | collective-permute-start | bytes 3538952 | tf_op jit(solution)/shard_map/ppermute | solution.py:26
  5.5 0.1 collective-permute-start
  5.6 0.0 copy-start
  5.6 1.9 %collective-permute-start.2 = (f32[192,768]{1,0:T(8,128)}, f32[192,768]{1,0:T(8,128)S(1)}, u32[]{:S(2)}, u32[]{:S(2)}) collective-permute-start(f32[192,768]{1,0:T(8,128)} %bitcast.6), channel_id=1, source_target_pairs={{0,0},{1,4},{2,2},{3,6},{4,1},{5,5},{6,3},{7,7},{8,8},{9,12},{10,1... | collective-permute-start | bytes 1769480 | tf_op jit(solution)/shard_map/ppermute | solution.py:36
  7.5 1.9 %collective-permute-start.3 = (f32[192,768]{1,0:T(8,128)}, f32[192,768]{1,0:T(8,128)S(1)}, u32[]{:S(2)}, u32[]{:S(2)}) collective-permute-start(f32[192,768]{1,0:T(8,128)} %bitcast.7), channel_id=1, source_target_pairs={{0,2},{2,0},{5,7},{7,5},{8,10},{10,8},{13,15},{15,13},{16,18},{18,... | collective-permute-start | bytes 1769480 | tf_op jit(solution)/shard_map/ppermute | solution.py:26
  9.4 0.2 collective-permute-start.1
  9.6 2.0 %collective-permute-done.1.other_inverse = f32[2,128,512]{2,1,0:T(8,128)S(1)} collective-permute-done((f32[2,128,512]{2,1,0:T(8,128)}, f32[2,128,512]{2,1,0:T(8,128)S(1)}, u32[]{:S(2)}, u32[]{:S(2)}) %collective-permute-start.1) | collective-permute-done | bytes 524320 | tf_op jit(solution)/shard_map/ppermute | solution.py:26
  11.6 0.0 collective-permute-done.other_rows
  11.6 1.6 %shard_map.86 = (f32[2,384,512]{2,1,0:T(8,128)S(1)}, s32[2,4,256]{2,1,0:T(4,128)S(1)}) custom-call(s32[16]{0:T(128)} %parent_ref.3, s32[16,1024]{1,0:T(8,128)} %index_ref.1, f32[2,256,512]{2,1,0:T(8,128)} %own_rows.1, f32[2,128,512]{2,1,0:T(8,128)} %own_inverse.1, f32[2,256,512]{2,1,0:T(8,128)S(1)} %collective-permute-done.other_rows, ...), custom_call_target="tpu_custom_call" | custom-call | bytes 1000 | tf_op jit(solution)/shard_map/pallas_call | solution.py:259
  13.1 0.0 collective-permute-done.2.refs_0_
  13.1 15.7 %collective-permute-done.3.refs_2_ = f32[192,768]{1,0:T(8,128)S(1)} collective-permute-done((f32[192,768]{1,0:T(8,128)}, f32[192,768]{1,0:T(8,128)S(1)}, u32[]{:S(2)}, u32[]{:S(2)}) %collective-permute-start.3) | collective-permute-done | bytes 589856 | tf_op jit(solution)/shard_map/ppermute | solution.py:26
  28.8 0.0 collective-permute-done.4.refs_2_
  28.8 0.8 collective-permute-start.5
  29.6 0.7 collective-permute-start.7
  30.3 0.0 collective-permute-done.7.refs_3_
  30.3 0.0 collective-permute-done.5.refs_0_
  30.3 2.4 %collective-permute-start.8 = (f32[2,384,512]{2,1,0:T(8,128)S(1)}, f32[2,384,512]{2,1,0:T(8,128)S(1)}, u32[]{:S(2)}, u32[]{:S(2)}) collective-permute-start(f32[2,384,512]{2,1,0:T(8,128)S(1)} %collective-permute-done.5.refs_0_), channel_id=1, source_target_pairs={{0,2},{1,3},{2,0},{3,1},{4,6},{5,7},{6,4},{7,5},{8,10},{9,11},{10,... | collective-permute-start | bytes 4718600 | tf_op jit(solution)/shard_map/ppermute | solution.py:26
  32.8 1.3 %collective-permute-start.12 = (f32[192,768]{1,0:T(8,128)S(1)}, f32[192,768]{1,0:T(8,128)S(1)}, u32[]{:S(2)}, u32[]{:S(2)}) collective-permute-start(f32[192,768]{1,0:T(8,128)S(1)} %collective-permute-done.7.refs_3_), channel_id=1, source_target_pairs={{1,5},{3,7},{4,0},{6,2},{9,13},{11,15},{12,8},{14,10},{17,21},{19,... | collective-permute-start | bytes 1769480 | tf_op jit(solution)/shard_map/ppermute | solution.py:26
  34.0 1.9 %collective-permute-start.6 = (f32[384,768]{1,0:T(8,128)}, f32[384,768]{1,0:T(8,128)S(1)}, u32[]{:S(2)}, u32[]{:S(2)}) collective-permute-start(f32[384,768]{1,0:T(8,128)} %bitcast.5), channel_id=1, source_target_pairs={{0,0},{1,4},{2,2},{3,6},{4,1},{5,5},{6,3},{7,7},{8,8},{9,12},{10,1... | collective-permute-start | bytes 3538952 | tf_op jit(solution)/shard_map/ppermute | solution.py:36
  36.0 0.0 copy-done
  36.0 0.8 collective-permute-start.16
  36.8 10.1 %collective-permute-start.11 = (f32[192,768]{1,0:T(8,128)S(1)}, f32[192,768]{1,0:T(8,128)S(1)}, u32[]{:S(2)}, u32[]{:S(2)}) collective-permute-start(f32[192,768]{1,0:T(8,128)S(1)} %collective-permute-done.2.refs_0_), channel_id=1, source_target_pairs={{0,4},{1,5},{2,6},{3,7},{4,0},{5,1},{6,2},{7,3},{8,12},{9,13},{10,... | collective-permute-start | bytes 1769480 | tf_op jit(solution)/shard_map/ppermute | solution.py:26
  46.9 0.0 collective-permute-done.12.refs_4_
  46.9 2.0 %collective-permute-start.13 = (f32[192,768]{1,0:T(8,128)S(1)}, f32[192,768]{1,0:T(8,128)S(1)}, u32[]{:S(2)}, u32[]{:S(2)}) collective-permute-start(f32[192,768]{1,0:T(8,128)S(1)} %collective-permute-done.3.refs_2_), channel_id=1, source_target_pairs={{0,4},{2,6},{5,1},{7,3},{8,12},{10,14},{13,9},{15,11},{16,20},{18,... | collective-permute-start | bytes 1769480 | tf_op jit(solution)/shard_map/ppermute | solution.py:26
  48.9 0.0 collective-permute-done.11.refs_1_
  48.9 0.1 collective-permute-start.14
  49.0 1.5 %collective-permute-done.13.refs_5_ = f32[192,768]{1,0:T(8,128)S(1)} collective-permute-done((f32[192,768]{1,0:T(8,128)S(1)}, f32[192,768]{1,0:T(8,128)S(1)}, u32[]{:S(2)}, u32[]{:S(2)}) %collective-permute-start.13) | collective-permute-done | bytes 589856 | tf_op jit(solution)/shard_map/ppermute | solution.py:26
  50.5 0.0 collective-permute-done.6.factor.refs_0_
  50.5 4.5 %shard_map.87 = (bf16[768,768]{1,0:T(8,128)(2,1)S(1)}, bf16[768,768]{1,0:T(8,128)(2,1)S(1)}, bf16[2,4,768,256]{3,2,1,0:T(8,128)(2,1)S(1)}, f32[384,768]{1,0:T(8,128)S(1)}, f32[1,768]{1,0:T(1,128)S(1)}) custom-call(s32[2,4,256]{2,1,0:T(4,128)S(1)} %get-tuple-element.32.index, f32[384,768]{1,0:T(8,128)S(1)} %collective-permute-done.6.factor.refs_0_, ...), custom_call_target="tpu_custom_call" | custom-call | bytes 1000 | tf_op jit(solution)/shard_map/pallas_call | solution.py:259
  55.0 6.0 %collective-permute-done.8.refs_2_ = f32[2,384,512]{2,1,0:T(8,128)S(1)} collective-permute-done((f32[2,384,512]{2,1,0:T(8,128)S(1)}, f32[2,384,512]{2,1,0:T(8,128)S(1)}, u32[]{:S(2)}, u32[]{:S(2)}) %collective-permute-start.8) | collective-permute-done | bytes 1572896 | tf_op jit(solution)/shard_map/ppermute | solution.py:26
  61.0 6.9 %collective-permute-start.15 = (f32[2,384,512]{2,1,0:T(8,128)S(1)}, f32[2,384,512]{2,1,0:T(8,128)S(1)}, u32[]{:S(2)}, u32[]{:S(2)}) collective-permute-start(f32[2,384,512]{2,1,0:T(8,128)S(1)} %collective-permute-done.8.refs_2_), channel_id=1, source_target_pairs={{0,4},{1,5},{2,6},{3,7},{4,0},{5,1},{6,2},{7,3},{8,12},{9,13},{10,... | collective-permute-start | bytes 4718600 | tf_op jit(solution)/shard_map/ppermute | solution.py:26
  67.8 0.7 collective-permute-start.10
  68.6 3.0 %collective-permute-start.9 = (f32[384,768]{1,0:T(8,128)S(1)}, f32[384,768]{1,0:T(8,128)S(1)}, u32[]{:S(2)}, u32[]{:S(2)}) collective-permute-start(f32[384,768]{1,0:T(8,128)S(1)} %collective-permute-done.6.factor.refs_0_), channel_id=1, source_target_pairs={{0,4},{1,5},{2,6},{3,7},{4,0},{5,1},{6,2},{7,3},{8,12},{9,13},{10,... | collective-permute-start | bytes 3538952 | tf_op jit(solution)/shard_map/ppermute | solution.py:26
  71.5 0.0 collective-permute-done.14.refs_1_
  71.5 2.2 %collective-permute-start.18 = (f32[384,768]{1,0:T(8,128)S(1)}, f32[384,768]{1,0:T(8,128)S(1)}, u32[]{:S(2)}, u32[]{:S(2)}) collective-permute-start(f32[384,768]{1,0:T(8,128)S(1)} %collective-permute-done.4.refs_2_), channel_id=1, source_target_pairs={{0,4},{2,6},{5,1},{7,3},{8,12},{10,14},{13,9},{15,11},{16,20},{18,... | collective-permute-start | bytes 3538952 | tf_op jit(solution)/shard_map/ppermute | solution.py:26
  73.7 0.0 collective-permute-done.15.refs_3_
  73.7 12.0 %shard_map.88 = (f32[2,384,512]{2,1,0:T(8,128)S(1)}, bf16[2,768,512]{2,1,0:T(8,128)(2,1)S(1)}, bf16[2,1536,512]{2,1,0:T(8,128)(2,1)S(1)}, f32[2,512]{1,0:T(2,128)S(1)}) custom-call(s32[2,4,256]{2,1,0:T(4,128)S(1)} %get-tuple-element.32.index, bf16[2,4,768,256]{3,2,1,0:T(8,128)(2,1)S(1)} %get-tuple-element.36.pick_high, ...), custom_call_target="tpu_custom_call" | custom-call | bytes 1000 | tf_op jit(solution)/shard_map/pallas_call | solution.py:259
  85.8 0.0 collective-permute-done.16.border
  85.8 0.0 collective-permute-done.10.refs_3_
  85.8 1.3 %collective-permute-start.17 = (f32[384,768]{1,0:T(8,128)S(1)}, f32[384,768]{1,0:T(8,128)S(1)}, u32[]{:S(2)}, u32[]{:S(2)}) collective-permute-start(f32[384,768]{1,0:T(8,128)S(1)} %collective-permute-done.10.refs_3_), channel_id=1, source_target_pairs={{1,5},{3,7},{4,0},{6,2},{9,13},{11,15},{12,8},{14,10},{17,21},{19,... | collective-permute-start | bytes 3538952 | tf_op jit(solution)/shard_map/ppermute | solution.py:26
  87.1 1.4 %shard_map.89 = (bf16[384,1536]{1,0:T(8,128)(2,1)S(1)}, f32[2,384,512]{2,1,0:T(8,128)S(1)}) custom-call(f32[384,1536]{1,0:T(8,128)S(1)} %collective-permute-done.16.border, bf16[2,1536,512]{2,1,0:T(8,128)(2,1)S(1)} %get-tuple-element.43.lower_high), custom_call_target="tpu_custom_call" | custom-call | bytes 1000 | tf_op jit(solution)/shard_map/pallas_call | solution.py:259
  88.5 0.0 collective-permute-done.9.refs_1_
  88.5 0.0 collective-permute-done.18.refs_5_
  88.5 2.0 %collective-permute-done.17.refs_4_ = f32[384,768]{1,0:T(8,128)S(1)} collective-permute-done((f32[384,768]{1,0:T(8,128)S(1)}, f32[384,768]{1,0:T(8,128)S(1)}, u32[]{:S(2)}, u32[]{:S(2)}) %collective-permute-start.17) | collective-permute-done | bytes 1179680 | tf_op jit(solution)/shard_map/ppermute | solution.py:26
  90.5 3.7 %shard_map.90 = f32[1,1792]{1,0:T(1,128)S(1)} custom-call(f32[384,768]{1,0:T(8,128)S(1)} %collective-permute-done.6.factor.refs_0_, f32[384,768]{1,0:T(8,128)S(1)} %collective-permute-done.9.refs_1_, f32[384,768]{1,0:T(8,128)S(1)} %collective-permute-done.4.refs_2_, f32[384,768]{1,0:T(8,128)S(1)} %collective-permute-done.10.refs_3_, ...), custom_call_target="tpu_custom_call" | custom-call | bytes 1000 | tf_op jit(solution)/shard_map/pallas_call | solution.py:259
  94.2 0.2 collective-permute-start.19
  94.4 1.0 %collective-permute-done.19 = f32[1,1792]{1,0:T(1,128)S(1)} collective-permute-done((f32[1,1792]{1,0:T(1,128)S(1)}, f32[1,1792]{1,0:T(1,128)S(1)}, u32[]{:S(2)}, u32[]{:S(2)}) %collective-permute-start.19) | collective-permute-done | bytes 7200 | tf_op jit(solution)/shard_map/ppermute | solution.py:26
  95.5 0.4 collective-permute-start.20
  95.9 0.0 collective-permute-start.21
  95.9 3.2 %collective-permute-start.22 = (f32[1,1792]{1,0:T(1,128)S(1)}, f32[1,1792]{1,0:T(1,128)S(1)}, u32[]{:S(2)}, u32[]{:S(2)}) collective-permute-start(f32[1,1792]{1,0:T(1,128)S(1)} %add.3.refs_0_), channel_id=1, source_target_pairs={{0,3},{1,2},{2,1},{3,0},{4,7},{5,6},{6,5},{7,4},{8,11},{9,10},{10,... | collective-permute-start | bytes 21512 | tf_op jit(solution)/shard_map/ppermute | solution.py:26
  99.1 0.2 collective-permute-done.20.refs_1_
  99.2 0.3 collective-permute-done.21.refs_2_
  99.5 1.2 %collective-permute-done.22.refs_3_ = f32[1,1792]{1,0:T(1,128)S(1)} collective-permute-done((f32[1,1792]{1,0:T(1,128)S(1)}, f32[1,1792]{1,0:T(1,128)S(1)}, u32[]{:S(2)}, u32[]{:S(2)}) %collective-permute-start.22) | collective-permute-done | bytes 7200 | tf_op jit(solution)/shard_map/ppermute | solution.py:26
  100.7 1.3 %shard_map.91 = (f32[1,768]{1,0:T(1,128)}, f32[2,512]{1,0:T(2,128)}) custom-call(s32[16]{0:T(128)} %parent_ref.3, f32[1,1792]{1,0:T(1,128)S(1)} %add.3.refs_0_, f32[1,1792]{1,0:T(1,128)S(1)} %collective-permute-done.20.refs_1_, f32[1,1792]{1,0:T(1,128)S(1)} %collective-permute-done.21.refs_2_, f32[1,1792]{1,0:T(1,128)S(1)} %collective-permute-done.22.refs_3_), custom_call_target="tpu_custom_call" | custom-call | bytes 1000 | tf_op jit(solution)/shard_map/pallas_call | solution.py:259
  (1 shorter events, 0.0 us)
Async XLA Ops:
  0.6 28.2 %collective-permute-start.4 = (f32[384,768]{1,0:T(8,128)}, f32[384,768]{1,0:T(8,128)S(1)}, u32[]{:S(2)}, u32[]{:S(2)}) collective-permute-start(f32[384,768]{1,0:T(8,128)} %bitcast.4), channel_id=1, source_target_pairs={{0,2},{2,0},{5,7},{7,5},{8,10},{10,8},{13,15},{15,13},{16,18},{18,... | collective-permute-start | bytes 3538952 | tf_op jit(solution)/shard_map/ppermute | solution.py:26
  5.5 6.0 %collective-permute-start = (f32[2,256,512]{2,1,0:T(8,128)}, f32[2,256,512]{2,1,0:T(8,128)S(1)}, u32[]{:S(2)}, u32[]{:S(2)}) collective-permute-start(f32[2,256,512]{2,1,0:T(8,128)} %own_rows.1), channel_id=1, source_target_pairs={{0,4},{1,5},{2,6},{3,7},{4,0},{5,1},{6,2},{7,3},{8,12},{9,13},{10,... | collective-permute-start | bytes 3145736 | tf_op jit(solution)/shard_map/ppermute | solution.py:26
  5.6 30.4 %copy-start = (f32[1,384,1536]{2,1,0:T(8,128)S(1)}, f32[1,384,1536]{2,1,0:T(8,128)}, u32[]{:S(2)}) copy-start(f32[1,384,1536]{2,1,0:T(8,128)} %param.7) | copy-start | bytes 7077892
  5.6 7.5 %collective-permute-start.2 = (f32[192,768]{1,0:T(8,128)}, f32[192,768]{1,0:T(8,128)S(1)}, u32[]{:S(2)}, u32[]{:S(2)}) collective-permute-start(f32[192,768]{1,0:T(8,128)} %bitcast.6), channel_id=1, source_target_pairs={{0,0},{1,4},{2,2},{3,6},{4,1},{5,5},{6,3},{7,7},{8,8},{9,12},{10,1... | collective-permute-start | bytes 1769480 | tf_op jit(solution)/shard_map/ppermute | solution.py:36
  7.5 21.4 %collective-permute-start.3 = (f32[192,768]{1,0:T(8,128)}, f32[192,768]{1,0:T(8,128)S(1)}, u32[]{:S(2)}, u32[]{:S(2)}) collective-permute-start(f32[192,768]{1,0:T(8,128)} %bitcast.7), channel_id=1, source_target_pairs={{0,2},{2,0},{5,7},{7,5},{8,10},{10,8},{13,15},{15,13},{16,18},{18,... | collective-permute-start | bytes 1769480 | tf_op jit(solution)/shard_map/ppermute | solution.py:26
  9.4 2.2 %collective-permute-start.1 = (f32[2,128,512]{2,1,0:T(8,128)}, f32[2,128,512]{2,1,0:T(8,128)S(1)}, u32[]{:S(2)}, u32[]{:S(2)}) collective-permute-start(f32[2,128,512]{2,1,0:T(8,128)} %own_inverse.1), channel_id=1, source_target_pairs={{0,4},{1,5},{2,6},{3,7},{4,0},{5,1},{6,2},{7,3},{8,12},{9,13},{10,... | collective-permute-start | bytes 1572872 | tf_op jit(solution)/shard_map/ppermute | solution.py:26
  28.8 1.5 %collective-permute-start.5 = (f32[2,384,512]{2,1,0:T(8,128)S(1)}, f32[2,384,512]{2,1,0:T(8,128)S(1)}, u32[]{:S(2)}, u32[]{:S(2)}) collective-permute-start(f32[2,384,512]{2,1,0:T(8,128)S(1)} %get-tuple-element.28), channel_id=1, source_target_pairs={{0,0},{1,4},{2,2},{3,6},{4,1},{5,5},{6,3},{7,7},{8,8},{9,12},{10,1... | collective-permute-start | bytes 4718600 | tf_op jit(solution)/shard_map/ppermute | solution.py:36
  29.6 0.7 collective-permute-start.7
  30.3 30.7 %collective-permute-start.8 = (f32[2,384,512]{2,1,0:T(8,128)S(1)}, f32[2,384,512]{2,1,0:T(8,128)S(1)}, u32[]{:S(2)}, u32[]{:S(2)}) collective-permute-start(f32[2,384,512]{2,1,0:T(8,128)S(1)} %collective-permute-done.5.refs_0_), channel_id=1, source_target_pairs={{0,2},{1,3},{2,0},{3,1},{4,6},{5,7},{6,4},{7,5},{8,10},{9,11},{10,... | collective-permute-start | bytes 4718600 | tf_op jit(solution)/shard_map/ppermute | solution.py:26
  32.8 14.2 %collective-permute-start.12 = (f32[192,768]{1,0:T(8,128)S(1)}, f32[192,768]{1,0:T(8,128)S(1)}, u32[]{:S(2)}, u32[]{:S(2)}) collective-permute-start(f32[192,768]{1,0:T(8,128)S(1)} %collective-permute-done.7.refs_3_), channel_id=1, source_target_pairs={{1,5},{3,7},{4,0},{6,2},{9,13},{11,15},{12,8},{14,10},{17,21},{19,... | collective-permute-start | bytes 1769480 | tf_op jit(solution)/shard_map/ppermute | solution.py:26
  34.0 16.4 %collective-permute-start.6 = (f32[384,768]{1,0:T(8,128)}, f32[384,768]{1,0:T(8,128)S(1)}, u32[]{:S(2)}, u32[]{:S(2)}) collective-permute-start(f32[384,768]{1,0:T(8,128)} %bitcast.5), channel_id=1, source_target_pairs={{0,0},{1,4},{2,2},{3,6},{4,1},{5,5},{6,3},{7,7},{8,8},{9,12},{10,1... | collective-permute-start | bytes 3538952 | tf_op jit(solution)/shard_map/ppermute | solution.py:36
  36.0 49.8 %collective-permute-start.16 = (f32[384,1536]{1,0:T(8,128)S(1)}, f32[384,1536]{1,0:T(8,128)S(1)}, u32[]{:S(2)}, u32[]{:S(2)}) collective-permute-start(f32[384,1536]{1,0:T(8,128)S(1)} %bitcast.3), channel_id=1, source_target_pairs={{0,0},{1,4},{2,2},{3,6},{4,1},{5,5},{6,3},{7,7},{8,8},{9,12},{10,1... | collective-permute-start | bytes 7077896 | tf_op jit(solution)/shard_map/ppermute | solution.py:36
  36.8 12.1 %collective-permute-start.11 = (f32[192,768]{1,0:T(8,128)S(1)}, f32[192,768]{1,0:T(8,128)S(1)}, u32[]{:S(2)}, u32[]{:S(2)}) collective-permute-start(f32[192,768]{1,0:T(8,128)S(1)} %collective-permute-done.2.refs_0_), channel_id=1, source_target_pairs={{0,4},{1,5},{2,6},{3,7},{4,0},{5,1},{6,2},{7,3},{8,12},{9,13},{10,... | collective-permute-start | bytes 1769480 | tf_op jit(solution)/shard_map/ppermute | solution.py:26
  46.9 3.5 %collective-permute-start.13 = (f32[192,768]{1,0:T(8,128)S(1)}, f32[192,768]{1,0:T(8,128)S(1)}, u32[]{:S(2)}, u32[]{:S(2)}) collective-permute-start(f32[192,768]{1,0:T(8,128)S(1)} %collective-permute-done.3.refs_2_), channel_id=1, source_target_pairs={{0,4},{2,6},{5,1},{7,3},{8,12},{10,14},{13,9},{15,11},{16,20},{18,... | collective-permute-start | bytes 1769480 | tf_op jit(solution)/shard_map/ppermute | solution.py:26
  48.9 22.6 %collective-permute-start.14 = (f32[2,384,512]{2,1,0:T(8,128)S(1)}, f32[2,384,512]{2,1,0:T(8,128)S(1)}, u32[]{:S(2)}, u32[]{:S(2)}) collective-permute-start(f32[2,384,512]{2,1,0:T(8,128)S(1)} %collective-permute-done.5.refs_0_), channel_id=1, source_target_pairs={{0,4},{1,5},{2,6},{3,7},{4,0},{5,1},{6,2},{7,3},{8,12},{9,13},{10,... | collective-permute-start | bytes 4718600 | tf_op jit(solution)/shard_map/ppermute | solution.py:26
  61.0 12.8 %collective-permute-start.15 = (f32[2,384,512]{2,1,0:T(8,128)S(1)}, f32[2,384,512]{2,1,0:T(8,128)S(1)}, u32[]{:S(2)}, u32[]{:S(2)}) collective-permute-start(f32[2,384,512]{2,1,0:T(8,128)S(1)} %collective-permute-done.8.refs_2_), channel_id=1, source_target_pairs={{0,4},{1,5},{2,6},{3,7},{4,0},{5,1},{6,2},{7,3},{8,12},{9,13},{10,... | collective-permute-start | bytes 4718600 | tf_op jit(solution)/shard_map/ppermute | solution.py:26
  67.8 17.9 %collective-permute-start.10 = (f32[384,768]{1,0:T(8,128)S(1)}, f32[384,768]{1,0:T(8,128)S(1)}, u32[]{:S(2)}, u32[]{:S(2)}) collective-permute-start(f32[384,768]{1,0:T(8,128)S(1)} %collective-permute-done.6.factor.refs_0_), channel_id=1, source_target_pairs={{1,3},{3,1},{4,6},{6,4},{9,11},{11,9},{12,14},{14,12},{17,19},{19,... | collective-permute-start | bytes 3538952 | tf_op jit(solution)/shard_map/ppermute | solution.py:26
  68.6 19.9 %collective-permute-start.9 = (f32[384,768]{1,0:T(8,128)S(1)}, f32[384,768]{1,0:T(8,128)S(1)}, u32[]{:S(2)}, u32[]{:S(2)}) collective-permute-start(f32[384,768]{1,0:T(8,128)S(1)} %collective-permute-done.6.factor.refs_0_), channel_id=1, source_target_pairs={{0,4},{1,5},{2,6},{3,7},{4,0},{5,1},{6,2},{7,3},{8,12},{9,13},{10,... | collective-permute-start | bytes 3538952 | tf_op jit(solution)/shard_map/ppermute | solution.py:26
  71.5 17.0 %collective-permute-start.18 = (f32[384,768]{1,0:T(8,128)S(1)}, f32[384,768]{1,0:T(8,128)S(1)}, u32[]{:S(2)}, u32[]{:S(2)}) collective-permute-start(f32[384,768]{1,0:T(8,128)S(1)} %collective-permute-done.4.refs_2_), channel_id=1, source_target_pairs={{0,4},{2,6},{5,1},{7,3},{8,12},{10,14},{13,9},{15,11},{16,20},{18,... | collective-permute-start | bytes 3538952 | tf_op jit(solution)/shard_map/ppermute | solution.py:26
  85.8 4.7 %collective-permute-start.17 = (f32[384,768]{1,0:T(8,128)S(1)}, f32[384,768]{1,0:T(8,128)S(1)}, u32[]{:S(2)}, u32[]{:S(2)}) collective-permute-start(f32[384,768]{1,0:T(8,128)S(1)} %collective-permute-done.10.refs_3_), channel_id=1, source_target_pairs={{1,5},{3,7},{4,0},{6,2},{9,13},{11,15},{12,8},{14,10},{17,21},{19,... | collective-permute-start | bytes 3538952 | tf_op jit(solution)/shard_map/ppermute | solution.py:26
  94.2 1.2 %collective-permute-start.19 = (f32[1,1792]{1,0:T(1,128)S(1)}, f32[1,1792]{1,0:T(1,128)S(1)}, u32[]{:S(2)}, u32[]{:S(2)}) collective-permute-start(f32[1,1792]{1,0:T(1,128)S(1)} %shard_map.90), channel_id=1, source_target_pairs={{0,4},{1,5},{2,6},{3,7},{4,0},{5,1},{6,2},{7,3},{8,12},{9,13},{10,... | collective-permute-start | bytes 21512 | tf_op jit(solution)/shard_map/ppermute | solution.py:26
  95.5 3.7 %collective-permute-start.20 = (f32[1,1792]{1,0:T(1,128)S(1)}, f32[1,1792]{1,0:T(1,128)S(1)}, u32[]{:S(2)}, u32[]{:S(2)}) collective-permute-start(f32[1,1792]{1,0:T(1,128)S(1)} %add.3.refs_0_), channel_id=1, source_target_pairs={{0,2},{1,3},{2,0},{3,1},{4,6},{5,7},{6,4},{7,5},{8,10},{9,11},{10,... | collective-permute-start | bytes 21512 | tf_op jit(solution)/shard_map/ppermute | solution.py:26
  95.9 3.6 %collective-permute-start.21 = (f32[1,1792]{1,0:T(1,128)S(1)}, f32[1,1792]{1,0:T(1,128)S(1)}, u32[]{:S(2)}, u32[]{:S(2)}) collective-permute-start(f32[1,1792]{1,0:T(1,128)S(1)} %add.3.refs_0_), channel_id=1, source_target_pairs={{0,1},{1,0},{2,3},{3,2},{4,5},{5,4},{6,7},{7,6},{8,9},{9,8},{10,11... | collective-permute-start | bytes 21512 | tf_op jit(solution)/shard_map/ppermute | solution.py:26
  95.9 4.9 %collective-permute-start.22 = (f32[1,1792]{1,0:T(1,128)S(1)}, f32[1,1792]{1,0:T(1,128)S(1)}, u32[]{:S(2)}, u32[]{:S(2)}) collective-permute-start(f32[1,1792]{1,0:T(1,128)S(1)} %add.3.refs_0_), channel_id=1, source_target_pairs={{0,3},{1,2},{2,1},{3,0},{4,7},{5,6},{6,5},{7,4},{8,11},{9,10},{10,... | collective-permute-start | bytes 21512 | tf_op jit(solution)/shard_map/ppermute | solution.py:26

commit v5 on v4

--- a/solution.py
+++ b/solution.py
@@ -171,15 +171,21 @@
             inv_high[pl.ds(start, inv_block), :] = high
             inv_low[pl.ds(start, inv_block), :] = low
         inverse = inv_high[...], inv_low[...]
-        for mask in range(pieces):
-            high, low = halves(product(halves(kids[mask][kid, :kid_block]), inverse))
-            lifted_part = dot(pick_high[kid, mask], high)
-            places = index[kid, mask : mask + 1, :]
+        parts = [halves(product(halves(kids[mask][kid, :kid_block]), inverse)) for mask in range(pieces)]
+        group = pieces if kid_block % 128 == 0 else 1
+        for first in range(0, pieces, group):
+            masks = range(first, first + group)
+            high = jnp.concatenate([parts[mask][0] for mask in masks], axis=0)
+            low = jnp.concatenate([parts[mask][1] for mask in masks], axis=0)
+            pick = jnp.concatenate([pick_high[kid, mask] for mask in masks], axis=1)
+            places = jnp.concatenate([index[kid, mask : mask + 1, :] for mask in masks], axis=1)
+            lifted_part = dot(pick, high)
             low_part = dot(picks(places, size + block * own_border, own_border), low)
-            part = dot(picks(places, size, border_size), high)
-            lifted[...] = lifted_part if mask == 0 else lifted[...] + lifted_part
-            reduced[kid] = low_part if mask == 0 else reduced[kid] + low_part
-            lower[...] = part if mask == 0 else lower[...] + part
+            lifted[...] = lifted_part if first == 0 else lifted[...] + lifted_part
+            reduced[kid] = low_part if first == 0 else reduced[kid] + low_part
+            for start in range(0, border_size, 384):
+                part = dot(picks(places, size + start, 384), high)
+                lower[start : start + 384] = part if first == 0 else lower[start : start + 384] + part
         own = lifted[pl.ds(pl.multiple_of(block * own_rows, 16), own_rows), :]
         kid_sum[kid : kid + 1] = column_sum(own_inverse * own_inverse) + column_sum(own * own)
         lift_high[kid] = rounded(lifted[...])

time: 102 us -> 102 us (level)
  Pallas kernels: 24.5 us -> 23 us
    pallas_call x6, Pallas kernels: 24.5 us -> 23 us  [run(): pl.pallas_call(kernel, out_shape=results, in_specs=specs, out_specs=jax.t...]
  transfers between devices with their start and end apart: 23 -> 23, of which waited for: 9 -> 9; matrix products, arithmetic and copies ran while one was open for 0% -> 0% of each run, Pallas kernels for 19% -> 18%
where the time goes in v5:
time: 102 us; the launch traced here: 101 us
  starting transfers between devices  46.7 us (46%)
  waiting for transfers between devices  30.6 us (30%)
  Pallas kernels  23 us (23%)
    ppermute x19, starting transfers between devices, exchange(): return lax.ppermute(value, ('leaf', 'front'), pairs)  41.4 us
    ppermute x19, waiting for transfers between devices, exchange(): return lax.ppermute(value, ('leaf', 'front'), pairs)  30.6 us
    pallas_call x6, Pallas kernels, run(): pl.pallas_call(kernel, out_shape=results, in_specs=specs, out_specs=jax.t...  23 us
    ppermute x4, starting transfers between devices, cross(): return lax.ppermute(value, ('leaf', 'front'), pairs)  5.34 us
  transfers between devices with their start and end apart: 23, of which 9 were waited for; matrix products, arithmetic and copies ran while one was open for 0% of the time, Pallas kernels for 18%

profile of v5, /device:TPU:0, one launch (start us, length us, event | category | flops | bytes accessed | tf_op | source)
XLA Modules:
  0.0 101.2 jit_solution(5019221649533553513)
XLA Ops:
  0.6 4.9 %collective-permute-start.4 = (f32[384,768]{1,0:T(8,128)}, f32[384,768]{1,0:T(8,128)S(1)}, u32[]{:S(2)}, u32[]{:S(2)}) collective-permute-start(f32[384,768]{1,0:T(8,128)} %bitcast.4), channel_id=1, source_target_pairs={{0,2},{2,0},{5,7},{7,5},{8,10},{10,8},{13,15},{15,13},{16,18},{18,... | collective-permute-start | bytes 3538952 | tf_op jit(solution)/shard_map/ppermute | solution.py:26
  5.5 0.1 collective-permute-start
  5.6 0.0 copy-start
  5.6 1.9 %collective-permute-start.2 = (f32[192,768]{1,0:T(8,128)}, f32[192,768]{1,0:T(8,128)S(1)}, u32[]{:S(2)}, u32[]{:S(2)}) collective-permute-start(f32[192,768]{1,0:T(8,128)} %bitcast.6), channel_id=1, source_target_pairs={{0,0},{1,4},{2,2},{3,6},{4,1},{5,5},{6,3},{7,7},{8,8},{9,12},{10,1... | collective-permute-start | bytes 1769480 | tf_op jit(solution)/shard_map/ppermute | solution.py:36
  7.5 1.9 %collective-permute-start.3 = (f32[192,768]{1,0:T(8,128)}, f32[192,768]{1,0:T(8,128)S(1)}, u32[]{:S(2)}, u32[]{:S(2)}) collective-permute-start(f32[192,768]{1,0:T(8,128)} %bitcast.7), channel_id=1, source_target_pairs={{0,2},{2,0},{5,7},{7,5},{8,10},{10,8},{13,15},{15,13},{16,18},{18,... | collective-permute-start | bytes 1769480 | tf_op jit(solution)/shard_map/ppermute | solution.py:26
  9.4 0.2 collective-permute-start.1
  9.6 2.0 %collective-permute-done.1.other_inverse = f32[2,128,512]{2,1,0:T(8,128)S(1)} collective-permute-done((f32[2,128,512]{2,1,0:T(8,128)}, f32[2,128,512]{2,1,0:T(8,128)S(1)}, u32[]{:S(2)}, u32[]{:S(2)}) %collective-permute-start.1) | collective-permute-done | bytes 524320 | tf_op jit(solution)/shard_map/ppermute | solution.py:26
  11.6 0.0 collective-permute-done.other_rows
  11.6 1.6 %shard_map.86 = (f32[2,384,512]{2,1,0:T(8,128)S(1)}, s32[2,4,256]{2,1,0:T(4,128)S(1)}) custom-call(s32[16]{0:T(128)} %parent_ref.3, s32[16,1024]{1,0:T(8,128)} %index_ref.1, f32[2,256,512]{2,1,0:T(8,128)} %own_rows.1, f32[2,128,512]{2,1,0:T(8,128)} %own_inverse.1, f32[2,256,512]{2,1,0:T(8,128)S(1)} %collective-permute-done.other_rows, ...), custom_call_target="tpu_custom_call" | custom-call | bytes 1000 | tf_op jit(solution)/shard_map/pallas_call | solution.py:265
  13.1 0.0 collective-permute-done.2.refs_0_
  13.1 15.7 %collective-permute-done.3.refs_2_ = f32[192,768]{1,0:T(8,128)S(1)} collective-permute-done((f32[192,768]{1,0:T(8,128)}, f32[192,768]{1,0:T(8,128)S(1)}, u32[]{:S(2)}, u32[]{:S(2)}) %collective-permute-start.3) | collective-permute-done | bytes 589856 | tf_op jit(solution)/shard_map/ppermute | solution.py:26
  28.8 0.0 collective-permute-done.4.refs_2_
  28.8 0.8 collective-permute-start.5
  29.6 0.7 collective-permute-start.7
  30.3 0.0 collective-permute-done.7.refs_3_
  30.3 0.0 collective-permute-done.5.refs_0_
  30.3 2.4 %collective-permute-start.8 = (f32[2,384,512]{2,1,0:T(8,128)S(1)}, f32[2,384,512]{2,1,0:T(8,128)S(1)}, u32[]{:S(2)}, u32[]{:S(2)}) collective-permute-start(f32[2,384,512]{2,1,0:T(8,128)S(1)} %collective-permute-done.5.refs_0_), channel_id=1, source_target_pairs={{0,2},{1,3},{2,0},{3,1},{4,6},{5,7},{6,4},{7,5},{8,10},{9,11},{10,... | collective-permute-start | bytes 4718600 | tf_op jit(solution)/shard_map/ppermute | solution.py:26
  32.8 1.3 %collective-permute-start.12 = (f32[192,768]{1,0:T(8,128)S(1)}, f32[192,768]{1,0:T(8,128)S(1)}, u32[]{:S(2)}, u32[]{:S(2)}) collective-permute-start(f32[192,768]{1,0:T(8,128)S(1)} %collective-permute-done.7.refs_3_), channel_id=1, source_target_pairs={{1,5},{3,7},{4,0},{6,2},{9,13},{11,15},{12,8},{14,10},{17,21},{19,... | collective-permute-start | bytes 1769480 | tf_op jit(solution)/shard_map/ppermute | solution.py:26
  34.0 1.9 %collective-permute-start.6 = (f32[384,768]{1,0:T(8,128)}, f32[384,768]{1,0:T(8,128)S(1)}, u32[]{:S(2)}, u32[]{:S(2)}) collective-permute-start(f32[384,768]{1,0:T(8,128)} %bitcast.5), channel_id=1, source_target_pairs={{0,0},{1,4},{2,2},{3,6},{4,1},{5,5},{6,3},{7,7},{8,8},{9,12},{10,1... | collective-permute-start | bytes 3538952 | tf_op jit(solution)/shard_map/ppermute | solution.py:36
  36.0 0.0 copy-done
  36.0 0.8 collective-permute-start.16
  36.8 10.1 %collective-permute-start.11 = (f32[192,768]{1,0:T(8,128)S(1)}, f32[192,768]{1,0:T(8,128)S(1)}, u32[]{:S(2)}, u32[]{:S(2)}) collective-permute-start(f32[192,768]{1,0:T(8,128)S(1)} %collective-permute-done.2.refs_0_), channel_id=1, source_target_pairs={{0,4},{1,5},{2,6},{3,7},{4,0},{5,1},{6,2},{7,3},{8,12},{9,13},{10,... | collective-permute-start | bytes 1769480 | tf_op jit(solution)/shard_map/ppermute | solution.py:26
  46.9 0.0 collective-permute-done.12.refs_4_
  46.9 2.0 %collective-permute-start.13 = (f32[192,768]{1,0:T(8,128)S(1)}, f32[192,768]{1,0:T(8,128)S(1)}, u32[]{:S(2)}, u32[]{:S(2)}) collective-permute-start(f32[192,768]{1,0:T(8,128)S(1)} %collective-permute-done.3.refs_2_), channel_id=1, source_target_pairs={{0,4},{2,6},{5,1},{7,3},{8,12},{10,14},{13,9},{15,11},{16,20},{18,... | collective-permute-start | bytes 1769480 | tf_op jit(solution)/shard_map/ppermute | solution.py:26
  48.9 0.0 collective-permute-done.11.refs_1_
  48.9 0.1 collective-permute-start.14
  49.0 1.5 %collective-permute-done.13.refs_5_ = f32[192,768]{1,0:T(8,128)S(1)} collective-permute-done((f32[192,768]{1,0:T(8,128)S(1)}, f32[192,768]{1,0:T(8,128)S(1)}, u32[]{:S(2)}, u32[]{:S(2)}) %collective-permute-start.13) | collective-permute-done | bytes 589856 | tf_op jit(solution)/shard_map/ppermute | solution.py:26
  50.5 0.0 collective-permute-done.6.factor.refs_0_
  50.5 4.5 %shard_map.87 = (bf16[768,768]{1,0:T(8,128)(2,1)S(1)}, bf16[768,768]{1,0:T(8,128)(2,1)S(1)}, bf16[2,4,768,256]{3,2,1,0:T(8,128)(2,1)S(1)}, f32[384,768]{1,0:T(8,128)S(1)}, f32[1,768]{1,0:T(1,128)S(1)}) custom-call(s32[2,4,256]{2,1,0:T(4,128)S(1)} %get-tuple-element.32.index, f32[384,768]{1,0:T(8,128)S(1)} %collective-permute-done.6.factor.refs_0_, ...), custom_call_target="tpu_custom_call" | custom-call | bytes 1000 | tf_op jit(solution)/shard_map/pallas_call | solution.py:265
  55.0 6.0 %collective-permute-done.8.refs_2_ = f32[2,384,512]{2,1,0:T(8,128)S(1)} collective-permute-done((f32[2,384,512]{2,1,0:T(8,128)S(1)}, f32[2,384,512]{2,1,0:T(8,128)S(1)}, u32[]{:S(2)}, u32[]{:S(2)}) %collective-permute-start.8) | collective-permute-done | bytes 1572896 | tf_op jit(solution)/shard_map/ppermute | solution.py:26
  61.0 6.9 %collective-permute-start.15 = (f32[2,384,512]{2,1,0:T(8,128)S(1)}, f32[2,384,512]{2,1,0:T(8,128)S(1)}, u32[]{:S(2)}, u32[]{:S(2)}) collective-permute-start(f32[2,384,512]{2,1,0:T(8,128)S(1)} %collective-permute-done.8.refs_2_), channel_id=1, source_target_pairs={{0,4},{1,5},{2,6},{3,7},{4,0},{5,1},{6,2},{7,3},{8,12},{9,13},{10,... | collective-permute-start | bytes 4718600 | tf_op jit(solution)/shard_map/ppermute | solution.py:26
  67.8 0.7 collective-permute-start.10
  68.6 3.0 %collective-permute-start.9 = (f32[384,768]{1,0:T(8,128)S(1)}, f32[384,768]{1,0:T(8,128)S(1)}, u32[]{:S(2)}, u32[]{:S(2)}) collective-permute-start(f32[384,768]{1,0:T(8,128)S(1)} %collective-permute-done.6.factor.refs_0_), channel_id=1, source_target_pairs={{0,4},{1,5},{2,6},{3,7},{4,0},{5,1},{6,2},{7,3},{8,12},{9,13},{10,... | collective-permute-start | bytes 3538952 | tf_op jit(solution)/shard_map/ppermute | solution.py:26
  71.5 0.0 collective-permute-done.14.refs_1_
  71.5 2.2 %collective-permute-start.18 = (f32[384,768]{1,0:T(8,128)S(1)}, f32[384,768]{1,0:T(8,128)S(1)}, u32[]{:S(2)}, u32[]{:S(2)}) collective-permute-start(f32[384,768]{1,0:T(8,128)S(1)} %collective-permute-done.4.refs_2_), channel_id=1, source_target_pairs={{0,4},{2,6},{5,1},{7,3},{8,12},{10,14},{13,9},{15,11},{16,20},{18,... | collective-permute-start | bytes 3538952 | tf_op jit(solution)/shard_map/ppermute | solution.py:26
  73.7 0.0 collective-permute-done.15.refs_3_
  73.7 10.7 %shard_map.88 = (f32[2,384,512]{2,1,0:T(8,128)S(1)}, bf16[2,768,512]{2,1,0:T(8,128)(2,1)S(1)}, bf16[2,1536,512]{2,1,0:T(8,128)(2,1)S(1)}, f32[2,512]{1,0:T(2,128)S(1)}) custom-call(s32[2,4,256]{2,1,0:T(4,128)S(1)} %get-tuple-element.32.index, bf16[2,4,768,256]{3,2,1,0:T(8,128)(2,1)S(1)} %get-tuple-element.36.pick_high, ...), custom_call_target="tpu_custom_call" | custom-call | bytes 1000 | tf_op jit(solution)/shard_map/pallas_call | solution.py:265
  84.4 0.0 collective-permute-done.16.border
  84.4 0.0 collective-permute-done.10.refs_3_
  84.4 1.3 %collective-permute-start.17 = (f32[384,768]{1,0:T(8,128)S(1)}, f32[384,768]{1,0:T(8,128)S(1)}, u32[]{:S(2)}, u32[]{:S(2)}) collective-permute-start(f32[384,768]{1,0:T(8,128)S(1)} %collective-permute-done.10.refs_3_), channel_id=1, source_target_pairs={{1,5},{3,7},{4,0},{6,2},{9,13},{11,15},{12,8},{14,10},{17,21},{19,... | collective-permute-start | bytes 3538952 | tf_op jit(solution)/shard_map/ppermute | solution.py:26
  85.7 1.4 %shard_map.89 = (bf16[384,1536]{1,0:T(8,128)(2,1)S(1)}, f32[2,384,512]{2,1,0:T(8,128)S(1)}) custom-call(f32[384,1536]{1,0:T(8,128)S(1)} %collective-permute-done.16.border, bf16[2,1536,512]{2,1,0:T(8,128)(2,1)S(1)} %get-tuple-element.43.lower_high), custom_call_target="tpu_custom_call" | custom-call | bytes 1000 | tf_op jit(solution)/shard_map/pallas_call | solution.py:265
  87.2 0.0 collective-permute-done.9.refs_1_
  87.2 0.0 collective-permute-done.18.refs_5_
  87.2 2.0 %collective-permute-done.17.refs_4_ = f32[384,768]{1,0:T(8,128)S(1)} collective-permute-done((f32[384,768]{1,0:T(8,128)S(1)}, f32[384,768]{1,0:T(8,128)S(1)}, u32[]{:S(2)}, u32[]{:S(2)}) %collective-permute-start.17) | collective-permute-done | bytes 1179680 | tf_op jit(solution)/shard_map/ppermute | solution.py:26
  89.2 3.5 %shard_map.90 = f32[1,1792]{1,0:T(1,128)S(1)} custom-call(f32[384,768]{1,0:T(8,128)S(1)} %collective-permute-done.6.factor.refs_0_, f32[384,768]{1,0:T(8,128)S(1)} %collective-permute-done.9.refs_1_, f32[384,768]{1,0:T(8,128)S(1)} %collective-permute-done.4.refs_2_, f32[384,768]{1,0:T(8,128)S(1)} %collective-permute-done.10.refs_3_, ...), custom_call_target="tpu_custom_call" | custom-call | bytes 1000 | tf_op jit(solution)/shard_map/pallas_call | solution.py:265
  92.7 0.2 collective-permute-start.19
  92.9 1.0 %collective-permute-done.19 = f32[1,1792]{1,0:T(1,128)S(1)} collective-permute-done((f32[1,1792]{1,0:T(1,128)S(1)}, f32[1,1792]{1,0:T(1,128)S(1)}, u32[]{:S(2)}, u32[]{:S(2)}) %collective-permute-start.19) | collective-permute-done | bytes 7200 | tf_op jit(solution)/shard_map/ppermute | solution.py:26
  93.9 1.3 %collective-permute-start.20 = (f32[1,1792]{1,0:T(1,128)S(1)}, f32[1,1792]{1,0:T(1,128)S(1)}, u32[]{:S(2)}, u32[]{:S(2)}) collective-permute-start(f32[1,1792]{1,0:T(1,128)S(1)} %add.3.refs_0_), channel_id=1, source_target_pairs={{0,2},{1,3},{2,0},{3,1},{4,6},{5,7},{6,4},{7,5},{8,10},{9,11},{10,... | collective-permute-start | bytes 21512 | tf_op jit(solution)/shard_map/ppermute | solution.py:26
  95.2 0.1 collective-permute-start.21
  95.3 2.2 %collective-permute-start.22 = (f32[1,1792]{1,0:T(1,128)S(1)}, f32[1,1792]{1,0:T(1,128)S(1)}, u32[]{:S(2)}, u32[]{:S(2)}) collective-permute-start(f32[1,1792]{1,0:T(1,128)S(1)} %add.3.refs_0_), channel_id=1, source_target_pairs={{0,3},{1,2},{2,1},{3,0},{4,7},{5,6},{6,5},{7,4},{8,11},{9,10},{10,... | collective-permute-start | bytes 21512 | tf_op jit(solution)/shard_map/ppermute | solution.py:26
  97.5 0.2 collective-permute-done.20.refs_1_
  97.7 1.2 %collective-permute-done.21.refs_2_ = f32[1,1792]{1,0:T(1,128)S(1)} collective-permute-done((f32[1,1792]{1,0:T(1,128)S(1)}, f32[1,1792]{1,0:T(1,128)S(1)}, u32[]{:S(2)}, u32[]{:S(2)}) %collective-permute-start.21) | collective-permute-done | bytes 7200 | tf_op jit(solution)/shard_map/ppermute | solution.py:26
  98.9 1.0 collective-permute-done.22.refs_3_
  99.8 1.3 %shard_map.91 = (f32[1,768]{1,0:T(1,128)}, f32[2,512]{1,0:T(2,128)}) custom-call(s32[16]{0:T(128)} %parent_ref.3, f32[1,1792]{1,0:T(1,128)S(1)} %add.3.refs_0_, f32[1,1792]{1,0:T(1,128)S(1)} %collective-permute-done.20.refs_1_, f32[1,1792]{1,0:T(1,128)S(1)} %collective-permute-done.21.refs_2_, f32[1,1792]{1,0:T(1,128)S(1)} %collective-permute-done.22.refs_3_), custom_call_target="tpu_custom_call" | custom-call | bytes 1000 | tf_op jit(solution)/shard_map/pallas_call | solution.py:265
  (1 shorter events, 0.0 us)
Async XLA Ops:
  0.6 28.2 %collective-permute-start.4 = (f32[384,768]{1,0:T(8,128)}, f32[384,768]{1,0:T(8,128)S(1)}, u32[]{:S(2)}, u32[]{:S(2)}) collective-permute-start(f32[384,768]{1,0:T(8,128)} %bitcast.4), channel_id=1, source_target_pairs={{0,2},{2,0},{5,7},{7,5},{8,10},{10,8},{13,15},{15,13},{16,18},{18,... | collective-permute-start | bytes 3538952 | tf_op jit(solution)/shard_map/ppermute | solution.py:26
  5.5 6.0 %collective-permute-start = (f32[2,256,512]{2,1,0:T(8,128)}, f32[2,256,512]{2,1,0:T(8,128)S(1)}, u32[]{:S(2)}, u32[]{:S(2)}) collective-permute-start(f32[2,256,512]{2,1,0:T(8,128)} %own_rows.1), channel_id=1, source_target_pairs={{0,4},{1,5},{2,6},{3,7},{4,0},{5,1},{6,2},{7,3},{8,12},{9,13},{10,... | collective-permute-start | bytes 3145736 | tf_op jit(solution)/shard_map/ppermute | solution.py:26
  5.6 30.4 %copy-start = (f32[1,384,1536]{2,1,0:T(8,128)S(1)}, f32[1,384,1536]{2,1,0:T(8,128)}, u32[]{:S(2)}) copy-start(f32[1,384,1536]{2,1,0:T(8,128)} %param.7) | copy-start | bytes 7077892
  5.6 7.5 %collective-permute-start.2 = (f32[192,768]{1,0:T(8,128)}, f32[192,768]{1,0:T(8,128)S(1)}, u32[]{:S(2)}, u32[]{:S(2)}) collective-permute-start(f32[192,768]{1,0:T(8,128)} %bitcast.6), channel_id=1, source_target_pairs={{0,0},{1,4},{2,2},{3,6},{4,1},{5,5},{6,3},{7,7},{8,8},{9,12},{10,1... | collective-permute-start | bytes 1769480 | tf_op jit(solution)/shard_map/ppermute | solution.py:36
  7.5 21.4 %collective-permute-start.3 = (f32[192,768]{1,0:T(8,128)}, f32[192,768]{1,0:T(8,128)S(1)}, u32[]{:S(2)}, u32[]{:S(2)}) collective-permute-start(f32[192,768]{1,0:T(8,128)} %bitcast.7), channel_id=1, source_target_pairs={{0,2},{2,0},{5,7},{7,5},{8,10},{10,8},{13,15},{15,13},{16,18},{18,... | collective-permute-start | bytes 1769480 | tf_op jit(solution)/shard_map/ppermute | solution.py:26
  9.4 2.2 %collective-permute-start.1 = (f32[2,128,512]{2,1,0:T(8,128)}, f32[2,128,512]{2,1,0:T(8,128)S(1)}, u32[]{:S(2)}, u32[]{:S(2)}) collective-permute-start(f32[2,128,512]{2,1,0:T(8,128)} %own_inverse.1), channel_id=1, source_target_pairs={{0,4},{1,5},{2,6},{3,7},{4,0},{5,1},{6,2},{7,3},{8,12},{9,13},{10,... | collective-permute-start | bytes 1572872 | tf_op jit(solution)/shard_map/ppermute | solution.py:26
  28.8 1.5 %collective-permute-start.5 = (f32[2,384,512]{2,1,0:T(8,128)S(1)}, f32[2,384,512]{2,1,0:T(8,128)S(1)}, u32[]{:S(2)}, u32[]{:S(2)}) collective-permute-start(f32[2,384,512]{2,1,0:T(8,128)S(1)} %get-tuple-element.28), channel_id=1, source_target_pairs={{0,0},{1,4},{2,2},{3,6},{4,1},{5,5},{6,3},{7,7},{8,8},{9,12},{10,1... | collective-permute-start | bytes 4718600 | tf_op jit(solution)/shard_map/ppermute | solution.py:36
  29.6 0.7 collective-permute-start.7
  30.3 30.7 %collective-permute-start.8 = (f32[2,384,512]{2,1,0:T(8,128)S(1)}, f32[2,384,512]{2,1,0:T(8,128)S(1)}, u32[]{:S(2)}, u32[]{:S(2)}) collective-permute-start(f32[2,384,512]{2,1,0:T(8,128)S(1)} %collective-permute-done.5.refs_0_), channel_id=1, source_target_pairs={{0,2},{1,3},{2,0},{3,1},{4,6},{5,7},{6,4},{7,5},{8,10},{9,11},{10,... | collective-permute-start | bytes 4718600 | tf_op jit(solution)/shard_map/ppermute | solution.py:26
  32.8 14.2 %collective-permute-start.12 = (f32[192,768]{1,0:T(8,128)S(1)}, f32[192,768]{1,0:T(8,128)S(1)}, u32[]{:S(2)}, u32[]{:S(2)}) collective-permute-start(f32[192,768]{1,0:T(8,128)S(1)} %collective-permute-done.7.refs_3_), channel_id=1, source_target_pairs={{1,5},{3,7},{4,0},{6,2},{9,13},{11,15},{12,8},{14,10},{17,21},{19,... | collective-permute-start | bytes 1769480 | tf_op jit(solution)/shard_map/ppermute | solution.py:26
  34.0 16.4 %collective-permute-start.6 = (f32[384,768]{1,0:T(8,128)}, f32[384,768]{1,0:T(8,128)S(1)}, u32[]{:S(2)}, u32[]{:S(2)}) collective-permute-start(f32[384,768]{1,0:T(8,128)} %bitcast.5), channel_id=1, source_target_pairs={{0,0},{1,4},{2,2},{3,6},{4,1},{5,5},{6,3},{7,7},{8,8},{9,12},{10,1... | collective-permute-start | bytes 3538952 | tf_op jit(solution)/shard_map/ppermute | solution.py:36
  36.0 48.5 %collective-permute-start.16 = (f32[384,1536]{1,0:T(8,128)S(1)}, f32[384,1536]{1,0:T(8,128)S(1)}, u32[]{:S(2)}, u32[]{:S(2)}) collective-permute-start(f32[384,1536]{1,0:T(8,128)S(1)} %bitcast.3), channel_id=1, source_target_pairs={{0,0},{1,4},{2,2},{3,6},{4,1},{5,5},{6,3},{7,7},{8,8},{9,12},{10,1... | collective-permute-start | bytes 7077896 | tf_op jit(solution)/shard_map/ppermute | solution.py:36
  36.8 12.1 %collective-permute-start.11 = (f32[192,768]{1,0:T(8,128)S(1)}, f32[192,768]{1,0:T(8,128)S(1)}, u32[]{:S(2)}, u32[]{:S(2)}) collective-permute-start(f32[192,768]{1,0:T(8,128)S(1)} %collective-permute-done.2.refs_0_), channel_id=1, source_target_pairs={{0,4},{1,5},{2,6},{3,7},{4,0},{5,1},{6,2},{7,3},{8,12},{9,13},{10,... | collective-permute-start | bytes 1769480 | tf_op jit(solution)/shard_map/ppermute | solution.py:26
  46.9 3.5 %collective-permute-start.13 = (f32[192,768]{1,0:T(8,128)S(1)}, f32[192,768]{1,0:T(8,128)S(1)}, u32[]{:S(2)}, u32[]{:S(2)}) collective-permute-start(f32[192,768]{1,0:T(8,128)S(1)} %collective-permute-done.3.refs_2_), channel_id=1, source_target_pairs={{0,4},{2,6},{5,1},{7,3},{8,12},{10,14},{13,9},{15,11},{16,20},{18,... | collective-permute-start | bytes 1769480 | tf_op jit(solution)/shard_map/ppermute | solution.py:26
  48.9 22.6 %collective-permute-start.14 = (f32[2,384,512]{2,1,0:T(8,128)S(1)}, f32[2,384,512]{2,1,0:T(8,128)S(1)}, u32[]{:S(2)}, u32[]{:S(2)}) collective-permute-start(f32[2,384,512]{2,1,0:T(8,128)S(1)} %collective-permute-done.5.refs_0_), channel_id=1, source_target_pairs={{0,4},{1,5},{2,6},{3,7},{4,0},{5,1},{6,2},{7,3},{8,12},{9,13},{10,... | collective-permute-start | bytes 4718600 | tf_op jit(solution)/shard_map/ppermute | solution.py:26
  61.0 12.8 %collective-permute-start.15 = (f32[2,384,512]{2,1,0:T(8,128)S(1)}, f32[2,384,512]{2,1,0:T(8,128)S(1)}, u32[]{:S(2)}, u32[]{:S(2)}) collective-permute-start(f32[2,384,512]{2,1,0:T(8,128)S(1)} %collective-permute-done.8.refs_2_), channel_id=1, source_target_pairs={{0,4},{1,5},{2,6},{3,7},{4,0},{5,1},{6,2},{7,3},{8,12},{9,13},{10,... | collective-permute-start | bytes 4718600 | tf_op jit(solution)/shard_map/ppermute | solution.py:26
  67.8 16.6 %collective-permute-start.10 = (f32[384,768]{1,0:T(8,128)S(1)}, f32[384,768]{1,0:T(8,128)S(1)}, u32[]{:S(2)}, u32[]{:S(2)}) collective-permute-start(f32[384,768]{1,0:T(8,128)S(1)} %collective-permute-done.6.factor.refs_0_), channel_id=1, source_target_pairs={{1,3},{3,1},{4,6},{6,4},{9,11},{11,9},{12,14},{14,12},{17,19},{19,... | collective-permute-start | bytes 3538952 | tf_op jit(solution)/shard_map/ppermute | solution.py:26
  68.6 18.6 %collective-permute-start.9 = (f32[384,768]{1,0:T(8,128)S(1)}, f32[384,768]{1,0:T(8,128)S(1)}, u32[]{:S(2)}, u32[]{:S(2)}) collective-permute-start(f32[384,768]{1,0:T(8,128)S(1)} %collective-permute-done.6.factor.refs_0_), channel_id=1, source_target_pairs={{0,4},{1,5},{2,6},{3,7},{4,0},{5,1},{6,2},{7,3},{8,12},{9,13},{10,... | collective-permute-start | bytes 3538952 | tf_op jit(solution)/shard_map/ppermute | solution.py:26
  71.5 15.6 %collective-permute-start.18 = (f32[384,768]{1,0:T(8,128)S(1)}, f32[384,768]{1,0:T(8,128)S(1)}, u32[]{:S(2)}, u32[]{:S(2)}) collective-permute-start(f32[384,768]{1,0:T(8,128)S(1)} %collective-permute-done.4.refs_2_), channel_id=1, source_target_pairs={{0,4},{2,6},{5,1},{7,3},{8,12},{10,14},{13,9},{15,11},{16,20},{18,... | collective-permute-start | bytes 3538952 | tf_op jit(solution)/shard_map/ppermute | solution.py:26
  84.4 4.7 %collective-permute-start.17 = (f32[384,768]{1,0:T(8,128)S(1)}, f32[384,768]{1,0:T(8,128)S(1)}, u32[]{:S(2)}, u32[]{:S(2)}) collective-permute-start(f32[384,768]{1,0:T(8,128)S(1)} %collective-permute-done.10.refs_3_), channel_id=1, source_target_pairs={{1,5},{3,7},{4,0},{6,2},{9,13},{11,15},{12,8},{14,10},{17,21},{19,... | collective-permute-start | bytes 3538952 | tf_op jit(solution)/shard_map/ppermute | solution.py:26
  92.7 1.2 %collective-permute-start.19 = (f32[1,1792]{1,0:T(1,128)S(1)}, f32[1,1792]{1,0:T(1,128)S(1)}, u32[]{:S(2)}, u32[]{:S(2)}) collective-permute-start(f32[1,1792]{1,0:T(1,128)S(1)} %shard_map.90), channel_id=1, source_target_pairs={{0,4},{1,5},{2,6},{3,7},{4,0},{5,1},{6,2},{7,3},{8,12},{9,13},{10,... | collective-permute-start | bytes 21512 | tf_op jit(solution)/shard_map/ppermute | solution.py:26
  93.9 3.7 %collective-permute-start.20 = (f32[1,1792]{1,0:T(1,128)S(1)}, f32[1,1792]{1,0:T(1,128)S(1)}, u32[]{:S(2)}, u32[]{:S(2)}) collective-permute-start(f32[1,1792]{1,0:T(1,128)S(1)} %add.3.refs_0_), channel_id=1, source_target_pairs={{0,2},{1,3},{2,0},{3,1},{4,6},{5,7},{6,4},{7,5},{8,10},{9,11},{10,... | collective-permute-start | bytes 21512 | tf_op jit(solution)/shard_map/ppermute | solution.py:26
  95.2 3.6 %collective-permute-start.21 = (f32[1,1792]{1,0:T(1,128)S(1)}, f32[1,1792]{1,0:T(1,128)S(1)}, u32[]{:S(2)}, u32[]{:S(2)}) collective-permute-start(f32[1,1792]{1,0:T(1,128)S(1)} %add.3.refs_0_), channel_id=1, source_target_pairs={{0,1},{1,0},{2,3},{3,2},{4,5},{5,4},{6,7},{7,6},{8,9},{9,8},{10,11... | collective-permute-start | bytes 21512 | tf_op jit(solution)/shard_map/ppermute | solution.py:26
  95.3 4.5 %collective-permute-start.22 = (f32[1,1792]{1,0:T(1,128)S(1)}, f32[1,1792]{1,0:T(1,128)S(1)}, u32[]{:S(2)}, u32[]{:S(2)}) collective-permute-start(f32[1,1792]{1,0:T(1,128)S(1)} %add.3.refs_0_), channel_id=1, source_target_pairs={{0,3},{1,2},{2,1},{3,0},{4,7},{5,6},{6,5},{7,4},{8,11},{9,10},{10,... | collective-permute-start | bytes 21512 | tf_op jit(solution)/shard_map/ppermute | solution.py:26
